TPU v7x, 128 devices: a whole 4x4x4 slice. The times are simulated.
128 devices in a mesh: inst: 16 (over z, y_hi, core), tp: 8 (over x, y_lo).
Axes of the slice: x: 4, y: 4 (y_hi: 2, y_lo: 2; y = y_hi * 2 + y_lo), z: 4, core: 2. Of those that a mesh axis runs over, the one named last changes fastest.
Arguments:
- queries: bfloat16 [352, 2, 8192], P('inst', None, 'tp'), may hold values from -10 to 10
- hidden_in: bfloat16 [352, 2, 8192], P('inst', None, 'tp'), may hold values from -6 to 6
- kv_weight: bfloat16 [8192, 2, 1024], P(None, None, 'tp'), may hold values from -0.0625 to 0.0625
- kv_pool: bfloat16 [3328, 2, 128, 1024], P('inst', None, None, 'tp'), may hold values from -6 to 6
- page_table: int32 [16, 208], P('inst'), may hold values from 0 to 207, each once within a row
- long_lengths: int32 [16, 2], P('inst'), may hold values from 1 to 8192
- short_lengths: int32 [16, 20], P('inst'), may hold values from 1 to 510
- mig_order: int32 [16, 20], P('inst'), may hold values from 0 to 19, each once within a row
- destination: int32 [256, 1], P('inst'), may hold values from 0 to 15; in each aligned block of 16 rows (0 to 15, 16 to 31, ...) at most 2 rows name the same one
Outputs:
- stay_out: bfloat16 [352, 2, 8192], P('inst', None, 'tp')
- moved_out: bfloat16 [512, 2, 8192], P('inst', None, 'tp')
- moved_cache: bfloat16 [512, 2, 512, 1024], P('inst', None, None, 'tp')
- load_share: float32 [16], P('inst')
Inputs may be any that keep to these rules, and one draw needn't show every extreme that they name: `page_table`: each row holds every page number of its instance once. `mig_order`: each row holds every short request id once. Among the 16 rows of one instance no destination appears more than 2 times.
All inputs are finite; a program needn't handle non-finite values.
Results may differ from a plain program's by a relative error of at most 0.0051.
Values may be sent and summed in bfloat16 or wider, within the bound.
No kernel may reach another device: no remote copies, remote signals or barrier semaphores. Data moves between devices by JAX's collectives and lax.ppermute only.
A program may use at most 128 MiB of HBM per device.

v0:
```python
import math

import jax
import jax.numpy as jnp
from jax import lax
from jax.sharding import PartitionSpec as P

HEADS = 64
KV_HEADS = 8
HD = 128
PAGE = 128
MAXPG = 64
MIGPG = 4
LONG = 2
MIG = 16
CAP = 2
STEPS = 2
SHORT = 20
MIGLEN = 512


def attend(query, cache_keys, cache_values, length, fresh_kv):
    step_count = query.shape[0]
    key_total = cache_keys.shape[0]
    head_count = cache_keys.shape[-1] // HD
    group_size = HEADS // KV_HEADS
    query_heads = query.reshape(step_count, head_count, group_size, HD)
    old_keys = cache_keys.reshape(key_total, head_count, HD)
    old_values = cache_values.reshape(key_total, head_count, HD)
    new_keys = fresh_kv[:, 0].reshape(step_count, head_count, HD)
    new_values = fresh_kv[:, 1].reshape(step_count, head_count, HD)
    old_scores = jnp.einsum(
        "tkgd,skd->tkgs", query_heads, old_keys, preferred_element_type=jnp.float32
    ) / math.sqrt(HD)
    new_scores = jnp.einsum(
        "tkgd,skd->tkgs", query_heads, new_keys, preferred_element_type=jnp.float32
    ) / math.sqrt(HD)
    old_valid = jnp.arange(key_total) < length
    step_index = jnp.arange(step_count)
    new_valid = step_index[None, :] <= step_index[:, None]
    old_scores = jnp.where(old_valid[None, None, None, :], old_scores, -1e30)
    new_scores = jnp.where(new_valid[:, None, None, :], new_scores, -1e30)
    peak = jnp.maximum(
        jnp.max(old_scores, axis=-1, keepdims=True), jnp.max(new_scores, axis=-1, keepdims=True)
    )
    old_exp = jnp.exp(old_scores - peak)
    new_exp = jnp.exp(new_scores - peak)
    denominator = jnp.sum(old_exp, axis=-1, keepdims=True) + jnp.sum(
        new_exp, axis=-1, keepdims=True
    )
    old_weights = (old_exp / denominator).astype(jnp.bfloat16)
    new_weights = (new_exp / denominator).astype(jnp.bfloat16)
    blended = jnp.einsum(
        "tkgs,skd->tkgd", old_weights, old_values, preferred_element_type=jnp.float32
    )
    blended = blended + jnp.einsum(
        "tkgs,skd->tkgd", new_weights, new_values, preferred_element_type=jnp.float32
    )
    return blended.reshape(step_count, head_count * group_size * HD).astype(jnp.bfloat16)


def finish(cache, length, fresh_kv):
    position = jnp.arange(cache.shape[1])
    retained = jnp.where((position < length)[None, :, None], cache, jnp.zeros_like(cache))
    for step_index in range(fresh_kv.shape[0]):
        retained = jnp.where(
            (position == length + step_index)[None, :, None],
            fresh_kv[step_index][:, None, :],
            retained,
        )
    return retained


def slot_ranks(targets):
    size_rows = targets.shape[0]
    earlier = jnp.arange(size_rows)[None, :] < jnp.arange(size_rows)[:, None]
    return jnp.sum((targets[:, None] == targets[None, :]) & earlier, axis=1)


def place_rows(inst_count, targets, slot_rank, values):
    holder = jnp.zeros((inst_count, CAP) + values.shape[1:], values.dtype)
    return holder.at[targets, slot_rank].set(values)


def on_device(
    queries,
    hidden_in,
    kv_weight,
    kv_pool,
    page_table,
    long_lengths,
    short_lengths,
    mig_order,
    destination,
):
    inst_count = lax.axis_size("inst")
    inst_index = lax.axis_index("inst")
    channel_width = kv_pool.shape[-1]
    fresh_kv = jnp.einsum(
        "rtd,dck->rtck",
        lax.all_gather(hidden_in, "tp", axis=2, tiled=True),
        kv_weight,
        preferred_element_type=jnp.float32,
    ).astype(jnp.bfloat16)
    page_list = page_table[0]
    long_pages = kv_pool[page_list[: LONG * MAXPG]].reshape(LONG, MAXPG, 2, PAGE, channel_width)
    long_keys = long_pages[:, :, 0].reshape(LONG, MAXPG * PAGE, channel_width)
    long_values = long_pages[:, :, 1].reshape(LONG, MAXPG * PAGE, channel_width)
    long_out = jax.vmap(attend)(
        queries[:LONG], long_keys, long_values, long_lengths[0], fresh_kv[:LONG]
    )
    short_pages = kv_pool[page_list[LONG * MAXPG :]].reshape(SHORT, MIGPG, 2, PAGE, channel_width)
    short_keys = short_pages[:, :, 0].reshape(SHORT, MIGLEN, channel_width)
    short_values = short_pages[:, :, 1].reshape(SHORT, MIGLEN, channel_width)
    short_query = queries[LONG:]
    short_fresh = fresh_kv[LONG:]
    lengths = short_lengths[0]
    mig_list = mig_order[0]
    leaving = mig_list[:MIG]
    staying = mig_list[MIG:]
    stay_result = jax.vmap(attend)(
        short_query[staying],
        short_keys[staying],
        short_values[staying],
        lengths[staying],
        short_fresh[staying],
    )
    short_out = (
        jnp.zeros((SHORT,) + stay_result.shape[1:], jnp.bfloat16).at[staying].set(stay_result)
    )
    stay_out = jnp.concatenate([long_out, short_out], axis=0)
    leaving_len = lengths[leaving]
    leaving_query = short_query[leaving]
    leaving_fresh = short_fresh[leaving]
    leaving_cache = jnp.stack([short_keys[leaving], short_values[leaving]], axis=1)
    targets = destination[:, 0]
    slot_rank = slot_ranks(targets)
    resident = jnp.sum(long_lengths[0]) + jnp.sum(lengths[staying]) + STEPS * (LONG + SHORT - MIG)
    all_targets, all_lengths, all_resident = (
        lax.all_gather(targets[None, :], "inst", axis=0, tiled=True),
        lax.all_gather(leaving_len[None, :], "inst", axis=0, tiled=True),
        lax.all_gather(resident.reshape(1, 1), "inst", axis=0, tiled=True),
    )
    all_slots = jax.vmap(slot_ranks)(all_targets)
    arrive = all_targets == inst_index
    chosen = arrive[:, None, :] & (all_slots[:, None, :] == jnp.arange(CAP)[None, :, None])
    recv_len = jnp.sum(jnp.where(chosen, all_lengths[:, None, :], 0), axis=2).reshape(
        inst_count * CAP
    )
    own_load = resident + jnp.sum(jnp.where(arrive, all_lengths + STEPS, 0))
    all_load = jnp.sum(all_resident) + jnp.sum(all_lengths + STEPS)
    load_share = (own_load.astype(jnp.float32) * inst_count / all_load.astype(jnp.float32)).reshape(
        1
    )
    send_cache = place_rows(inst_count, targets, slot_rank, leaving_cache)
    send_fresh = place_rows(inst_count, targets, slot_rank, leaving_fresh)
    send_query = place_rows(inst_count, targets, slot_rank, leaving_query)
    got_cache, got_fresh, got_query = (
        lax.all_to_all(send_cache, "inst", split_axis=0, concat_axis=0, tiled=True),
        lax.all_to_all(send_fresh, "inst", split_axis=0, concat_axis=0, tiled=True),
        lax.all_to_all(send_query, "inst", split_axis=0, concat_axis=0, tiled=True),
    )
    got_cache = got_cache.reshape((inst_count * CAP,) + got_cache.shape[2:])
    got_fresh = got_fresh.reshape((inst_count * CAP,) + got_fresh.shape[2:])
    got_query = got_query.reshape((inst_count * CAP,) + got_query.shape[2:])
    moved_out = jax.vmap(attend)(got_query, got_cache[:, 0], got_cache[:, 1], recv_len, got_fresh)
    moved_cache = jax.vmap(finish)(got_cache, recv_len, got_fresh)
    return (stay_out, moved_out, moved_cache, load_share)


def solution(mesh):
    placed = (
        P("inst", None, "tp"),
        P("inst", None, "tp"),
        P(None, None, "tp"),
        P("inst", None, None, "tp"),
        P("inst", None),
        P("inst", None),
        P("inst", None),
        P("inst", None),
        P("inst", None),
    )
    return jax.shard_map(
        on_device,
        mesh=mesh,
        in_specs=placed,
        out_specs=(
            P("inst", None, "tp"),
            P("inst", None, "tp"),
            P("inst", None, None, "tp"),
            P("inst"),
        ),
        check_vma=False,
    )
```

profile of v0, /device:TPU:1, one launch (start us, length us, event | category | flops | bytes accessed | tf_op | source)
XLA Modules:
  0.0 260.3 jit_solution(4294963052886022040)
XLA Ops:
  3.9 25.5 %all_gather.12 = bf16[22,2,8192]{2,0,1:T(8,128)(2,1)S(1)} all-gather(bf16[22,2,1024]{2,0,1:T(8,128)(2,1)S(1)} %copy.52), channel_id=1, replica_groups=mesh['inst'=16,'tp'=8] {'tp'}, dimensions={2}, use_global_device_ids=true | all-gather | bytes 811008 | tf_op jit(solution)/shard_map/all_gather | solution.py:101
  29.4 3.0 %fusion.18 = bf16[22,2,2,128]{3,0,2,1:T(8,128)(2,1)S(1)} fusion(bf16[8192,2,128]{2,1,0:T(2,128)(2,1)} %param.11, bf16[22,2,8192]{2,0,1:T(8,128)(2,1)S(1)} %all_gather.12), kind=kOutput, calls=%fused_computation.42 | convolution fusion | flops 184560640 | bytes 4937728 | tf_op jit(solution)/shard_map/rtd,dck->rtck/dot_general | solution.py:99
  33.7 2.5 scatter_fusion.3
  36.3 13.8 %all-to-all-start.2 = ((bf16[16,2,2,2,128]{4,3,2,1,0:T(2,128)(2,1)}), bf16[16,2,2,2,128]{4,3,2,1,0:T(2,128)(2,1)S(1)}, u32[]{:S(2)}, u32[]{:S(2)}) async-start(bf16[16,2,2,2,128]{4,3,2,1,0:T(2,128)(2,1)} %scatter_fusion.3), calls=%async_computation.2 | async-start | bytes 65536 | tf_op jit(solution)/shard_map/all_to_all | solution.py:160
  57.0 11.3 %all-reduce.3 = (s32[256]{0:T(256)S(1)}, s32[256]{0:T(256)S(1)}, s32[16]{0:T(128)S(1)}) all-reduce(s32[256]{0:T(256)S(1)} %dynamic-update-slice.1, s32[256]{0:T(256)S(1)} %bitcast_dynamic-update-slice_fusion, s32[16]{0:T(128)S(1)} %dynamic-update-slice.2), channel_id=3, replica_groups=mesh['inst'=16,'tp'=8] {'inst'}, use_global_device_ids=true, to_apply=%add.1 | all-reduce | flops 528 | bytes 4224
  68.5 10.6 %gather_fusion.1 = bf16[80,2,128,128]{3,2,1,0:T(8,128)(2,1)} fusion(bf16[208,2,128,128]{3,2,1,0:T(8,128)(2,1)} %param.12, s32[1024]{0:T(1024)S(1)} %pad_clamp_fusion.2), kind=kCustom, calls=%fused_computation.1 | custom fusion | bytes 10486080 | tf_op jit(solution)/shard_map/gather | solution.py:112
  79.0 5.7 %fusion.61 = (bf16[20,4,1,128,128]{4,3,2,1,0:T(8,128)(2,1)S(1)}, bf16[20,4,1,128,128]{4,3,2,1,0:T(8,128)(2,1)}) fusion(bf16[20,4,2,128,128]{4,3,2,1,0:T(8,128)(2,1)} %bitcast.243), kind=kLoop, calls=%fused_computation.139 | loop fusion | bytes 10485760 | tf_op jit(solution)/shard_map/slice | solution.py:113
  84.7 3.9 %gather_fusion.8 = bf16[16,512,128]{2,1,0:T(8,128)(2,1)} fusion(bf16[20,512,128]{2,1,0:T(8,128)(2,1)} %bitcast.247, s32[1024]{0:T(1024)S(1)} %pad_clamp_fusion), kind=kCustom, calls=%fused_computation.8 | custom fusion | bytes 4194368 | tf_op jit(solution)/shard_map/gather | solution.py:135
  88.6 2.1 gather_fusion.7
  90.7 4.7 %pad_maximum_fusion = bf16[16,2,512,128]{3,2,1,0:T(8,128)(2,1)} fusion(bf16[16,1,512,128]{3,2,1,0:T(8,128)(2,1)} %bitcast.249, bf16[16,1,512,128]{3,2,1,0:T(8,128)(2,1)} %bitcast.250), kind=kLoop, calls=%fused_computation.25 | loop fusion | flops 2097152 | bytes 8388608 | tf_op jit(solution)/shard_map/stack | solution.py:135
  97.5 2.6 scatter_fusion.2
  100.1 6.9 %all-to-all-start.1 = ((bf16[16,2,2,1024]{3,2,1,0:T(2,128)(2,1)}), bf16[16,2,2,1024]{3,2,1,0:T(2,128)(2,1)S(1)}, u32[]{:S(2)}, u32[]{:S(2)}) async-start(bf16[16,2,2,1024]{3,2,1,0:T(2,128)(2,1)} %scatter_fusion.2), calls=%async_computation.1 | async-start | bytes 262144 | tf_op jit(solution)/shard_map/all_to_all | solution.py:161
  107.4 5.2 %broadcast_in_dim.149 = bf16[16,2,2,512,128]{4,3,2,1,0:T(8,128)(2,1)} broadcast(bf16[]{:T(256)} %constant.21.clone.1), dimensions={} | broadcast | bytes 8388610 | tf_op jit(solution)/shard_map/broadcast_in_dim | solution.py:81
  112.7 11.0 %scatter_fusion.1 = bf16[16,2,2,512,128]{4,3,2,1,0:T(8,128)(2,1)} fusion(bf16[16,2,2,512,128]{4,3,2,1,0:T(8,128)(2,1)} %broadcast_in_dim.149, s32[16]{0:T(128)S(1)} %fusion.57, bf16[16,2,512,128]{3,2,1,0:T(8,128)(2,1)} %pad_maximum_fusion), kind=kCustom, calls=%fused_computation.13 | custom fusion | bytes 12583040 | tf_op jit(solution)/shard_map/scatter | solution.py:82
  123.8 7.3 %all-to-all-start = ((bf16[16,2,2,512,128]{4,3,2,1,0:T(8,128)(2,1)}), bf16[16,2,2,512,128]{4,3,2,1,0:T(8,128)(2,1)}, u32[]{:S(2)}, u32[]{:S(2)}) async-start(bf16[16,2,2,512,128]{4,3,2,1,0:T(8,128)(2,1)} %scatter_fusion.1), calls=%async_computation | async-start | bytes 16777216 | tf_op jit(solution)/shard_map/all_to_all | solution.py:159
  131.7 3.1 %gather_fusion.2 = bf16[4,512,128]{2,1,0:T(8,128)(2,1)} fusion(bf16[20,512,128]{2,1,0:T(8,128)(2,1)} %bitcast.248, s32[1024]{0:T(1024)S(1)} %pad_clamp_fusion.1), kind=kCustom, calls=%fused_computation.2 | custom fusion | bytes 1048592 | tf_op jit(solution)/shard_map/gather | solution.py:124
  141.0 11.6 %gather_fusion = bf16[128,2,128,128]{3,2,1,0:T(8,128)(2,1)} fusion(bf16[208,2,128,128]{3,2,1,0:T(8,128)(2,1)} %param.12, s32[1024]{0:T(1024)S(1)} %pad_clamp_fusion.3), kind=kCustom, calls=%fused_computation | custom fusion | bytes 16777728 | tf_op jit(solution)/shard_map/gather | solution.py:106
  152.9 4.0 %fusion.60 = (bf16[2,64,1,128,128]{4,3,2,1,0:T(8,128)(2,1)S(1)}, bf16[2,64,1,128,128]{4,3,2,1,0:T(8,128)(2,1)S(1)}) fusion(bf16[2,64,2,128,128]{4,3,2,1,0:T(8,128)(2,1)} %bitcast.242), kind=kLoop, calls=%fused_computation.138 | loop fusion | bytes 16777216 | tf_op jit(solution)/shard_map/slice | solution.py:108
  157.0 1.3 fusion.65
  162.4 64.7 %all-to-all-done = bf16[16,2,2,512,128]{4,3,2,1,0:T(8,128)(2,1)} async-done(((bf16[16,2,2,512,128]{4,3,2,1,0:T(8,128)(2,1)}), bf16[16,2,2,512,128]{4,3,2,1,0:T(8,128)(2,1)}, u32[]{:S(2)}, u32[]{:S(2)}) %all-to-all-start) | async-done | bytes 8388640 | tf_op jit(solution)/shard_map/all_to_all | solution.py:159
  227.2 7.8 %copy.65 = bf16[16,2,2,512,128]{4,3,1,0,2:T(8,128)(2,1)} copy(bf16[16,2,2,512,128]{4,3,2,1,0:T(8,128)(2,1)} %all-to-all-done) | data formatting | bytes 16777216 | tf_op jit(solution)/shard_map/all_to_all | solution.py:159
  234.9 3.6 %fusion.66 = (f32[32,2,8]{2,1,0:T(2,128)S(1)}, f32[32,2,1,8,512]{4,3,1,0,2:T(8,128)S(1)}) fusion(bf16[32,2,8,128]{3,2,1,0:T(8,128)(2,1)S(1)} %reshape.535, bf16[32,2,512,128]{3,2,0,1:T(8,128)(2,1)} %bitcast.239, pred[32,512]{1,0:T(8,128)(4,1)S(1)} %get-tuple-element.33), kind=kOutput, calls=%fused_computation.144 | convolution fusion | flops 67894784 | bytes 5392384 | tf_op jit(solution)/shard_map/vmap(tkgd,skd->tkgs)/dot_general | solution.py:32
  240.6 10.1 %select_select_fusion = bf16[32,2,512,128]{3,2,0,1:T(8,128)(2,1)} fusion(bf16[32,2,512,128]{3,2,0,1:T(8,128)(2,1)S(1)} %bitcast.241, pred[32,512]{1,0:T(8,128)(4,1)S(1)} %get-tuple-element.33, pred[32,512]{1,0:T(8,128)(4,1)S(1)} %get-tuple-element.32, pred[32,512]{1,0:T(8,128)(4,1)S(1)} %iota_compare_fusion.1, bf16[32,2,128]{2,0,1:T(8,128)(2,1)S(1)} %get-tuple-element.42, ...), kind=kLoop, calls=%fused_computation.20 | loop fusion | flops 12582912 | bytes 16859136 | tf_op jit(solution)/shard_map/vmap(jit(_where))/select_n | solution.py:66
  250.7 7.8 %copy.69 = bf16[32,2,512,128]{3,2,1,0:T(8,128)(2,1)} copy(bf16[32,2,512,128]{3,2,0,1:T(8,128)(2,1)} %select_select_fusion) | data formatting | bytes 16777216
  (110 shorter events, 23.9 us)
Async XLA Ops:
  0.6 49.5 %copy-start = (s32[1,20]{1,0:T(1,128)S(1)}, s32[1,20]{1,0:T(1,128)}, u32[]{:S(2)}) copy-start(s32[1,20]{1,0:T(1,128)} %param.15) | copy-start | bytes 244
  0.6 52.1 %copy-start.8 = (u32[128]{0:T(128)S(1)}, u32[128]{0:T(128)}, u32[]{:S(2)}) copy-start(u32[128]{0:T(128)} %constant.110) | copy-start | bytes 1540
  0.7 53.3 %copy-start.7 = (s32[16,1]{0,1:T(1,128)S(1)}, s32[16,1]{0,1:T(1,128)}, u32[]{:S(2)}) copy-start(s32[16,1]{0,1:T(1,128)} %param.17) | copy-start | bytes 196
  0.7 49.4 %copy-start.6 = (s32[1,20]{1,0:T(1,128)S(1)}, s32[1,20]{1,0:T(1,128)}, u32[]{:S(2)}) copy-start(s32[1,20]{1,0:T(1,128)} %param.16) | copy-start | bytes 244
  0.7 51.3 %copy-start.5 = (s32[1,208]{1,0:T(1,128)S(1)}, s32[1,208]{1,0:T(1,128)}, u32[]{:S(2)}) copy-start(s32[1,208]{1,0:T(1,128)} %param.13) | copy-start | bytes 2500
  0.7 51.4 %copy-start.4 = (s32[1,2]{1,0:T(1,128)S(1)}, s32[1,2]{1,0:T(1,128)}, u32[]{:S(2)}) copy-start(s32[1,2]{1,0:T(1,128)} %param.14) | copy-start | bytes 28
  36.3 63.8 %all-to-all-start.2 = ((bf16[16,2,2,2,128]{4,3,2,1,0:T(2,128)(2,1)}), bf16[16,2,2,2,128]{4,3,2,1,0:T(2,128)(2,1)S(1)}, u32[]{:S(2)}, u32[]{:S(2)}) async-start(bf16[16,2,2,2,128]{4,3,2,1,0:T(2,128)(2,1)} %scatter_fusion.3), calls=%async_computation.2 | async-start | bytes 65536 | tf_op jit(solution)/shard_map/all_to_all | solution.py:160
  90.7 5.3 %copy-start.3 = (bf16[22,2,1024]{2,1,0:T(2,128)(2,1)S(1)}, bf16[22,2,1024]{2,1,0:T(2,128)(2,1)}, u32[]{:S(2)}) copy-start(bf16[22,2,1024]{2,1,0:T(2,128)(2,1)} %param.9) | copy-start | bytes 270340
  100.1 23.7 %all-to-all-start.1 = ((bf16[16,2,2,1024]{3,2,1,0:T(2,128)(2,1)}), bf16[16,2,2,1024]{3,2,1,0:T(2,128)(2,1)S(1)}, u32[]{:S(2)}, u32[]{:S(2)}) async-start(bf16[16,2,2,1024]{3,2,1,0:T(2,128)(2,1)} %scatter_fusion.2), calls=%async_computation.1 | async-start | bytes 262144 | tf_op jit(solution)/shard_map/all_to_all | solution.py:161
  123.8 14.6 %slice-start = ((bf16[22,2,1024]{2,1,0:T(2,128)(2,1)}), bf16[2,2,1024]{2,1,0:T(2,128)(2,1)S(1)}, s32[]{:S(2)}) async-start(bf16[22,2,1024]{2,1,0:T(2,128)(2,1)} %param.9), calls=%async_computation.3 | async-start | bytes 16384 | tf_op jit(solution)/shard_map/slice | solution.py:110
  123.8 103.4 %all-to-all-start = ((bf16[16,2,2,512,128]{4,3,2,1,0:T(8,128)(2,1)}), bf16[16,2,2,512,128]{4,3,2,1,0:T(8,128)(2,1)}, u32[]{:S(2)}, u32[]{:S(2)}) async-start(bf16[16,2,2,512,128]{4,3,2,1,0:T(8,128)(2,1)} %scatter_fusion.1), calls=%async_computation | async-start | bytes 16777216 | tf_op jit(solution)/shard_map/all_to_all | solution.py:159
  234.9 4.6 %copy-start.2 = (bf16[16,2,2,512,128]{4,3,1,0,2:T(8,128)(2,1)S(1)}, bf16[16,2,2,512,128]{4,3,1,0,2:T(8,128)(2,1)}, u32[]{:S(2)}) copy-start(bf16[16,2,2,512,128]{4,3,1,0,2:T(8,128)(2,1)} %copy.65) | copy-start | bytes 25165828
  250.7 8.5 %copy-start.1 = (s32[1,20]{1,0:T(1,128)S(1)}, s32[1,20]{1,0:T(1,128)}, u32[]{:S(2)}) copy-start(s32[1,20]{1,0:T(1,128)} %param.15) | copy-start | bytes 244
where the time goes:
time: 261 us; the launch traced here: 260 us
  local copies, waits for them, and re-layouts  88.9 us (34%)
  waiting for transfers between devices  64.7 us (25%)
  blocking collectives  36.8 us (14%)
  starting transfers between devices  28 us (11%)
  other arithmetic  23 us (9%)
  matrix products  12.7 us (5%)
  between operations  6.09 us (2%)
    all_to_all x1, waiting for transfers between devices, on_device(): lax.all_to_all(send_cache, 'inst', split_axis=0, concat_axis=0, tiled=True)  64.7 us
    all_gather x1, blocking collectives, on_device(): lax.all_gather(hidden_in, 'tp', axis=2, tiled=True)  25.5 us
    scatter x3, local copies, waits for them, and re-layouts, place_rows(): return holder.at[targets, slot_rank].set(values)  16.1 us
    all_to_all x1, starting transfers between devices, on_device(): lax.all_to_all(send_fresh, 'inst', split_axis=0, concat_axis=0, tiled=True)  13.8 us
    gather x1, local copies, waits for them, and re-layouts, on_device(): kv_pool[page_list[:LONG * MAXPG]]  11.6 us
    unnamed x1, blocking collectives  11.3 us
    unnamed x28, local copies, waits for them, and re-layouts  10.9 us
    gather x1, local copies, waits for them, and re-layouts, on_device(): kv_pool[page_list[LONG * MAXPG:]]  10.6 us
  transfers between devices with their start and end apart: 3, of which 1 were waited for; matrix products, arithmetic and copies ran while one was open for 32% of the time, Pallas kernels for 0%

commit v1 on v0

v1 whole, which is shorter than its diff:
```python
import math

import jax
import jax.numpy as jnp
from jax import lax
from jax.experimental import pallas as pl
from jax.experimental.pallas import tpu as pltpu
from jax.sharding import PartitionSpec as P

HEADS = 64
KV_HEADS = 8
HD = 128
PAGE = 128
MAXPG = 64
MIGPG = 4
LONG = 2
MIG = 16
CAP = 2
STEPS = 2
SHORT = 20
REQS = 22
MIGLEN = 512
INST = 16
PAGES = 208
ROWS = 16
DUPS = 4
PIECE = MIGLEN // INST

A_DUP = MIGLEN
A_META = A_DUP + 2 * PIECE
A_ROWS = A_META + 16
B_SIDE = MIGLEN
B_ROWS = B_SIDE + 64

SMEM = pltpu.SMEM
VMEM = pltpu.VMEM


def spec(space):
    return pl.BlockSpec(memory_space=space)


def page_copy(pool, page, part, dst, sem):
    return pltpu.make_async_copy(pool.at[page, part], dst, sem)


def build_kernel(table, longs, shorts, order, dest, pool, out, count, meta, sems, dup_sems, meta_sems):
    for i in range(INST):
        count[i] = 0
    lane = lax.broadcasted_iota(jnp.int32, (16, 128), 1)

    def first_copy(k, p):
        page = table[0, LONG * MAXPG + order[0, k] * MIGPG + p]
        return page_copy(
            pool, page, 0, out.at[dest[0, k], pl.ds(p * PAGE, PAGE)], sems.at[k * MIGPG + p]
        )

    def dup_copy(k, m, c):
        page = table[0, LONG * MAXPG + order[0, k] * MIGPG + m // MIGPG]
        return pltpu.make_async_copy(
            pool.at[page, c, pl.ds(m % MIGPG * PIECE, PIECE)],
            out.at[m, pl.ds(A_DUP + c * PIECE, PIECE)],
            dup_sems.at[m * 2 + c],
        )

    def each(k, carry):
        row, dup_at, total = carry
        to = dest[0, k]
        slot = count[to]
        count[to] = slot + 1
        length = shorts[0, order[0, k]]

        @pl.when(slot == 0)
        def _():
            for p in range(MIGPG):
                first_copy(k, p).start()

        at = to * CAP + slot
        row = jnp.where(lane == at, length & 255, row)
        row = jnp.where(lane == at + 32, length >> 8, row)
        dup_at = jnp.where((slot == 1) & (dup_at < 0), k, dup_at)
        return row, dup_at, total

    row, dup_at, _ = lax.fori_loop(
        0, MIG, each, (jnp.zeros((16, 128), jnp.int32), jnp.int32(-1), jnp.int32(0))
    )

    @pl.when(dup_at >= 0)
    def _():
        for m in range(INST):
            for c in range(2):
                dup_copy(dup_at, m, c).start()

    total = jnp.int32(STEPS * REQS)
    for i in range(LONG):
        total = total + longs[0, i]
    for i in range(SHORT):
        total = total + shorts[0, i]
    row = jnp.where(lane == 64, total & 127, row)
    row = jnp.where(lane == 65, (total >> 7) & 127, row)
    row = jnp.where(lane == 66, total >> 14, row)
    meta[...] = row.astype(jnp.float32).astype(jnp.bfloat16)

    def meta_copy(m):
        return pltpu.make_async_copy(meta, out.at[m, pl.ds(A_META, 16)], meta_sems.at[m])

    for m in range(INST):
        meta_copy(m).start()
    for i in range(INST):
        count[i] = 0

    def finish(k, carry):
        to = dest[0, k]
        slot = count[to]
        count[to] = slot + 1

        @pl.when(slot == 0)
        def _():
            for p in range(MIGPG):
                first_copy(k, p).wait()

        return carry

    lax.fori_loop(0, MIG, finish, 0)

    @pl.when(dup_at >= 0)
    def _():
        for m in range(INST):
            for c in range(2):
                dup_copy(dup_at, m, c).wait()

    for m in range(INST):
        meta_copy(m).wait()


def build(tables, pool):
    return pl.pallas_call(
        build_kernel,
        out_shape=jax.ShapeDtypeStruct((INST, A_ROWS, 128), jnp.bfloat16),
        in_specs=[spec(SMEM)] * 5 + [spec(pl.ANY)],
        out_specs=spec(pl.ANY),
        scratch_shapes=[
            pltpu.SMEM((INST,), jnp.int32),
            pltpu.VMEM((16, 128), jnp.bfloat16),
            pltpu.SemaphoreType.DMA((MIG * MIGPG,)),
            pltpu.SemaphoreType.DMA((2 * INST,)),
            pltpu.SemaphoreType.DMA((INST,)),
        ],
        cost_estimate=pl.CostEstimate(flops=0, bytes_accessed=5 << 20, transcendentals=0),
        name="build_first",
    )(*tables, pool)


def second_kernel(table, order, dest, pool, out, count, sems):
    def copy(k, p, c):
        page = table[0, LONG * MAXPG + order[0, k] * MIGPG + p]
        return page_copy(
            pool,
            page,
            c,
            out.at[dest[0, k], pl.ds(c * MIGLEN + p * PAGE, PAGE)],
            sems.at[(k * MIGPG + p) * 2 + c],
        )

    for begin in (True, False):
        for i in range(INST):
            count[i] = 0

        def each(k, carry):
            to = dest[0, k]
            slot = count[to]
            count[to] = slot + 1

            @pl.when(slot == 1)
            def _():
                for p in range(MIGPG):
                    for c in range(2):
                        if begin:
                            copy(k, p, c).start()
                        else:
                            copy(k, p, c).wait()

            return carry

        lax.fori_loop(0, MIG, each, 0)


def build_second(table, order, dest, pool):
    return pl.pallas_call(
        second_kernel,
        out_shape=jax.ShapeDtypeStruct((INST, 2 * MIGLEN, 128), jnp.bfloat16),
        in_specs=[spec(SMEM)] * 3 + [spec(pl.ANY)],
        out_specs=spec(pl.ANY),
        scratch_shapes=[
            pltpu.SMEM((INST,), jnp.int32),
            pltpu.SemaphoreType.DMA((MIG * MIGPG * 2,)),
        ],
        name="build_second",
    )(table, order, dest, pool)


def dot_nt(a, b):
    return lax.dot_general(a, b, (((1,), (1,)), ((), ())), preferred_element_type=jnp.float32)


def dot_nn(a, b):
    return lax.dot_general(a, b, (((1,), (0,)), ((), ())), preferred_element_type=jnp.float32)


GROUP = 4
CHUNK = 1024
SCALE = 1.0 / math.sqrt(HD)


def attend_kernel(
    table, longs, shorts, order, dest, query, keys_values, values, pool, stay, out,
    count, place, cache, score, side, page_sems, move_sems, side_sem,
):
    def load(pg, sem):
        return pltpu.make_async_copy(pool.at[table[0, pg]], cache.at[:, pg], sem)

    def wait_pages(first, size, sem):
        pltpu.make_async_copy(
            cache.at[:, pl.ds(first, size)], cache.at[:, pl.ds(first, size)], sem
        ).wait()

    for r in range(SHORT // GROUP):
        def start_short(i, carry, r=r):
            load(LONG * MAXPG + r * GROUP * MIGPG + i, page_sems.at[r]).start()
            return carry

        lax.fori_loop(0, GROUP * MIGPG, start_short, 0)
    for j in range(LONG):
        def start_long(i, carry, j=j):
            load(j * MAXPG + i, page_sems.at[SHORT // GROUP + j]).start()
            return carry

        lax.fori_loop(0, MAXPG, start_long, 0)

    for i in range(INST):
        count[i] = 0
    for i in range(SHORT):
        place[i] = -1

    def move(k, p):
        page = table[0, LONG * MAXPG + order[0, k] * MIGPG + p]
        return page_copy(
            pool, page, 1, out.at[dest[0, k], pl.ds(p * PAGE, PAGE)], move_sems.at[k * MIGPG + p]
        )

    def settle(k, carry):
        to = dest[0, k]
        slot = count[to]
        count[to] = slot + 1
        place[order[0, k]] = to * CAP + slot

        @pl.when(slot == 0)
        def _():
            for p in range(MIGPG):
                move(k, p).start()

        return carry

    lax.fori_loop(0, MIG, settle, 0)

    def fresh_scores(q, r):
        s = dot_nt(q, keys_values[r]) * SCALE
        step = lax.broadcasted_iota(jnp.int32, s.shape, 0) // 8
        col = lax.broadcasted_iota(jnp.int32, s.shape, 1)
        return jnp.where((col <= step) & (col < STEPS), s, -1e30)

    def short_group(g, carry):
        first = pl.multiple_of(LONG * MAXPG + g * GROUP * MIGPG, GROUP * MIGPG)
        wait_pages(first, GROUP * MIGPG, page_sems.at[g])
        pos = lax.broadcasted_iota(jnp.int32, (ROWS, MIGLEN), 1)
        old, new = [], []
        for i in range(GROUP):
            r = g * GROUP + i
            q = query[LONG + r]
            k = cache[0, pl.ds(first + i * MIGPG, MIGPG)].reshape(MIGLEN, HD)
            s = dot_nt(q, k) * SCALE
            old.append(jnp.where(pos < shorts[0, r], s, -1e30))
            new.append(fresh_scores(q, LONG + r))
        old = jnp.concatenate(old, axis=0)
        new = jnp.concatenate(new, axis=0)
        peak = jnp.maximum(jnp.max(old, 1, keepdims=True), jnp.max(new, 1, keepdims=True))
        old = jnp.exp(old - peak)
        new = jnp.exp(new - peak)
        denominator = jnp.sum(old, 1, keepdims=True) + jnp.sum(new, 1, keepdims=True)
        old = (old / denominator).astype(jnp.bfloat16)
        new = (new / denominator).astype(jnp.bfloat16)
        for i in range(GROUP):
            r = g * GROUP + i
            v = cache[1, pl.ds(first + i * MIGPG, MIGPG)].reshape(MIGLEN, HD)
            o = dot_nn(old[i * ROWS:(i + 1) * ROWS], v)
            o = o + dot_nn(new[i * ROWS:(i + 1) * ROWS], values[LONG + r])
            o = o.astype(jnp.bfloat16)
            at = place[r]

            @pl.when(at < 0)
            def _():
                stay[LONG + r] = o

            @pl.when(at >= 0)
            def _():
                stay[LONG + r] = jnp.zeros_like(o)
                side[at, pl.ds(0, ROWS)] = o
                side[at, pl.ds(ROWS, 16)] = keys_values[LONG + r]

        return carry

    lax.fori_loop(0, SHORT // GROUP, short_group, 0)
    side_copies = [
        pltpu.make_async_copy(
            side.at[i], out.at[i // CAP, pl.ds(B_SIDE + i % CAP * 32, 32)], side_sem.at[i]
        )
        for i in range(INST * CAP)
    ]
    for c in side_copies:
        c.start()

    for j in range(LONG):
        wait_pages(j * MAXPG, MAXPG, page_sems.at[SHORT // GROUP + j])
        q = query[j]
        new = fresh_scores(q, j)
        top = jnp.max(new, 1, keepdims=True)
        length = longs[0, j]
        steps = MAXPG * PAGE // CHUNK
        per = CHUNK // PAGE
        for i in range(steps):
            k = cache[0, pl.ds(j * MAXPG + i * per, per)].reshape(CHUNK, HD)
            s = dot_nt(q, k) * SCALE
            pos = lax.broadcasted_iota(jnp.int32, s.shape, 1) + i * CHUNK
            s = jnp.where(pos < length, s, -1e30)
            score[j, i] = s
            top = jnp.maximum(top, jnp.max(s, 1, keepdims=True))
        new = jnp.exp(new - top)
        denominator = jnp.sum(new, 1, keepdims=True)
        for i in range(steps):
            e = jnp.exp(score[j, i] - top)
            score[j, i] = e
            denominator = denominator + jnp.sum(e, 1, keepdims=True)
        inverse = 1.0 / denominator
        o = dot_nn((new * inverse).astype(jnp.bfloat16), values[j])
        for i in range(steps):
            v = cache[1, pl.ds(j * MAXPG + i * per, per)].reshape(CHUNK, HD)
            o = o + dot_nn((score[j, i] * inverse).astype(jnp.bfloat16), v)
        stay[j] = o.astype(jnp.bfloat16)

    for i in range(INST):
        count[i] = 0

    def finish(k, carry):
        to = dest[0, k]
        slot = count[to]
        count[to] = slot + 1

        @pl.when(slot == 0)
        def _():
            for p in range(MIGPG):
                move(k, p).wait()

        return carry

    lax.fori_loop(0, MIG, finish, 0)
    for c in side_copies:
        c.wait()


def attend(tables, query, keys_values, values, pool):
    return pl.pallas_call(
        attend_kernel,
        out_shape=(
            jax.ShapeDtypeStruct((REQS, ROWS, HD), jnp.bfloat16),
            jax.ShapeDtypeStruct((INST, B_ROWS, HD), jnp.bfloat16),
        ),
        in_specs=[spec(SMEM)] * 5 + [spec(VMEM)] * 3 + [spec(pl.ANY)],
        out_specs=(spec(VMEM), spec(pl.ANY)),
        scratch_shapes=[
            pltpu.SMEM((INST,), jnp.int32),
            pltpu.SMEM((SHORT,), jnp.int32),
            pltpu.VMEM((2, PAGES, PAGE, HD), jnp.bfloat16),
            pltpu.VMEM((LONG, MAXPG * PAGE // CHUNK, ROWS, CHUNK), jnp.float32),
            pltpu.VMEM((INST * CAP, 32, HD), jnp.bfloat16),
            pltpu.SemaphoreType.DMA((SHORT // GROUP + LONG,)),
            pltpu.SemaphoreType.DMA((MIG * MIGPG,)),
            pltpu.SemaphoreType.DMA((INST * CAP,)),
        ],
        compiler_params=pltpu.CompilerParams(vmem_limit_bytes=24 << 20),
        cost_estimate=pl.CostEstimate(
            flops=4 * 26624 * 16 * 128, bytes_accessed=17 << 20, transcendentals=26624 * 16
        ),
        name="attend_all",
    )(*tables, query, keys_values, values, pool)


def join_kernel(here, *refs):
    pieces, out = refs[:-1], refs[-1]
    me = here[0]
    width = pieces[0].shape[1]
    for k, piece in enumerate(pieces):
        at = pl.multiple_of(((me + 8 - k) % 8) * width, width)
        out[:, pl.ds(at, width)] = piece[...]


def join(here, pieces):
    rows, width = pieces[0].shape
    return pl.pallas_call(
        join_kernel,
        out_shape=jax.ShapeDtypeStruct((rows, width * len(pieces)), jnp.bfloat16),
        in_specs=[spec(SMEM)] + [spec(VMEM)] * len(pieces),
        out_specs=spec(VMEM),
        name="join_hidden",
    )(here, *pieces)


def pick_kernel(source, block, out):
    out[...] = block[...]


def pick(source, received):
    return pl.pallas_call(
        pick_kernel,
        out_shape=jax.ShapeDtypeStruct((DUPS, 2 * PIECE, HD), jnp.bfloat16),
        grid_spec=pltpu.PrefetchScalarGridSpec(
            num_scalar_prefetch=1,
            grid=(DUPS,),
            in_specs=[
                pl.BlockSpec(
                    (1, 2 * PIECE, HD), lambda j, source: (source[j], A_DUP // (2 * PIECE), 0)
                )
            ],
            out_specs=pl.BlockSpec((1, 2 * PIECE, HD), lambda j, source: (j, 0, 0)),
        ),
        name="pick_pieces",
    )(source, received)


def place_kernel(full, lens, rank, here, first, second, dup, cache, out):
    s = pl.program_id(0)
    pos = lax.broadcasted_iota(jnp.int32, (PAGE, HD), 0)
    for slot in range(CAP):
        length = lens[s * CAP + slot]
        filled = length > 0
        if slot == 0:
            sources = [
                lambda p: first[0, pl.ds(p * PAGE, PAGE)],
                lambda p: second[0, pl.ds(p * PAGE, PAGE)],
            ]
        elif full:
            sources = [
                lambda p: dup[0, pl.ds(p * PAGE, PAGE)],
                lambda p: dup[0, pl.ds(MIGLEN + p * PAGE, PAGE)],
            ]
        else:
            me = here[0]
            j = rank[s]

            def piece(p, c):
                parts = []
                for q in range(MIGPG):
                    x = me ^ (p * MIGPG + q)
                    e = ((x >> 2) & 3) | (((x >> 1) & 1) << 2) | ((x & 1) << 3)
                    parts.append(dup[e, j, pl.ds(c * PIECE, PIECE)])
                return jnp.concatenate(parts, axis=0)

            sources = [lambda p: piece(p, 0), lambda p: piece(p, 1)]
        for p in range(MIGPG):
            whole = filled & (length >= (p + 1) * PAGE)
            empty = jnp.logical_not(filled) | (length + STEPS <= p * PAGE)

            @pl.when(whole)
            def _():
                for c in range(2):
                    cache[slot, c, pl.ds(p * PAGE, PAGE)] = sources[c](p)

            @pl.when(empty)
            def _():
                for c in range(2):
                    cache[slot, c, pl.ds(p * PAGE, PAGE)] = jnp.zeros((PAGE, HD), jnp.bfloat16)

            @pl.when(jnp.logical_not(whole | empty))
            def _():
                fresh = second[0, pl.ds(B_SIDE + slot * 32 + ROWS, 16)].astype(jnp.float32)
                at = pos + p * PAGE
                for c in range(2):
                    x = sources[c](p).astype(jnp.float32)
                    x = jnp.where(at < length, x, 0.0)
                    for t in range(STEPS):
                        x = jnp.where(at == length + t, fresh[c * 2 + t:c * 2 + t + 1], x)
                    cache[slot, c, pl.ds(p * PAGE, PAGE)] = x.astype(jnp.bfloat16)

        @pl.when(filled)
        def _():
            out[slot] = second[0, pl.ds(B_SIDE + slot * 32, ROWS)]

        @pl.when(jnp.logical_not(filled))
        def _():
            out[slot] = jnp.zeros((ROWS, HD), jnp.bfloat16)


def place_all(full, lens, rank, here, first, second, dup):
    def kernel(*refs):
        place_kernel(full, *refs)

    if full:
        dup_spec = pl.BlockSpec((1, 2 * MIGLEN, HD), lambda s, *_: (s, 0, 0))
    else:
        dup_spec = pl.BlockSpec(dup.shape, lambda s, *_: (0, 0, 0, 0))
    return pl.pallas_call(
        kernel,
        out_shape=(
            jax.ShapeDtypeStruct((INST * CAP, 2, MIGLEN, HD), jnp.bfloat16),
            jax.ShapeDtypeStruct((INST * CAP, ROWS, HD), jnp.bfloat16),
        ),
        grid_spec=pltpu.PrefetchScalarGridSpec(
            num_scalar_prefetch=3,
            grid=(INST,),
            in_specs=[
                pl.BlockSpec((1, MIGLEN, HD), lambda s, *_: (s, 0, 0)),
                pl.BlockSpec((1, B_ROWS, HD), lambda s, *_: (s, 0, 0)),
                dup_spec,
            ],
            out_specs=[
                pl.BlockSpec((CAP, 2, MIGLEN, HD), lambda s, *_: (s, 0, 0, 0)),
                pl.BlockSpec((CAP, ROWS, HD), lambda s, *_: (s, 0, 0)),
            ],
        ),
        compiler_params=pltpu.CompilerParams(vmem_limit_bytes=16 << 20),
        name="place_full" if full else "place_short",
    )(lens, rank, here, first, second, dup)


def swap(value, axis, bit):
    count = lax.axis_size(axis)
    return lax.ppermute(value, axis, [(i, i ^ bit) for i in range(count)])


def on_device(
    queries,
    hidden_in,
    kv_weight,
    kv_pool,
    page_table,
    long_lengths,
    short_lengths,
    mig_order,
    destination,
):
    inst_index = lax.axis_index("inst")
    tp_index = lax.axis_index("tp")
    targets = destination.reshape(1, MIG)
    tables = (page_table, long_lengths, short_lengths, mig_order, targets)

    first = build(tables, kv_pool)
    got_first = lax.all_to_all(first, "inst", split_axis=0, concat_axis=0, tiled=True)

    hidden = hidden_in.reshape(REQS * STEPS, -1)
    pieces = [hidden]
    for k in range(1, 8):
        pieces.append(lax.ppermute(hidden, "tp", [(i, (i + k) % 8) for i in range(8)]))
    hidden_all = join(tp_index.reshape(1), pieces)
    fresh = jnp.einsum(
        "rd,dcn->rcn", hidden_all, kv_weight, preferred_element_type=jnp.float32
    ).astype(jnp.bfloat16)
    fresh = fresh.reshape(REQS, STEPS, 2, HD)
    values = jnp.pad(fresh[:, :, 1], ((0, 0), (0, 16 - STEPS), (0, 0)))
    keys_values = jnp.pad(
        fresh.transpose(0, 2, 1, 3).reshape(REQS, 2 * STEPS, HD),
        ((0, 0), (0, 16 - 2 * STEPS), (0, 0)),
    )
    stay, second = attend(
        tables, queries.reshape(REQS, ROWS, HD), keys_values, values, kv_pool
    )
    stay_out = stay.reshape(REQS, STEPS, KV_HEADS * HD)
    got_second = lax.all_to_all(second, "inst", split_axis=0, concat_axis=0, tiled=True)

    meta = got_first[:, A_META].astype(jnp.float32).astype(jnp.int32)
    lengths = (meta[:, :32] + 256 * meta[:, 32:64]).reshape(INST, INST, CAP)
    all_load = jnp.sum(meta[:, 64] + 128 * meta[:, 65] + 16384 * meta[:, 66])
    doubled = jnp.sum((lengths[:, :, 1] > 0).astype(jnp.int32), axis=1)
    index = jnp.arange(INST)
    rank = jnp.sum(jnp.where(index[None, :] < index[:, None], doubled[None, :], 0), axis=1)
    overflow = (jnp.sum(doubled) > DUPS) | (jnp.max(doubled) > 1)
    rank = jnp.minimum(rank, DUPS - 1)
    source = jnp.sum(
        jnp.where(
            (rank[None, :] == jnp.arange(DUPS)[:, None]) & (doubled[None, :] > 0), index[None, :], 0
        ),
        axis=1,
    )
    source = jnp.minimum(source, INST - 1)
    arriving = jnp.sum(
        jnp.where(index[None, :, None] == inst_index, lengths, 0), axis=1
    ).reshape(INST * CAP)
    staying = jnp.any(
        mig_order[0, MIG:][:, None] == jnp.arange(SHORT)[None, :], axis=0
    )
    resident = (
        jnp.sum(long_lengths)
        + jnp.sum(jnp.where(staying, short_lengths[0], 0))
        + STEPS * (LONG + SHORT - MIG)
    )
    own_load = resident + jnp.sum(jnp.where(arriving > 0, arriving + STEPS, 0))
    load_share = (own_load.astype(jnp.float32) * INST / all_load.astype(jnp.float32)).reshape(1)

    dup = pick(source, got_first)[None]
    for bit in (4, 8, 2, 1):
        dup = jnp.concatenate([dup, swap(dup, "inst", bit)], axis=0)

    here = inst_index.reshape(1)

    def short_path(args):
        lens, rank, first, second, dup = args
        return tuple(place_all(False, lens, rank, here, first, second, dup))

    def long_path(args):
        lens, rank, first, second, _ = args
        send = build_second(page_table, mig_order, targets, kv_pool)
        got = lax.all_to_all(send, "inst", split_axis=0, concat_axis=0, tiled=True)
        return tuple(place_all(True, lens, rank, here, first, second, got))

    moved_cache, moved = lax.cond(
        overflow, long_path, short_path, (arriving, rank, got_first, got_second, dup)
    )
    moved_out = moved.reshape(INST * CAP, STEPS, KV_HEADS * HD)
    return (stay_out, moved_out, moved_cache, load_share)


def solution(mesh):
    placed = (
        P("inst", None, "tp"),
        P("inst", None, "tp"),
        P(None, None, "tp"),
        P("inst", None, None, "tp"),
        P("inst", None),
        P("inst", None),
        P("inst", None),
        P("inst", None),
        P("inst", None),
    )
    return jax.shard_map(
        on_device,
        mesh=mesh,
        in_specs=placed,
        out_specs=(
            P("inst", None, "tp"),
            P("inst", None, "tp"),
            P("inst", None, None, "tp"),
            P("inst"),
        ),
        check_vma=False,
    )
```

time: 261 us -> 274 us (1.050)
  Pallas kernels: 0 us -> 151 us
  local copies, waits for them, and re-layouts: 88.9 us -> 7.42 us
  blocking collectives: 36.8 us -> 0 us
  other arithmetic: 23 us -> 8.42 us
  starting transfers between devices: 28 us -> 39.5 us
  matrix products: 12.7 us -> 3.27 us
  waiting for transfers between devices: 64.7 us -> 57.6 us
    pallas_call x0 -> x5, Pallas kernels: none -> 151 us  [the longest x1 67.8 us: attend(): pl.pallas_call(attend_kernel, out_shape=(jax.ShapeDtypeStruct((REQS, ROWS...]
    all_to_all x3 -> x2, waiting for transfers between devices: 64.7 us -> 0.01 us  [the longest x1 0.01 us: on_device(): lax.all_to_all(first, 'inst', split_axis=0, concat_axis=0, tiled=True)]
    ppermute x0 -> x11, waiting for transfers between devices: none -> 57.6 us  [the longest x7 33.1 us: on_device(): lax.ppermute(hidden, 'tp', [(i, (i + k) % 8) for i in range(8)])]
    gather x12 -> x0, local copies, waits for them, and re-layouts: 35.8 us -> none  [the longest x1 11.6 us: on_device(): kv_pool[page_list[:LONG * MAXPG]]]
    all_gather x1 -> x0, blocking collectives: 25.5 us -> none  [on_device(): lax.all_gather(hidden_in, 'tp', axis=2, tiled=True)]
    ppermute x0 -> x11, starting transfers between devices: none -> 17.1 us  [the longest x4 9.21 us: swap(): return lax.ppermute(value, axis, [(i, i ^ bit) for i in range(count)])]
    scatter x4 -> x0, local copies, waits for them, and re-layouts: 16.8 us -> none  [the longest x3 16.1 us: place_rows(): return holder.at[targets, slot_rank].set(values)]
    unnamed x1 -> x0, blocking collectives: 11.3 us -> none
  transfers between devices with their start and end apart: 3 -> 13, of which waited for: 1 -> 6; matrix products, arithmetic and copies ran while one was open for 32% -> 6% of each run, Pallas kernels for 0% -> 26%
where the time goes in v1:
time: 274 us; the launch traced here: 273 us
  Pallas kernels  151 us (55%)
  waiting for transfers between devices  57.6 us (21%)
  starting transfers between devices  39.5 us (14%)
  other arithmetic  8.42 us (3%)
  local copies, waits for them, and re-layouts  7.42 us (3%)
  between operations  6.1 us (2%)
  matrix products  3.27 us (1%)
    pallas_call x1, Pallas kernels, attend(): pl.pallas_call(attend_kernel, out_shape=(jax.ShapeDtypeStruct((REQS, ROWS...  67.8 us
    pallas_call x1, Pallas kernels, build(): pl.pallas_call(build_kernel, out_shape=jax.ShapeDtypeStruct((INST, A_ROWS...  66.4 us
    ppermute x7, waiting for transfers between devices, on_device(): lax.ppermute(hidden, 'tp', [(i, (i + k) % 8) for i in range(8)])  33.1 us
    ppermute x4, waiting for transfers between devices, swap(): return lax.ppermute(value, axis, [(i, i ^ bit) for i in range(count)])  24.4 us
    all_to_all x1, starting transfers between devices, on_device(): lax.all_to_all(first, 'inst', split_axis=0, concat_axis=0, tiled=True)  12.9 us
    pallas_call x1, Pallas kernels, place_all(): pl.pallas_call(kernel, out_shape=(jax.ShapeDtypeStruct((INST * CAP, 2, MI...  12.7 us
    all_to_all x1, starting transfers between devices, on_device(): lax.all_to_all(second, 'inst', split_axis=0, concat_axis=0, tiled=True)  9.45 us
    ppermute x4, starting transfers between devices, swap(): return lax.ppermute(value, axis, [(i, i ^ bit) for i in range(count)])  9.21 us
  transfers between devices with their start and end apart: 13, of which 6 were waited for; matrix products, arithmetic and copies ran while one was open for 6% of the time, Pallas kernels for 26%

profile of v1, /device:TPU:1, one launch (start us, length us, event | category | flops | bytes accessed | tf_op | source)
XLA Modules:
  0.0 273.3 jit_solution(15697869737679876009)
XLA Ops:
  0.6 66.4 %build_first.1 = bf16[16,592,128]{2,1,0:T(8,128)(2,1)} custom-call(s32[1,208]{1,0:T(1,128)} %table.3, s32[1,2]{1,0:T(1,128)} %longs.3, s32[1,20]{1,0:T(1,128)} %shorts.3, s32[1,20]{1,0:T(1,128)} %order.3, s32[1,16]{1,0:T(1,128)} %bitcast.36, bf16[208,2,128,128]{3,2,1,0:T(8,128)(2,1)} %pool.3), custom_call_target="tpu_custom_call" | custom-call | bytes 5242880 | tf_op jit(solution)/shard_map/build_first/pallas_call | solution.py:137
  67.1 12.9 %all-to-all-start.1 = ((bf16[16,592,128]{2,1,0:T(8,128)(2,1)}), bf16[16,592,128]{2,1,0:T(8,128)(2,1)S(1)}, u32[]{:S(2)}, u32[]{:S(2)}) async-start(bf16[16,592,128]{2,1,0:T(8,128)(2,1)} %build_first.1), calls=%async_computation.1 | async-start | bytes 4849664 | tf_op jit(solution)/shard_map/all_to_all | solution.py:556
  80.0 2.7 collective-permute-start.6
  83.3 1.0 collective-permute-start.4
  84.3 2.5 collective-permute-start.3
  86.8 27.8 %collective-permute-done.6.refs_7_ = bf16[44,1024]{1,0:T(8,128)(2,1)S(1)} collective-permute-done((bf16[44,1024]{1,0:T(8,128)(2,1)S(1)}, bf16[44,1024]{1,0:T(8,128)(2,1)S(1)}, u32[]{:S(2)}, u32[]{:S(2)}) %collective-permute-start.6) | collective-permute-done | bytes 90144 | tf_op jit(solution)/shard_map/ppermute | solution.py:561
  114.5 1.2 collective-permute-start.1
  116.0 3.2 %collective-permute-done.1.refs_2_ = bf16[44,1024]{1,0:T(8,128)(2,1)S(1)} collective-permute-done((bf16[44,1024]{1,0:T(8,128)(2,1)S(1)}, bf16[44,1024]{1,0:T(8,128)(2,1)S(1)}, u32[]{:S(2)}, u32[]{:S(2)}) %collective-permute-start.1) | collective-permute-done | bytes 90144 | tf_op jit(solution)/shard_map/ppermute | solution.py:561
  119.2 2.1 collective-permute-done.refs_1_
  122.0 2.1 join_hidden.1
  124.1 3.3 %fusion.2 = bf16[44,2,128]{2,0,1:T(8,128)(2,1)S(1)} fusion(bf16[8192,2,128]{2,1,0:T(2,128)(2,1)} %param.13, bf16[44,8192]{1,0:T(8,128)(2,1)} %join_hidden.1), kind=kOutput, calls=%fused_computation.2 | convolution fusion | flops 184560640 | bytes 4937728 | tf_op jit(solution)/shard_map/rd,dcn->rcn/dot_general | solution.py:563
  127.6 67.8 %attend_all.1 = (bf16[22,16,128]{2,1,0:T(8,128)(2,1)S(1)}, bf16[16,576,128]{2,1,0:T(8,128)(2,1)}) custom-call(s32[1,208]{1,0:T(1,128)S(1)} %copy-done.16, s32[1,2]{1,0:T(1,128)S(1)} %copy-done.1, s32[1,20]{1,0:T(1,128)S(1)} %copy-done, s32[1,20]{1,0:T(1,128)S(1)} %copy-done.17, s32[1,16]{1,0:T(1,128)S(1)} %bitcast.37, ...), custom_call_target="tpu_custom_call" | custom-call | flops 218103808 | bytes 17825792 | tf_op jit(solution)/shard_map/attend_all/pallas_call | solution.py:371
  195.4 9.4 %all-to-all-start.2 = ((bf16[16,576,128]{2,1,0:T(8,128)(2,1)}), bf16[16,576,128]{2,1,0:T(8,128)(2,1)}, u32[]{:S(2)}, u32[]{:S(2)}) async-start(bf16[16,576,128]{2,1,0:T(8,128)(2,1)} %get-tuple-element.63), calls=%async_computation.2 | async-start | bytes 4718592 | tf_op jit(solution)/shard_map/all_to_all | solution.py:576
  206.5 1.9 pick_pieces.1
  208.4 1.4 collective-permute-start.7
  209.9 24.3 %collective-permute-done.7 = bf16[1,4,64,128]{3,2,1,0:T(8,128)(2,1)S(1)} collective-permute-done((bf16[1,4,64,128]{3,2,1,0:T(8,128)(2,1)}, bf16[1,4,64,128]{3,2,1,0:T(8,128)(2,1)S(1)}, u32[]{:S(2)}, u32[]{:S(2)}) %collective-permute-start.7) | collective-permute-done | bytes 65568 | tf_op jit(solution)/shard_map/ppermute | solution.py:536
  235.0 2.5 collective-permute-start.8
  241.7 2.8 %collective-permute-start.9 = (bf16[4,4,64,128]{3,2,1,0:T(8,128)(2,1)S(1)}, bf16[4,4,64,128]{3,2,1,0:T(8,128)(2,1)S(1)}, u32[]{:S(2)}, u32[]{:S(2)}) collective-permute-start(bf16[4,4,64,128]{3,2,1,0:T(8,128)(2,1)S(1)} %pad_maximum_fusion.1), channel_id=1, source_target_pairs={{0,16},{8,24},{16,0},{24,8},{32,48},{40,56},{48,32},{56,40},{64,80... | collective-permute-start | bytes 786440 | tf_op jit(solution)/shard_map/ppermute | solution.py:536
  249.5 1.7 pad_maximum_fusion
  251.2 2.6 collective-permute-start.10
  255.6 1.0 constant_dynamic-update-slice_fusion.1
  256.6 1.1 constant_dynamic-update-slice_fusion
  257.7 13.8 %conditional.1 = (bf16[32,2,512,128]{3,2,1,0:T(8,128)(2,1)}, bf16[32,2,1024]{2,1,0:T(2,128)(2,1)S(1)}) conditional(s32[]{:T(128)} %convert_element_type.35, (s32[32]{0:T(128)S(1)}, s32[16]{0:T(128)}, s32[1]{0:T(128)}, bf16[16,592,128]{2,1,0:T(8,128)(2,1)S(1)}, bf16[16,576,128]{2,1,0:T(8,128)(2,1)}, ...), branch_computations={%region_6.7_spmd, %region_7.8_spmd} | conditional | bytes 8651052 | solution.py:623
  258.7 12.7 %place_short.1 = (bf16[32,2,512,128]{3,2,1,0:T(8,128)(2,1)}, bf16[32,16,128]{2,1,0:T(8,128)(2,1)S(1)}) custom-call(s32[32]{0:T(128)S(1)} %get-tuple-element.35.refs_0_, s32[16]{0:T(128)} %get-tuple-element.36.refs_1_, s32[1]{0:T(128)} %get-tuple-element.37.refs_2_, bf16[16,592,128]{2,1,0:T(8,128)(2,1)S(1)} %get-tuple-element.38.refs_3_, ...), custom_call_target="tpu_custom_call" | custom-call | tf_op jit(solution)/shard_map/cond/branch_0_fun/place_short/pallas_call | solution.py:510
  (87 shorter events, 12.8 us)
Async XLA Ops:
  67.0 12.9 %copy-start.14 = (bf16[22,2,1024]{2,1,0:T(2,128)(2,1)S(1)}, bf16[22,2,1024]{2,1,0:T(2,128)(2,1)}, u32[]{:S(2)}) copy-start(bf16[22,2,1024]{2,1,0:T(2,128)(2,1)} %param.12) | copy-start | bytes 270340
  67.0 48.7 %copy-start.17 = (s32[1,20]{1,0:T(1,128)S(1)}, s32[1,20]{1,0:T(1,128)}, u32[]{:S(2)}) copy-start(s32[1,20]{1,0:T(1,128)} %order.3) | copy-start | bytes 244
  67.1 48.8 %copy-start.15 = (bf16[22,2,1024]{2,1,0:T(2,128)(2,1)S(1)}, bf16[22,2,1024]{2,1,0:T(2,128)(2,1)}, u32[]{:S(2)}) copy-start(bf16[22,2,1024]{2,1,0:T(2,128)(2,1)} %param.11) | copy-start | bytes 270340
  67.1 128.4 %all-to-all-start.1 = ((bf16[16,592,128]{2,1,0:T(8,128)(2,1)}), bf16[16,592,128]{2,1,0:T(8,128)(2,1)S(1)}, u32[]{:S(2)}, u32[]{:S(2)}) async-start(bf16[16,592,128]{2,1,0:T(8,128)(2,1)} %build_first.1), calls=%async_computation.1 | async-start | bytes 4849664 | tf_op jit(solution)/shard_map/all_to_all | solution.py:556
  79.9 47.6 %copy-start = (s32[1,20]{1,0:T(1,128)S(1)}, s32[1,20]{1,0:T(1,128)}, u32[]{:S(2)}) copy-start(s32[1,20]{1,0:T(1,128)} %shorts.3) | copy-start | bytes 244
  79.9 47.6 %copy-start.1 = (s32[1,2]{1,0:T(1,128)S(1)}, s32[1,2]{1,0:T(1,128)}, u32[]{:S(2)}) copy-start(s32[1,2]{1,0:T(1,128)} %longs.3) | copy-start | bytes 28
  80.0 47.6 %copy-start.16 = (s32[1,208]{1,0:T(1,128)S(1)}, s32[1,208]{1,0:T(1,128)}, u32[]{:S(2)}) copy-start(s32[1,208]{1,0:T(1,128)} %table.3) | copy-start | bytes 2500
  80.0 47.6 %copy-start.18 = (s32[16,1]{0,1:T(1,128)S(1)}, s32[16,1]{0,1:T(1,128)}, u32[]{:S(2)}) copy-start(s32[16,1]{0,1:T(1,128)} %param.19) | copy-start | bytes 196
  80.0 41.3 %copy-start.5 = (bf16[44,1024]{1,0:T(8,128)(2,1)}, bf16[44,1024]{1,0:T(8,128)(2,1)S(1)}, u32[]{:S(2)}) copy-start(bf16[44,1024]{1,0:T(8,128)(2,1)S(1)} %reshape.76.refs_0_) | copy-start | bytes 270340
  80.0 34.5 %collective-permute-start.6 = (bf16[44,1024]{1,0:T(8,128)(2,1)S(1)}, bf16[44,1024]{1,0:T(8,128)(2,1)S(1)}, u32[]{:S(2)}, u32[]{:S(2)}) collective-permute-start(bf16[44,1024]{1,0:T(8,128)(2,1)S(1)} %reshape.76.refs_0_), channel_id=1, source_target_pairs={{0,7},{1,0},{2,1},{3,2},{4,3},{5,4},{6,5},{7,6},{8,15},{9,8},{10,9... | collective-permute-start | bytes 270344 | tf_op jit(solution)/shard_map/ppermute | solution.py:561
  82.7 33.0 %collective-permute-start.5 = (bf16[44,1024]{1,0:T(8,128)(2,1)S(1)}, bf16[44,1024]{1,0:T(8,128)(2,1)S(1)}, u32[]{:S(2)}, u32[]{:S(2)}) collective-permute-start(bf16[44,1024]{1,0:T(8,128)(2,1)S(1)} %reshape.76.refs_0_), channel_id=1, source_target_pairs={{0,6},{1,7},{2,0},{3,1},{4,2},{5,3},{6,4},{7,5},{8,14},{9,15},{10,... | collective-permute-start | bytes 270344 | tf_op jit(solution)/shard_map/ppermute | solution.py:561
  83.3 32.6 %collective-permute-start.4 = (bf16[44,1024]{1,0:T(8,128)(2,1)S(1)}, bf16[44,1024]{1,0:T(8,128)(2,1)S(1)}, u32[]{:S(2)}, u32[]{:S(2)}) collective-permute-start(bf16[44,1024]{1,0:T(8,128)(2,1)S(1)} %reshape.76.refs_0_), channel_id=1, source_target_pairs={{0,5},{1,6},{2,7},{3,0},{4,1},{5,2},{6,3},{7,4},{8,13},{9,14},{10,... | collective-permute-start | bytes 270344 | tf_op jit(solution)/shard_map/ppermute | solution.py:561
  84.3 31.6 %collective-permute-start.3 = (bf16[44,1024]{1,0:T(8,128)(2,1)S(1)}, bf16[44,1024]{1,0:T(8,128)(2,1)S(1)}, u32[]{:S(2)}, u32[]{:S(2)}) collective-permute-start(bf16[44,1024]{1,0:T(8,128)(2,1)S(1)} %reshape.76.refs_0_), channel_id=1, source_target_pairs={{0,4},{1,5},{2,6},{3,7},{4,0},{5,1},{6,2},{7,3},{8,12},{9,13},{10,... | collective-permute-start | bytes 270344 | tf_op jit(solution)/shard_map/ppermute | solution.py:561
  86.8 29.2 %collective-permute-start.2 = (bf16[44,1024]{1,0:T(8,128)(2,1)S(1)}, bf16[44,1024]{1,0:T(8,128)(2,1)S(1)}, u32[]{:S(2)}, u32[]{:S(2)}) collective-permute-start(bf16[44,1024]{1,0:T(8,128)(2,1)S(1)} %reshape.76.refs_0_), channel_id=1, source_target_pairs={{0,3},{1,4},{2,5},{3,6},{4,7},{5,0},{6,1},{7,2},{8,11},{9,12},{10,... | collective-permute-start | bytes 270344 | tf_op jit(solution)/shard_map/ppermute | solution.py:561
  114.5 6.8 %copy-start.7 = (bf16[44,1024]{1,0:T(8,128)(2,1)}, bf16[44,1024]{1,0:T(8,128)(2,1)S(1)}, u32[]{:S(2)}) copy-start(bf16[44,1024]{1,0:T(8,128)(2,1)S(1)} %collective-permute-done.6.refs_7_) | copy-start | bytes 270340
  114.5 4.7 %collective-permute-start.1 = (bf16[44,1024]{1,0:T(8,128)(2,1)S(1)}, bf16[44,1024]{1,0:T(8,128)(2,1)S(1)}, u32[]{:S(2)}, u32[]{:S(2)}) collective-permute-start(bf16[44,1024]{1,0:T(8,128)(2,1)S(1)} %reshape.76.refs_0_), channel_id=1, source_target_pairs={{0,2},{1,3},{2,4},{3,5},{4,6},{5,7},{6,0},{7,1},{8,10},{9,11},{10,... | collective-permute-start | bytes 270344 | tf_op jit(solution)/shard_map/ppermute | solution.py:561
  115.8 5.6 %collective-permute-start = (bf16[44,1024]{1,0:T(8,128)(2,1)S(1)}, bf16[44,1024]{1,0:T(8,128)(2,1)S(1)}, u32[]{:S(2)}, u32[]{:S(2)}) collective-permute-start(bf16[44,1024]{1,0:T(8,128)(2,1)S(1)} %reshape.76.refs_0_), channel_id=1, source_target_pairs={{0,1},{1,2},{2,3},{3,4},{4,5},{5,6},{6,7},{7,0},{8,9},{9,10},{10,1... | collective-permute-start | bytes 270344 | tf_op jit(solution)/shard_map/ppermute | solution.py:561
  195.4 59.2 %all-to-all-start.2 = ((bf16[16,576,128]{2,1,0:T(8,128)(2,1)}), bf16[16,576,128]{2,1,0:T(8,128)(2,1)}, u32[]{:S(2)}, u32[]{:S(2)}) async-start(bf16[16,576,128]{2,1,0:T(8,128)(2,1)} %get-tuple-element.63), calls=%async_computation.2 | async-start | bytes 4718592 | tf_op jit(solution)/shard_map/all_to_all | solution.py:576
  205.8 34.9 %copy-start.19 = (s32[16]{0:T(128)}, s32[16]{0:T(128)S(1)}, u32[]{:S(2)}) copy-start(s32[16]{0:T(128)S(1)} %broadcast_minimum_fusion.1) | copy-start | bytes 196
  208.4 25.7 %collective-permute-start.7 = (bf16[1,4,64,128]{3,2,1,0:T(8,128)(2,1)}, bf16[1,4,64,128]{3,2,1,0:T(8,128)(2,1)S(1)}, u32[]{:S(2)}, u32[]{:S(2)}) collective-permute-start(bf16[1,4,64,128]{3,2,1,0:T(8,128)(2,1)} %bitcast.24), channel_id=1, source_target_pairs={{0,32},{8,40},{16,48},{24,56},{32,0},{40,8},{48,16},{56,24},{64,96... | collective-permute-start | bytes 196616 | tf_op jit(solution)/shard_map/ppermute | solution.py:536
  235.0 5.8 %collective-permute-start.8 = (bf16[2,4,64,128]{3,2,1,0:T(8,128)(2,1)S(1)}, bf16[2,4,64,128]{3,2,1,0:T(8,128)(2,1)S(1)}, u32[]{:S(2)}, u32[]{:S(2)}) collective-permute-start(bf16[2,4,64,128]{3,2,1,0:T(8,128)(2,1)S(1)} %pad_maximum_fusion.2), channel_id=1, source_target_pairs={{0,64},{8,72},{16,80},{24,88},{32,96},{40,104},{48,112},{56,120},{... | collective-permute-start | bytes 393224 | tf_op jit(solution)/shard_map/ppermute | solution.py:536
  240.8 10.4 %copy-start.3 = (bf16[2,4,64,128]{3,2,1,0:T(8,128)(2,1)}, bf16[2,4,64,128]{3,2,1,0:T(8,128)(2,1)S(1)}, u32[]{:S(2)}) copy-start(bf16[2,4,64,128]{3,2,1,0:T(8,128)(2,1)S(1)} %collective-permute-done.8) | copy-start | bytes 393220
  241.7 7.7 %collective-permute-start.9 = (bf16[4,4,64,128]{3,2,1,0:T(8,128)(2,1)S(1)}, bf16[4,4,64,128]{3,2,1,0:T(8,128)(2,1)S(1)}, u32[]{:S(2)}, u32[]{:S(2)}) collective-permute-start(bf16[4,4,64,128]{3,2,1,0:T(8,128)(2,1)S(1)} %pad_maximum_fusion.1), channel_id=1, source_target_pairs={{0,16},{8,24},{16,0},{24,8},{32,48},{40,56},{48,32},{56,40},{64,80... | collective-permute-start | bytes 786440 | tf_op jit(solution)/shard_map/ppermute | solution.py:536
  251.2 5.4 %collective-permute-start.10 = (bf16[8,4,64,128]{3,2,1,0:T(8,128)(2,1)}, bf16[8,4,64,128]{3,2,1,0:T(8,128)(2,1)}, u32[]{:S(2)}, u32[]{:S(2)}) collective-permute-start(bf16[8,4,64,128]{3,2,1,0:T(8,128)(2,1)} %pad_maximum_fusion), channel_id=1, source_target_pairs={{0,8},{8,0},{16,24},{24,16},{32,40},{40,32},{48,56},{56,48},{64,72... | collective-permute-start | bytes 1572872 | tf_op jit(solution)/shard_map/ppermute | solution.py:536
  (9 other events, 28.0 us)

commit v2 on v1

v2 whole, which is shorter than its diff:
```python
import math

import jax
import jax.numpy as jnp
from jax import lax
from jax.experimental import pallas as pl
from jax.experimental.pallas import tpu as pltpu
from jax.sharding import PartitionSpec as P

HEADS = 64
KV_HEADS = 8
HD = 128
PAGE = 128
MAXPG = 64
MIGPG = 4
LONG = 2
MIG = 16
CAP = 2
STEPS = 2
SHORT = 20
REQS = 22
MIGLEN = 512
INST = 16
PAGES = 208
ROWS = 16
DUPS = 4
PIECE = MIGLEN // INST

A_DUP = 2 * MIGLEN
A_META = A_DUP + 2 * PIECE
A_ROWS = A_META + 16
B_DUP = 64
B_ROWS = B_DUP + DUPS * 2 * PIECE

SMEM = pltpu.SMEM
VMEM = pltpu.VMEM


def spec(space):
    return pl.BlockSpec(memory_space=space)


def clear(count):
    for i in range(INST):
        count[i] = 0


def take_slot(count, to):
    slot = count[to]
    count[to] = slot + 1
    return slot


def build_kernel(
    table, longs, shorts, order, dest, pool, out, count, held, extra, stage, sems, extra_sems, out_sems, stage_sem
):
    def load(k, p):
        page = table[0, LONG * MAXPG + order[0, k] * MIGPG + p]
        return pltpu.make_async_copy(
            pool.at[page], held.at[dest[0, k], pl.ds(p * 2 * PAGE, 2 * PAGE)], sems.at[k * MIGPG + p]
        )

    def load_extra(k, p):
        page = table[0, LONG * MAXPG + order[0, k] * MIGPG + p]
        return pltpu.make_async_copy(pool.at[page], extra.at[p], extra_sems.at[p])

    def send(k):
        to = dest[0, k]
        return pltpu.make_async_copy(
            held.at[to], out.at[to, pl.ds(0, 2 * MIGLEN)], out_sems.at[k]
        )

    clear(count)

    def begin(k, dup_at):
        slot = take_slot(count, dest[0, k])

        @pl.when(slot == 0)
        def _():
            for p in range(MIGPG):
                load(k, p).start()

        first = (slot == 1) & (dup_at < 0)

        @pl.when(first)
        def _():
            for p in range(MIGPG):
                load_extra(k, p).start()

        return jnp.where(first, k, dup_at)

    dup_at = lax.fori_loop(0, MIG, begin, jnp.int32(-1))
    clear(count)
    lane = lax.broadcasted_iota(jnp.int32, (16, 128), 1)

    def each(k, row):
        to = dest[0, k]
        slot = take_slot(count, to)
        length = shorts[0, order[0, k]]

        @pl.when(slot == 0)
        def _():
            for p in range(MIGPG):
                load(k, p).wait()
            send(k).start()

        at = to * CAP + slot
        row = jnp.where(lane == at, length & 255, row)
        return jnp.where(lane == at + 32, length >> 8, row)

    row = lax.fori_loop(0, MIG, each, jnp.zeros((16, 128), jnp.int32))
    total = jnp.int32(STEPS * REQS)
    for i in range(LONG):
        total = total + longs[0, i]
    for i in range(SHORT):
        total = total + shorts[0, i]
    row = jnp.where(lane == 64, total & 127, row)
    row = jnp.where(lane == 65, (total >> 7) & 127, row)
    row = jnp.where(lane == 66, total >> 14, row)
    dup_to = jnp.where(dup_at >= 0, dest[0, jnp.maximum(dup_at, 0)] + 1, 0)
    row = jnp.where(lane == 67, dup_to, row)
    tables = row.astype(jnp.float32).astype(jnp.bfloat16)

    @pl.when(dup_at >= 0)
    def _():
        for p in range(MIGPG):
            load_extra(dup_at, p).wait()
        for m in range(INST):
            for c in range(2):
                stage[m, pl.ds(c * PIECE, PIECE)] = extra[
                    m // MIGPG, pl.ds(c * PAGE + m % MIGPG * PIECE, PIECE)
                ]

    for m in range(INST):
        stage[m, pl.ds(2 * PIECE, 16)] = tables
    last = pltpu.make_async_copy(stage, out.at[:, pl.ds(A_DUP, A_ROWS - A_DUP)], stage_sem)
    last.start()
    clear(count)

    def finish(k, carry):
        slot = take_slot(count, dest[0, k])

        @pl.when(slot == 0)
        def _():
            send(k).wait()

        return carry

    lax.fori_loop(0, MIG, finish, 0)
    last.wait()


def build(tables, pool):
    return pl.pallas_call(
        build_kernel,
        out_shape=jax.ShapeDtypeStruct((INST, A_ROWS, HD), jnp.bfloat16),
        in_specs=[spec(SMEM)] * 5 + [spec(pl.ANY)],
        out_specs=spec(pltpu.HBM),
        scratch_shapes=[
            pltpu.SMEM((INST,), jnp.int32),
            pltpu.VMEM((INST, 2 * MIGLEN, HD), jnp.bfloat16),
            pltpu.VMEM((MIGPG, 2 * PAGE, HD), jnp.bfloat16),
            pltpu.VMEM((INST, A_ROWS - A_DUP, HD), jnp.bfloat16),
            pltpu.SemaphoreType.DMA((MIG * MIGPG,)),
            pltpu.SemaphoreType.DMA((MIGPG,)),
            pltpu.SemaphoreType.DMA((MIG,)),
            pltpu.SemaphoreType.DMA(()),
        ],
        compiler_params=pltpu.CompilerParams(vmem_limit_bytes=60 << 20),
        cost_estimate=pl.CostEstimate(flops=0, bytes_accessed=9 << 20, transcendentals=0),
        name="build_first",
    )(*tables, pool)


def second_kernel(table, order, dest, pool, out, count, held, sems, out_sems):
    def load(k, p):
        page = table[0, LONG * MAXPG + order[0, k] * MIGPG + p]
        return pltpu.make_async_copy(
            pool.at[page], held.at[dest[0, k], pl.ds(p * 2 * PAGE, 2 * PAGE)], sems.at[k * MIGPG + p]
        )

    def send(k):
        to = dest[0, k]
        return pltpu.make_async_copy(held.at[to], out.at[to], out_sems.at[k])

    for stage in range(3):
        clear(count)

        def each(k, carry):
            slot = take_slot(count, dest[0, k])

            @pl.when(slot == 1)
            def _():
                if stage == 0:
                    for p in range(MIGPG):
                        load(k, p).start()
                elif stage == 1:
                    for p in range(MIGPG):
                        load(k, p).wait()
                    send(k).start()
                else:
                    send(k).wait()

            return carry

        lax.fori_loop(0, MIG, each, 0)


def build_second(table, order, dest, pool):
    return pl.pallas_call(
        second_kernel,
        out_shape=jax.ShapeDtypeStruct((INST, 2 * MIGLEN, HD), jnp.bfloat16),
        in_specs=[spec(SMEM)] * 3 + [spec(pl.ANY)],
        out_specs=spec(pl.ANY),
        scratch_shapes=[
            pltpu.SMEM((INST,), jnp.int32),
            pltpu.VMEM((INST, 2 * MIGLEN, HD), jnp.bfloat16),
            pltpu.SemaphoreType.DMA((MIG * MIGPG,)),
            pltpu.SemaphoreType.DMA((MIG,)),
        ],
        compiler_params=pltpu.CompilerParams(vmem_limit_bytes=12 << 20),
        name="build_second",
    )(table, order, dest, pool)


def dot_nt(a, b):
    return lax.dot_general(a, b, (((1,), (1,)), ((), ())), preferred_element_type=jnp.float32)


def dot_nn(a, b):
    return lax.dot_general(a, b, (((1,), (0,)), ((), ())), preferred_element_type=jnp.float32)


GROUP = 4
CHUNK = 1024
SCALE = 1.0 / math.sqrt(HD)


def attend_kernel(
    table, longs, shorts, order, dest, query, keys_values, values, pool, stay, side,
    count, place, cache, score, page_sems,
):
    def load(pg, sem):
        return pltpu.make_async_copy(pool.at[table[0, pg]], cache.at[:, pg], sem)

    def wait_pages(first, size, sem):
        pltpu.make_async_copy(
            cache.at[:, pl.ds(first, size)], cache.at[:, pl.ds(first, size)], sem
        ).wait()

    for r in range(SHORT // GROUP):
        def start_short(i, carry, r=r):
            load(LONG * MAXPG + r * GROUP * MIGPG + i, page_sems.at[r]).start()
            return carry

        lax.fori_loop(0, GROUP * MIGPG, start_short, 0)
    for j in range(LONG):
        def start_long(i, carry, j=j):
            load(j * MAXPG + i, page_sems.at[SHORT // GROUP + j]).start()
            return carry

        lax.fori_loop(0, MAXPG, start_long, 0)

    clear(count)
    for i in range(SHORT):
        place[i] = -1

    def settle(k, carry):
        to = dest[0, k]
        place[order[0, k]] = to * CAP + take_slot(count, to)
        return carry

    lax.fori_loop(0, MIG, settle, 0)

    def fresh_scores(q, r):
        s = dot_nt(q, keys_values[r]) * SCALE
        step = lax.broadcasted_iota(jnp.int32, s.shape, 0) // 8
        col = lax.broadcasted_iota(jnp.int32, s.shape, 1)
        return jnp.where((col <= step) & (col < STEPS), s, -1e30)

    def short_group(g, carry):
        first = pl.multiple_of(LONG * MAXPG + g * GROUP * MIGPG, GROUP * MIGPG)
        wait_pages(first, GROUP * MIGPG, page_sems.at[g])
        pos = lax.broadcasted_iota(jnp.int32, (ROWS, MIGLEN), 1)
        old, new = [], []
        for i in range(GROUP):
            r = g * GROUP + i
            q = query[LONG + r]
            k = cache[0, pl.ds(first + i * MIGPG, MIGPG)].reshape(MIGLEN, HD)
            s = dot_nt(q, k) * SCALE
            old.append(jnp.where(pos < shorts[0, r], s, -1e30))
            new.append(fresh_scores(q, LONG + r))
        old = jnp.concatenate(old, axis=0)
        new = jnp.concatenate(new, axis=0)
        peak = jnp.maximum(jnp.max(old, 1, keepdims=True), jnp.max(new, 1, keepdims=True))
        old = jnp.exp(old - peak)
        new = jnp.exp(new - peak)
        denominator = jnp.sum(old, 1, keepdims=True) + jnp.sum(new, 1, keepdims=True)
        old = (old / denominator).astype(jnp.bfloat16)
        new = (new / denominator).astype(jnp.bfloat16)
        for i in range(GROUP):
            r = g * GROUP + i
            v = cache[1, pl.ds(first + i * MIGPG, MIGPG)].reshape(MIGLEN, HD)
            o = dot_nn(old[i * ROWS:(i + 1) * ROWS], v)
            o = o + dot_nn(new[i * ROWS:(i + 1) * ROWS], values[LONG + r])
            o = o.astype(jnp.bfloat16)
            at = place[r]

            @pl.when(at < 0)
            def _():
                stay[LONG + r] = o

            @pl.when(at >= 0)
            def _():
                stay[LONG + r] = jnp.zeros_like(o)
                side[at, pl.ds(0, ROWS)] = o
                side[at, pl.ds(ROWS, 16)] = keys_values[LONG + r]

        return carry

    lax.fori_loop(0, SHORT // GROUP, short_group, 0)

    for j in range(LONG):
        wait_pages(j * MAXPG, MAXPG, page_sems.at[SHORT // GROUP + j])
        q = query[j]
        new = fresh_scores(q, j)
        top = jnp.max(new, 1, keepdims=True)
        length = longs[0, j]
        steps = MAXPG * PAGE // CHUNK
        per = CHUNK // PAGE
        for i in range(steps):
            k = cache[0, pl.ds(j * MAXPG + i * per, per)].reshape(CHUNK, HD)
            s = dot_nt(q, k) * SCALE
            pos = lax.broadcasted_iota(jnp.int32, s.shape, 1) + i * CHUNK
            s = jnp.where(pos < length, s, -1e30)
            score[j, i] = s
            top = jnp.maximum(top, jnp.max(s, 1, keepdims=True))
        new = jnp.exp(new - top)
        denominator = jnp.sum(new, 1, keepdims=True)
        for i in range(steps):
            e = jnp.exp(score[j, i] - top)
            score[j, i] = e
            denominator = denominator + jnp.sum(e, 1, keepdims=True)
        inverse = 1.0 / denominator
        o = dot_nn((new * inverse).astype(jnp.bfloat16), values[j])
        for i in range(steps):
            v = cache[1, pl.ds(j * MAXPG + i * per, per)].reshape(CHUNK, HD)
            o = o + dot_nn((score[j, i] * inverse).astype(jnp.bfloat16), v)
        stay[j] = o.astype(jnp.bfloat16)


def attend(tables, query, keys_values, values, pool):
    return pl.pallas_call(
        attend_kernel,
        out_shape=(
            jax.ShapeDtypeStruct((REQS, ROWS, HD), jnp.bfloat16),
            jax.ShapeDtypeStruct((INST * CAP, 32, HD), jnp.bfloat16),
        ),
        in_specs=[spec(SMEM)] * 5 + [spec(VMEM)] * 3 + [spec(pl.ANY)],
        out_specs=(spec(VMEM), spec(VMEM)),
        scratch_shapes=[
            pltpu.SMEM((INST,), jnp.int32),
            pltpu.SMEM((SHORT,), jnp.int32),
            pltpu.VMEM((2, PAGES, PAGE, HD), jnp.bfloat16),
            pltpu.VMEM((LONG, MAXPG * PAGE // CHUNK, ROWS, CHUNK), jnp.float32),
            pltpu.SemaphoreType.DMA((SHORT // GROUP + LONG,)),
        ],
        compiler_params=pltpu.CompilerParams(vmem_limit_bytes=24 << 20),
        cost_estimate=pl.CostEstimate(
            flops=4 * 26624 * 16 * 128, bytes_accessed=14 << 20, transcendentals=26624 * 16
        ),
        name="attend_all",
    )(*tables, query, keys_values, values, pool)


def join_kernel(here, own, mate, out):
    me = here[0]
    width = own.shape[2]
    for k in range(4):
        for other in range(2):
            x = (me // 2 + 4 - k) % 4
            y = (me + other) % 2
            at = pl.multiple_of((x * 2 + y) * width, width)
            out[:, pl.ds(at, width)] = (mate if other else own)[k]


def join(here, own, mate):
    _, rows, width = own.shape
    return pl.pallas_call(
        join_kernel,
        out_shape=jax.ShapeDtypeStruct((rows, width * 8), jnp.bfloat16),
        in_specs=[spec(SMEM), spec(VMEM), spec(VMEM)],
        out_specs=spec(VMEM),
        name="join_hidden",
    )(here, own, mate)


def route_kernel(received, side, out, small, count, sem):
    copy = pltpu.make_async_copy(received.at[:, pl.ds(A_DUP, A_ROWS - A_DUP)], small, sem)
    copy.start()
    clear(count)
    for d in range(INST):
        for c in range(CAP):
            out[d, pl.ds(c * 32, 32)] = side[d * CAP + c]
    copy.wait()
    lane = lax.broadcasted_iota(jnp.int32, (16, 128), 1)
    targets = []
    for s in range(INST):
        tables = small[s, pl.ds(2 * PIECE, 16)].astype(jnp.float32)
        targets.append(jnp.max(jnp.where(lane == 67, tables, 0.0)).astype(jnp.int32) - 1)
    for s in range(INST):
        to = targets[s]
        at = jnp.maximum(to, 0)

        @pl.when((to >= 0) & (count[at] < DUPS))
        def _():
            slot = take_slot(count, at)
            row = pl.multiple_of(B_DUP + slot * 2 * PIECE, 2 * PIECE)
            out[at, pl.ds(row, 2 * PIECE)] = small[s, pl.ds(0, 2 * PIECE)]


def route(received, side):
    return pl.pallas_call(
        route_kernel,
        out_shape=jax.ShapeDtypeStruct((INST, B_ROWS, HD), jnp.bfloat16),
        in_specs=[spec(pl.ANY), spec(VMEM)],
        out_specs=spec(VMEM),
        scratch_shapes=[
            pltpu.VMEM((INST, A_ROWS - A_DUP, HD), jnp.bfloat16),
            pltpu.SMEM((INST,), jnp.int32),
            pltpu.SemaphoreType.DMA(()),
        ],
        cost_estimate=pl.CostEstimate(flops=0, bytes_accessed=2 << 20, transcendentals=0),
        name="route_pieces",
    )(received, side)


def window_base(length):
    return pl.multiple_of(jnp.minimum(length // 16 * 16, MIGLEN - 32), 16)


def masked_page(read, write, length, fresh, p):
    grown = length + STEPS if fresh is not None else length
    whole = length >= (p + 1) * PAGE
    empty = grown <= p * PAGE

    @pl.when(whole)
    def _():
        for c in range(2):
            write(p, c, read(p, c))

    @pl.when(empty)
    def _():
        for c in range(2):
            write(p, c, jnp.zeros((PAGE, HD), jnp.bfloat16))

    @pl.when(jnp.logical_not(whole | empty))
    def _():
        at = lax.broadcasted_iota(jnp.int32, (PAGE, HD), 0) + p * PAGE
        for c in range(2):
            x = jnp.where(at < length, read(p, c).astype(jnp.float32), 0.0)
            if fresh is not None:
                rows = fresh().astype(jnp.float32)
                for t in range(STEPS):
                    x = jnp.where(at == length + t, rows[c * 2 + t:c * 2 + t + 1], x)
            write(p, c, x.astype(jnp.bfloat16))


def place_kernel(lens, block, cache, window):
    s = pl.program_id(0)
    length = lens[s * CAP]

    def read(p, c):
        return block[0, pl.ds((p * 2 + c) * PAGE, PAGE)]

    def write(p, c, x):
        cache[0, c, pl.ds(p * PAGE, PAGE)] = x

    for p in range(MIGPG):
        masked_page(read, write, length, None, p)
    cache[1] = jnp.zeros((2, MIGLEN, HD), jnp.bfloat16)
    base = window_base(length)
    for c in range(2):
        window[0, c] = cache[0, c, pl.ds(base, 32)]


def place_first(lens, received):
    return pl.pallas_call(
        place_kernel,
        out_shape=(
            jax.ShapeDtypeStruct((INST * CAP, 2, MIGLEN, HD), jnp.bfloat16),
            jax.ShapeDtypeStruct((INST, 2, 32, HD), jnp.bfloat16),
        ),
        grid_spec=pltpu.PrefetchScalarGridSpec(
            num_scalar_prefetch=1,
            grid=(INST,),
            in_specs=[pl.BlockSpec((1, 2 * MIGLEN, HD), lambda s, _: (s, 0, 0))],
            out_specs=[
                pl.BlockSpec((CAP, 2, MIGLEN, HD), lambda s, _: (s, 0, 0, 0)),
                pl.BlockSpec((1, 2, 32, HD), lambda s, _: (s, 0, 0, 0)),
            ],
        ),
        compiler_params=pltpu.CompilerParams(vmem_limit_bytes=8 << 20),
        cost_estimate=pl.CostEstimate(flops=0, bytes_accessed=13 << 20, transcendentals=0),
        name="place_first",
    )(lens, received)


def settle_kernel(full, lens, window, second, extra, _, cache, out, patched, dups, sems, dup_sems):
    at = lax.broadcasted_iota(jnp.int32, (32, HD), 0)

    def patch_copy(s, c):
        return pltpu.make_async_copy(
            patched.at[s, c],
            cache.at[s * CAP, c, pl.ds(window_base(lens[s * CAP]), 32)],
            sems.at[s * 2 + c],
        )

    def dup_copy(s):
        return pltpu.make_async_copy(dups.at[s], cache.at[s * CAP + 1], dup_sems.at[s])

    for s in range(INST):
        length = lens[s * CAP]

        @pl.when(length > 0)
        def _():
            fresh = second[s, pl.ds(ROWS, 16)].astype(jnp.float32)
            where = at + window_base(length)
            for c in range(2):
                x = window[s, c].astype(jnp.float32)
                for t in range(STEPS):
                    x = jnp.where(where == length + t, fresh[c * 2 + t:c * 2 + t + 1], x)
                patched[s, c] = x.astype(jnp.bfloat16)
                patch_copy(s, c).start()

    order = jnp.int32(0)
    for s in range(INST):
        length = lens[s * CAP + 1]
        rank = jnp.minimum(order, DUPS - 1)
        order = order + (length > 0).astype(jnp.int32)

        @pl.when(length > 0)
        def _():
            def read(p, c):
                if full:
                    return extra[s, pl.ds((p * 2 + c) * PAGE, PAGE)]
                row = pl.multiple_of(B_DUP + rank * 2 * PIECE + c * PIECE, PIECE)
                return jnp.concatenate(
                    [second[p * MIGPG + i, pl.ds(row, PIECE)] for i in range(MIGPG)], axis=0
                )

            def write(p, c, x):
                dups[s, c, pl.ds(p * PAGE, PAGE)] = x

            for p in range(MIGPG):
                masked_page(read, write, length, lambda: second[s, pl.ds(32 + ROWS, 16)], p)
            dup_copy(s).start()

    for s in range(INST):
        for slot in range(CAP):
            filled = lens[s * CAP + slot] > 0
            rows = second[s, pl.ds(slot * 32, ROWS)]
            out[s * CAP + slot] = jnp.where(filled, rows, jnp.zeros_like(rows))
    for s in range(INST):
        @pl.when(lens[s * CAP] > 0)
        def _():
            for c in range(2):
                patch_copy(s, c).wait()

        @pl.when(lens[s * CAP + 1] > 0)
        def _():
            dup_copy(s).wait()


def settle_all(full, lens, window, second, extra, cache):
    def kernel(*refs):
        settle_kernel(full, *refs)

    return pl.pallas_call(
        kernel,
        out_shape=(
            jax.ShapeDtypeStruct(cache.shape, jnp.bfloat16),
            jax.ShapeDtypeStruct((INST * CAP, ROWS, HD), jnp.bfloat16),
        ),
        in_specs=[spec(SMEM)] + [spec(VMEM)] * 3 + [spec(pl.ANY)],
        out_specs=(spec(pl.ANY), spec(VMEM)),
        scratch_shapes=[
            pltpu.VMEM((INST, 2, 32, HD), jnp.bfloat16),
            pltpu.VMEM((INST, 2, MIGLEN, HD), jnp.bfloat16),
            pltpu.SemaphoreType.DMA((INST * 2,)),
            pltpu.SemaphoreType.DMA((INST,)),
        ],
        input_output_aliases={4: 0},
        compiler_params=pltpu.CompilerParams(vmem_limit_bytes=20 << 20),
        name="settle_full" if full else "settle_short",
    )(lens, window, second, extra, cache)


def on_device(
    queries,
    hidden_in,
    kv_weight,
    kv_pool,
    page_table,
    long_lengths,
    short_lengths,
    mig_order,
    destination,
):
    inst_index = lax.axis_index("inst")
    tp_index = lax.axis_index("tp")
    targets = destination.reshape(1, MIG)
    tables = (page_table, long_lengths, short_lengths, mig_order, targets)
    pages = kv_pool.reshape(PAGES, 2 * PAGE, HD)

    hidden = hidden_in.reshape(REQS * STEPS, -1)
    pieces = [hidden]
    for k in range(1, 4):
        pieces.append(
            lax.ppermute(hidden, "tp", [(i, (i // 2 + k) % 4 * 2 + i % 2) for i in range(8)])
        )
    own = jnp.stack(pieces)
    own, late_targets = lax.optimization_barrier((own, targets))
    mate = lax.ppermute(own, "tp", [(i, i ^ 1) for i in range(8)])
    first = build((*tables[:4], late_targets), pages)
    first, mate = lax.optimization_barrier((first, mate))
    got_first = lax.all_to_all(first, "inst", split_axis=0, concat_axis=0, tiled=True)

    hidden_all = join(tp_index.reshape(1), own, mate)
    fresh = jnp.einsum(
        "rd,dcn->rcn", hidden_all, kv_weight, preferred_element_type=jnp.float32
    ).astype(jnp.bfloat16)
    fresh = fresh.reshape(REQS, STEPS, 2, HD)
    values = jnp.pad(fresh[:, :, 1], ((0, 0), (0, 16 - STEPS), (0, 0)))
    keys_values = jnp.pad(
        fresh.transpose(0, 2, 1, 3).reshape(REQS, 2 * STEPS, HD),
        ((0, 0), (0, 16 - 2 * STEPS), (0, 0)),
    )
    stay, side = attend(
        tables, queries.reshape(REQS, ROWS, HD), keys_values, values, kv_pool
    )
    stay_out = stay.reshape(REQS, STEPS, KV_HEADS * HD)
    second = route(got_first, side)
    got_second = lax.all_to_all(second, "inst", split_axis=0, concat_axis=0, tiled=True)

    meta = got_first[:, A_META].astype(jnp.float32).astype(jnp.int32)
    lengths = (meta[:, :32] + 256 * meta[:, 32:64]).reshape(INST, INST, CAP)
    all_load = jnp.sum(meta[:, 64] + 128 * meta[:, 65] + 16384 * meta[:, 66])
    doubled = (lengths[:, :, 1] > 0).astype(jnp.int32)
    overflow = (jnp.max(jnp.sum(doubled, axis=0)) > DUPS) | (jnp.max(jnp.sum(doubled, axis=1)) > 1)
    index = jnp.arange(INST)
    arriving = jnp.sum(
        jnp.where(index[None, :, None] == inst_index, lengths, 0), axis=1
    ).reshape(INST * CAP)
    staying = jnp.any(
        mig_order[0, MIG:][:, None] == jnp.arange(SHORT)[None, :], axis=0
    )
    resident = (
        jnp.sum(long_lengths)
        + jnp.sum(jnp.where(staying, short_lengths[0], 0))
        + STEPS * (LONG + SHORT - MIG)
    )
    own_load = resident + jnp.sum(jnp.where(arriving > 0, arriving + STEPS, 0))
    load_share = (own_load.astype(jnp.float32) * INST / all_load.astype(jnp.float32)).reshape(1)

    cache, window = place_first(arriving, got_first)

    def short_path(args):
        lens, window, second, cache = args
        return tuple(settle_all(False, lens, window, second, window, cache))

    def long_path(args):
        lens, window, second, cache = args
        send = build_second(page_table, mig_order, targets, pages)
        got = lax.all_to_all(send, "inst", split_axis=0, concat_axis=0, tiled=True)
        return tuple(settle_all(True, lens, window, second, got, cache))

    moved_cache, moved = lax.cond(
        overflow, long_path, short_path, (arriving, window, got_second, cache)
    )
    moved_out = moved.reshape(INST * CAP, STEPS, KV_HEADS * HD)
    return (stay_out, moved_out, moved_cache, load_share)


def solution(mesh):
    placed = (
        P("inst", None, "tp"),
        P("inst", None, "tp"),
        P(None, None, "tp"),
        P("inst", None, None, "tp"),
        P("inst", None),
        P("inst", None),
        P("inst", None),
        P("inst", None),
        P("inst", None),
    )
    return jax.shard_map(
        on_device,
        mesh=mesh,
        in_specs=placed,
        out_specs=(
            P("inst", None, "tp"),
            P("inst", None, "tp"),
            P("inst", None, None, "tp"),
            P("inst"),
        ),
        check_vma=False,
    )
```

time: 274 us -> 122 us (0.45)
  Pallas kernels: 151 us -> 34.2 us
  starting transfers between devices: 39.5 us -> 20.3 us
  waiting for transfers between devices: 57.6 us -> 46.4 us
  other arithmetic: 8.42 us -> 5.35 us
    pallas_call x1, Pallas kernels: 66.4 us -> 5.59 us  [build(): pl.pallas_call(build_kernel, out_shape=jax.ShapeDtypeStruct((INST, A_ROWS...]
    pallas_call x1, Pallas kernels: 67.8 us -> 9.38 us  [attend(): pl.pallas_call(attend_kernel, out_shape=(jax.ShapeDtypeStruct((REQS, ROWS...]
    ppermute x11 -> x4, waiting for transfers between devices: 57.6 us -> 8.22 us  [the longest x3 5.65 us: on_device(): lax.ppermute(hidden, 'tp', [(i, (i // 2 + k) % 4 * 2 + i % 2) for i in ra...]
    all_to_all x1, waiting for transfers between devices: 0.01 us -> 38.2 us  [on_device(): lax.all_to_all(first, 'inst', split_axis=0, concat_axis=0, tiled=True)]
    ppermute x11 -> x4, starting transfers between devices: 17.1 us -> 5.88 us  [the longest x3 4.5 us: on_device(): lax.ppermute(hidden, 'tp', [(i, (i // 2 + k) % 4 * 2 + i % 2) for i in ra...]
    all_to_all x1, starting transfers between devices: 9.45 us -> 4.43 us  [on_device(): lax.all_to_all(second, 'inst', split_axis=0, concat_axis=0, tiled=True)]
    concatenate x3 -> x0, other arithmetic: 3.5 us -> none  [on_device(): dup = jnp.concatenate([dup, swap(dup, 'inst', bit)], axis=0)]
    all_to_all x1, starting transfers between devices: 12.9 us -> 9.98 us  [on_device(): lax.all_to_all(first, 'inst', split_axis=0, concat_axis=0, tiled=True)]
  transfers between devices with their start and end apart: 13 -> 6, of which waited for: 6 -> 4; matrix products, arithmetic and copies ran while one was open for 6% -> 9% of each run, Pallas kernels for 26% -> 24%
where the time goes in v2:
time: 122 us; the launch traced here: 121 us
  waiting for transfers between devices  46.4 us (38%)
  Pallas kernels  34.2 us (28%)
  starting transfers between devices  20.3 us (17%)
  between operations  5.98 us (5%)
  other arithmetic  5.35 us (4%)
  local copies, waits for them, and re-layouts  5.18 us (4%)
  matrix products  3.27 us (3%)
    all_to_all x1, waiting for transfers between devices, on_device(): lax.all_to_all(first, 'inst', split_axis=0, concat_axis=0, tiled=True)  38.2 us
    pallas_call x1, Pallas kernels, place_first(): pl.pallas_call(place_kernel, out_shape=(jax.ShapeDtypeStruct((INST * CAP,...  11.8 us
    all_to_all x1, starting transfers between devices, on_device(): lax.all_to_all(first, 'inst', split_axis=0, concat_axis=0, tiled=True)  9.98 us
    pallas_call x1, Pallas kernels, attend(): pl.pallas_call(attend_kernel, out_shape=(jax.ShapeDtypeStruct((REQS, ROWS...  9.38 us
    ppermute x3, waiting for transfers between devices, on_device(): lax.ppermute(hidden, 'tp', [(i, (i // 2 + k) % 4 * 2 + i % 2) for i in ra...  5.65 us
    pallas_call x1, Pallas kernels, build(): pl.pallas_call(build_kernel, out_shape=jax.ShapeDtypeStruct((INST, A_ROWS...  5.59 us
    ppermute x3, starting transfers between devices, on_device(): lax.ppermute(hidden, 'tp', [(i, (i // 2 + k) % 4 * 2 + i % 2) for i in ra...  4.5 us
    all_to_all x1, starting transfers between devices, on_device(): lax.all_to_all(second, 'inst', split_axis=0, concat_axis=0, tiled=True)  4.43 us
  transfers between devices with their start and end apart: 6, of which 4 were waited for; matrix products, arithmetic and copies ran while one was open for 9% of the time, Pallas kernels for 24%

profile of v2, /device:TPU:1, one launch (start us, length us, event | category | flops | bytes accessed | tf_op | source)
XLA Modules:
  0.0 120.9 jit_solution(17266549060136425431)
XLA Ops:
  0.6 0.9 reshape.68
  1.6 3.4 %collective-permute-start.2 = (bf16[44,1024]{1,0:T(8,128)(2,1)S(1)}, bf16[44,1024]{1,0:T(8,128)(2,1)S(1)}, u32[]{:S(2)}, u32[]{:S(2)}) collective-permute-start(bf16[44,1024]{1,0:T(8,128)(2,1)S(1)} %reshape.68), channel_id=1, source_target_pairs={{0,6},{1,7},{2,0},{3,1},{4,2},{5,3},{6,4},{7,5},{8,14},{9,15},{10,... | collective-permute-start | bytes 270344 | tf_op jit(solution)/shard_map/ppermute | solution.py:620
  6.1 0.9 stack_reshape.3
  7.0 3.0 %collective-permute-done.1 = bf16[44,1024]{1,0:T(8,128)(2,1)S(1)} collective-permute-done((bf16[44,1024]{1,0:T(8,128)(2,1)S(1)}, bf16[44,1024]{1,0:T(8,128)(2,1)S(1)}, u32[]{:S(2)}, u32[]{:S(2)}) %collective-permute-start.1) | collective-permute-done | bytes 90144 | tf_op jit(solution)/shard_map/ppermute | solution.py:620
  10.0 2.7 %collective-permute-done = bf16[44,1024]{1,0:T(8,128)(2,1)S(1)} collective-permute-done((bf16[44,1024]{1,0:T(8,128)(2,1)S(1)}, bf16[44,1024]{1,0:T(8,128)(2,1)S(1)}, u32[]{:S(2)}, u32[]{:S(2)}) %collective-permute-start) | collective-permute-done | bytes 90144 | tf_op jit(solution)/shard_map/ppermute | solution.py:620
  12.7 1.4 %collective-permute-start.3 = (bf16[4,44,1024]{2,1,0:T(8,128)(2,1)S(1)}, bf16[4,44,1024]{2,1,0:T(8,128)(2,1)S(1)}, u32[]{:S(2)}, u32[]{:S(2)}) collective-permute-start(bf16[4,44,1024]{2,1,0:T(8,128)(2,1)S(1)} %pad_maximum_fusion.own), channel_id=1, source_target_pairs={{0,1},{1,0},{2,3},{3,2},{4,5},{5,4},{6,7},{7,6},{8,9},{9,8},{10,11... | collective-permute-start | bytes 1081352 | tf_op jit(solution)/shard_map/ppermute | solution.py:624
  14.1 5.6 %build_first.1 = bf16[16,1104,128]{2,1,0:T(8,128)(2,1)} custom-call(s32[1,208]{1,0:T(1,128)} %table.3, s32[1,2]{1,0:T(1,128)} %longs.3, s32[1,20]{1,0:T(1,128)} %shorts.3, s32[1,20]{1,0:T(1,128)} %order.3, s32[1,16]{1,0:T(1,128)} %bitcast.40, bf16[208,256,128]{2,1,0:T(8,128)(2,1)} %bitcast.25), custom_call_target="tpu_custom_call" | custom-call | bytes 9437184 | tf_op jit(solution)/shard_map/build_first/pallas_call | solution.py:154
  19.7 2.6 %collective-permute-done.3.mate = bf16[4,44,1024]{2,1,0:T(8,128)(2,1)S(1)} collective-permute-done((bf16[4,44,1024]{2,1,0:T(8,128)(2,1)S(1)}, bf16[4,44,1024]{2,1,0:T(8,128)(2,1)S(1)}, u32[]{:S(2)}, u32[]{:S(2)}) %collective-permute-start.3) | collective-permute-done | bytes 360480 | tf_op jit(solution)/shard_map/ppermute | solution.py:624
  22.3 0.7 copy-done.5
  23.1 10.0 %all-to-all-start.1 = ((bf16[16,1104,128]{2,1,0:T(8,128)(2,1)}), bf16[16,1104,128]{2,1,0:T(8,128)(2,1)}, u32[]{:S(2)}, u32[]{:S(2)}) async-start(bf16[16,1104,128]{2,1,0:T(8,128)(2,1)} %build_first.1), calls=%async_computation.1 | async-start | bytes 9043968 | tf_op jit(solution)/shard_map/all_to_all | solution.py:627
  33.9 2.1 %join_hidden.1 = bf16[44,8192]{1,0:T(8,128)(2,1)} custom-call(s32[1]{0:T(128)} %bitcast.1.here, bf16[4,44,1024]{2,1,0:T(8,128)(2,1)} %copy-done.4, bf16[4,44,1024]{2,1,0:T(8,128)(2,1)} %copy-done.5), custom_call_target="tpu_custom_call" | custom-call | tf_op jit(solution)/shard_map/join_hidden/pallas_call | solution.py:389
  35.9 3.3 %fusion.2 = bf16[44,2,128]{2,0,1:T(8,128)(2,1)S(1)} fusion(bf16[8192,2,128]{2,1,0:T(2,128)(2,1)} %param.13, bf16[44,8192]{1,0:T(8,128)(2,1)} %join_hidden.1), kind=kOutput, calls=%fused_computation.2 | convolution fusion | flops 184560640 | bytes 4937728 | tf_op jit(solution)/shard_map/rd,dcn->rcn/dot_general | solution.py:630
  39.4 9.4 %attend_all.1 = (bf16[22,16,128]{2,1,0:T(8,128)(2,1)S(1)}, bf16[32,32,128]{2,1,0:T(8,128)(2,1)S(1)}) custom-call(s32[1,208]{1,0:T(1,128)S(1)} %copy-done.8, s32[1,2]{1,0:T(1,128)S(1)} %copy-done.1, s32[1,20]{1,0:T(1,128)S(1)} %copy-done.2, s32[1,20]{1,0:T(1,128)S(1)} %copy-done.9, s32[1,16]{1,0:T(1,128)S(1)} %bitcast.41, ...), custom_call_target="tpu_custom_call" | custom-call | flops 218103808 | bytes 14680064 | tf_op jit(solution)/shard_map/attend_all/pallas_call | solution.py:353
  48.8 0.7 copy-done
  49.5 38.2 %all-to-all-done.1.block.received = bf16[16,1104,128]{2,1,0:T(8,128)(2,1)} async-done(((bf16[16,1104,128]{2,1,0:T(8,128)(2,1)}), bf16[16,1104,128]{2,1,0:T(8,128)(2,1)}, u32[]{:S(2)}, u32[]{:S(2)}) %all-to-all-start.1) | async-done | bytes 4522016 | tf_op jit(solution)/shard_map/all_to_all | solution.py:627
  87.7 3.4 %route_pieces.1 = bf16[16,320,128]{2,1,0:T(8,128)(2,1)} custom-call(bf16[16,1104,128]{2,1,0:T(8,128)(2,1)} %all-to-all-done.1.block.received, bf16[32,32,128]{2,1,0:T(8,128)(2,1)} %copy-done), custom_call_target="tpu_custom_call" | custom-call | bytes 2097152 | tf_op jit(solution)/shard_map/route_pieces/pallas_call | solution.py:423
  91.0 4.4 %all-to-all-start.2 = ((bf16[16,320,128]{2,1,0:T(8,128)(2,1)}), bf16[16,320,128]{2,1,0:T(8,128)(2,1)S(1)}, u32[]{:S(2)}, u32[]{:S(2)}) async-start(bf16[16,320,128]{2,1,0:T(8,128)(2,1)} %route_pieces.1), calls=%async_computation.2 | async-start | bytes 2621440 | tf_op jit(solution)/shard_map/all_to_all | solution.py:644
  97.5 0.7 reshape.72
  98.2 0.8 fusion.10
  98.9 0.7 fusion.7
  105.0 11.8 %place_first.1 = (bf16[32,2,512,128]{3,2,1,0:T(8,128)(2,1)}, bf16[16,2,32,128]{3,2,1,0:T(8,128)(2,1)S(1)}) custom-call(s32[32]{0:T(128)S(1)} %reshape.74.lens, bf16[16,1104,128]{2,1,0:T(8,128)(2,1)} %all-to-all-done.1.block.received), custom_call_target="tpu_custom_call" | custom-call | bytes 13631488 | tf_op jit(solution)/shard_map/place_first/pallas_call | solution.py:488
  116.9 2.2 %conditional.1 = (bf16[32,2,512,128]{3,2,1,0:T(8,128)(2,1)}, bf16[32,2,1024]{2,1,0:T(2,128)(2,1)S(1)}) conditional(s32[]{:T(128)} %convert_element_type.35, (s32[32]{0:T(128)S(1)}, bf16[16,2,32,128]{3,2,1,0:T(8,128)(2,1)S(1)}, bf16[16,320,128]{2,1,0:T(8,128)(2,1)S(1)}, bf16[32,2,512,128]{3,2,1,0:T(8,128)(2,1)}) %tuple.22, (s32[1,208]{1,0:T(1,128)S(1)}, ...), branch_computations={%region_5.6_spmd, %region_6.7_spmd} | conditional | bytes 67371104 | solution.py:678
  116.9 1.9 %settle_short.1 = (bf16[32,2,512,128]{3,2,1,0:T(8,128)(2,1)}, bf16[32,16,128]{2,1,0:T(8,128)(2,1)S(1)}) custom-call(s32[32]{0:T(128)S(1)} %get-tuple-element.29.refs_0_, bf16[16,2,32,128]{3,2,1,0:T(8,128)(2,1)S(1)} %get-tuple-element.30.refs_1_.refs_3_, bf16[16,320,128]{2,1,0:T(8,128)(2,1)S(1)} %get-tuple-element.31.refs_2_, ...), custom_call_target="tpu_custom_call", output_to_operand_aliasing={{0}: (4, {})} | custom-call | tf_op jit(solution)/shard_map/cond/branch_0_fun/settle_short/pallas_call | solution.py:579
  119.1 0.6 copy-done.6
  (44 shorter events, 5.6 us)
Async XLA Ops:
  1.6 5.4 %collective-permute-start.2 = (bf16[44,1024]{1,0:T(8,128)(2,1)S(1)}, bf16[44,1024]{1,0:T(8,128)(2,1)S(1)}, u32[]{:S(2)}, u32[]{:S(2)}) collective-permute-start(bf16[44,1024]{1,0:T(8,128)(2,1)S(1)} %reshape.68), channel_id=1, source_target_pairs={{0,6},{1,7},{2,0},{3,1},{4,2},{5,3},{6,4},{7,5},{8,14},{9,15},{10,... | collective-permute-start | bytes 270344 | tf_op jit(solution)/shard_map/ppermute | solution.py:620
  4.9 5.1 %collective-permute-start.1 = (bf16[44,1024]{1,0:T(8,128)(2,1)S(1)}, bf16[44,1024]{1,0:T(8,128)(2,1)S(1)}, u32[]{:S(2)}, u32[]{:S(2)}) collective-permute-start(bf16[44,1024]{1,0:T(8,128)(2,1)S(1)} %reshape.68), channel_id=1, source_target_pairs={{0,4},{1,5},{2,6},{3,7},{4,0},{5,1},{6,2},{7,3},{8,12},{9,13},{10,... | collective-permute-start | bytes 270344 | tf_op jit(solution)/shard_map/ppermute | solution.py:620
  5.5 7.2 %collective-permute-start = (bf16[44,1024]{1,0:T(8,128)(2,1)S(1)}, bf16[44,1024]{1,0:T(8,128)(2,1)S(1)}, u32[]{:S(2)}, u32[]{:S(2)}) collective-permute-start(bf16[44,1024]{1,0:T(8,128)(2,1)S(1)} %reshape.68), channel_id=1, source_target_pairs={{0,2},{1,3},{2,4},{3,5},{4,6},{5,7},{6,0},{7,1},{8,10},{9,11},{10,... | collective-permute-start | bytes 270344 | tf_op jit(solution)/shard_map/ppermute | solution.py:620
  12.7 7.0 %copy-start.4 = (bf16[4,44,1024]{2,1,0:T(8,128)(2,1)}, bf16[4,44,1024]{2,1,0:T(8,128)(2,1)S(1)}, u32[]{:S(2)}) copy-start(bf16[4,44,1024]{2,1,0:T(8,128)(2,1)S(1)} %pad_maximum_fusion.own) | copy-start | bytes 1081348
  12.7 9.6 %collective-permute-start.3 = (bf16[4,44,1024]{2,1,0:T(8,128)(2,1)S(1)}, bf16[4,44,1024]{2,1,0:T(8,128)(2,1)S(1)}, u32[]{:S(2)}, u32[]{:S(2)}) collective-permute-start(bf16[4,44,1024]{2,1,0:T(8,128)(2,1)S(1)} %pad_maximum_fusion.own), channel_id=1, source_target_pairs={{0,1},{1,0},{2,3},{3,2},{4,5},{5,4},{6,7},{7,6},{8,9},{9,8},{10,11... | collective-permute-start | bytes 1081352 | tf_op jit(solution)/shard_map/ppermute | solution.py:624
  19.7 13.4 %copy-start.1 = (s32[1,2]{1,0:T(1,128)S(1)}, s32[1,2]{1,0:T(1,128)}, u32[]{:S(2)}) copy-start(s32[1,2]{1,0:T(1,128)} %longs.3) | copy-start | bytes 28
  19.7 14.0 %copy-start.7 = (bf16[22,2,1024]{2,1,0:T(2,128)(2,1)S(1)}, bf16[22,2,1024]{2,1,0:T(2,128)(2,1)}, u32[]{:S(2)}) copy-start(bf16[22,2,1024]{2,1,0:T(2,128)(2,1)} %param.11) | copy-start | bytes 270340
  19.7 14.1 %copy-start.9 = (s32[1,20]{1,0:T(1,128)S(1)}, s32[1,20]{1,0:T(1,128)}, u32[]{:S(2)}) copy-start(s32[1,20]{1,0:T(1,128)} %order.3) | copy-start | bytes 244
  22.3 0.8 copy-start.5
  23.1 64.6 %all-to-all-start.1 = ((bf16[16,1104,128]{2,1,0:T(8,128)(2,1)}), bf16[16,1104,128]{2,1,0:T(8,128)(2,1)}, u32[]{:S(2)}, u32[]{:S(2)}) async-start(bf16[16,1104,128]{2,1,0:T(8,128)(2,1)} %build_first.1), calls=%async_computation.1 | async-start | bytes 9043968 | tf_op jit(solution)/shard_map/all_to_all | solution.py:627
  33.0 6.3 %copy-start.2 = (s32[1,20]{1,0:T(1,128)S(1)}, s32[1,20]{1,0:T(1,128)}, u32[]{:S(2)}) copy-start(s32[1,20]{1,0:T(1,128)} %shorts.3) | copy-start | bytes 244
  33.1 6.3 %copy-start.8 = (s32[1,208]{1,0:T(1,128)S(1)}, s32[1,208]{1,0:T(1,128)}, u32[]{:S(2)}) copy-start(s32[1,208]{1,0:T(1,128)} %table.3) | copy-start | bytes 2500
  33.1 6.3 %copy-start.10 = (s32[16,1]{0,1:T(1,128)S(1)}, s32[16,1]{0,1:T(1,128)}, u32[]{:S(2)}) copy-start(s32[16,1]{0,1:T(1,128)} %param.19) | copy-start | bytes 196
  48.8 0.7 copy-start
  91.0 25.8 %all-to-all-start.2 = ((bf16[16,320,128]{2,1,0:T(8,128)(2,1)}), bf16[16,320,128]{2,1,0:T(8,128)(2,1)S(1)}, u32[]{:S(2)}, u32[]{:S(2)}) async-start(bf16[16,320,128]{2,1,0:T(8,128)(2,1)} %route_pieces.1), calls=%async_computation.2 | async-start | bytes 2621440 | tf_op jit(solution)/shard_map/all_to_all | solution.py:644
  119.1 0.7 copy-start.6

commit v3 on v2

--- a/solution.py
+++ b/solution.py
@@ -51,13 +51,15 @@
     return slot
 
 
-def build_kernel(
-    table, longs, shorts, order, dest, pool, out, count, held, extra, stage, sems, extra_sems, out_sems, stage_sem
-):
+def build_kernel(part, table, longs, shorts, order, dest, pool, *refs):
+    out, count, held, extra, stage, sems, extra_sems, out_sems, stage_sem = refs[part:]
+    half = MIG // 2
+    begin_at, end_at = (half, MIG) if part else (0, half)
+
     def load(k, p):
         page = table[0, LONG * MAXPG + order[0, k] * MIGPG + p]
         return pltpu.make_async_copy(
-            pool.at[page], held.at[dest[0, k], pl.ds(p * 2 * PAGE, 2 * PAGE)], sems.at[k * MIGPG + p]
+            pool.at[page], held.at[k - begin_at, pl.ds(p * 2 * PAGE, 2 * PAGE)], sems.at[k * MIGPG + p]
         )
 
     def load_extra(k, p):
@@ -65,9 +67,8 @@
         return pltpu.make_async_copy(pool.at[page], extra.at[p], extra_sems.at[p])
 
     def send(k):
-        to = dest[0, k]
         return pltpu.make_async_copy(
-            held.at[to], out.at[to, pl.ds(0, 2 * MIGLEN)], out_sems.at[k]
+            held.at[k - begin_at], out.at[dest[0, k], pl.ds(0, 2 * MIGLEN)], out_sems.at[k]
         )
 
     clear(count)
@@ -75,21 +76,21 @@
     def begin(k, dup_at):
         slot = take_slot(count, dest[0, k])
 
-        @pl.when(slot == 0)
+        @pl.when((slot == 0) & (k >= begin_at))
         def _():
             for p in range(MIGPG):
                 load(k, p).start()
 
         first = (slot == 1) & (dup_at < 0)
-
-        @pl.when(first)
-        def _():
-            for p in range(MIGPG):
-                load_extra(k, p).start()
+        if part:
+            @pl.when(first)
+            def _():
+                for p in range(MIGPG):
+                    load_extra(k, p).start()
 
         return jnp.where(first, k, dup_at)
 
-    dup_at = lax.fori_loop(0, MIG, begin, jnp.int32(-1))
+    dup_at = lax.fori_loop(0, end_at, begin, jnp.int32(-1))
     clear(count)
     lane = lax.broadcasted_iota(jnp.int32, (16, 128), 1)
 
@@ -98,7 +99,7 @@
         slot = take_slot(count, to)
         length = shorts[0, order[0, k]]
 
-        @pl.when(slot == 0)
+        @pl.when((slot == 0) & (k >= begin_at))
         def _():
             for p in range(MIGPG):
                 load(k, p).wait()
@@ -108,57 +109,62 @@
         row = jnp.where(lane == at, length & 255, row)
         return jnp.where(lane == at + 32, length >> 8, row)
 
-    row = lax.fori_loop(0, MIG, each, jnp.zeros((16, 128), jnp.int32))
-    total = jnp.int32(STEPS * REQS)
-    for i in range(LONG):
-        total = total + longs[0, i]
-    for i in range(SHORT):
-        total = total + shorts[0, i]
-    row = jnp.where(lane == 64, total & 127, row)
-    row = jnp.where(lane == 65, (total >> 7) & 127, row)
-    row = jnp.where(lane == 66, total >> 14, row)
-    dup_to = jnp.where(dup_at >= 0, dest[0, jnp.maximum(dup_at, 0)] + 1, 0)
-    row = jnp.where(lane == 67, dup_to, row)
-    tables = row.astype(jnp.float32).astype(jnp.bfloat16)
-
-    @pl.when(dup_at >= 0)
-    def _():
-        for p in range(MIGPG):
-            load_extra(dup_at, p).wait()
+    row = lax.fori_loop(0, end_at, each, jnp.zeros((16, 128), jnp.int32))
+    if part:
+        last = pltpu.make_async_copy(stage, out.at[:, pl.ds(A_DUP, A_ROWS - A_DUP)], stage_sem)
+        total = jnp.int32(STEPS * REQS)
+        for i in range(LONG):
+            total = total + longs[0, i]
+        for i in range(SHORT):
+            total = total + shorts[0, i]
+        row = jnp.where(lane == 64, total & 127, row)
+        row = jnp.where(lane == 65, (total >> 7) & 127, row)
+        row = jnp.where(lane == 66, total >> 14, row)
+        dup_to = jnp.where(dup_at >= 0, dest[0, jnp.maximum(dup_at, 0)] + 1, 0)
+        row = jnp.where(lane == 67, dup_to, row)
+        tables = row.astype(jnp.float32).astype(jnp.bfloat16)
+
+        @pl.when(dup_at >= 0)
+        def _():
+            for p in range(MIGPG):
+                load_extra(dup_at, p).wait()
+            for m in range(INST):
+                for c in range(2):
+                    stage[m, pl.ds(c * PIECE, PIECE)] = extra[
+                        m // MIGPG, pl.ds(c * PAGE + m % MIGPG * PIECE, PIECE)
+                    ]
+
         for m in range(INST):
-            for c in range(2):
-                stage[m, pl.ds(c * PIECE, PIECE)] = extra[
-                    m // MIGPG, pl.ds(c * PAGE + m % MIGPG * PIECE, PIECE)
-                ]
-
-    for m in range(INST):
-        stage[m, pl.ds(2 * PIECE, 16)] = tables
-    last = pltpu.make_async_copy(stage, out.at[:, pl.ds(A_DUP, A_ROWS - A_DUP)], stage_sem)
-    last.start()
+            stage[m, pl.ds(2 * PIECE, 16)] = tables
+        last.start()
     clear(count)
 
     def finish(k, carry):
         slot = take_slot(count, dest[0, k])
 
-        @pl.when(slot == 0)
+        @pl.when((slot == 0) & (k >= begin_at))
         def _():
             send(k).wait()
 
         return carry
 
-    lax.fori_loop(0, MIG, finish, 0)
-    last.wait()
-
-
-def build(tables, pool):
+    lax.fori_loop(0, end_at, finish, 0)
+    if part:
+        last.wait()
+
+
+def build(part, tables, pool, *earlier):
+    def kernel(*refs):
+        build_kernel(part, *refs)
+
     return pl.pallas_call(
-        build_kernel,
+        kernel,
         out_shape=jax.ShapeDtypeStruct((INST, A_ROWS, HD), jnp.bfloat16),
-        in_specs=[spec(SMEM)] * 5 + [spec(pl.ANY)],
+        in_specs=[spec(SMEM)] * 5 + [spec(pl.ANY)] + [spec(pltpu.HBM)] * len(earlier),
         out_specs=spec(pltpu.HBM),
         scratch_shapes=[
             pltpu.SMEM((INST,), jnp.int32),
-            pltpu.VMEM((INST, 2 * MIGLEN, HD), jnp.bfloat16),
+            pltpu.VMEM((MIG // 2, 2 * MIGLEN, HD), jnp.bfloat16),
             pltpu.VMEM((MIGPG, 2 * PAGE, HD), jnp.bfloat16),
             pltpu.VMEM((INST, A_ROWS - A_DUP, HD), jnp.bfloat16),
             pltpu.SemaphoreType.DMA((MIG * MIGPG,)),
@@ -166,10 +172,11 @@
             pltpu.SemaphoreType.DMA((MIG,)),
             pltpu.SemaphoreType.DMA(()),
         ],
+        input_output_aliases={6: 0} if part else {},
         compiler_params=pltpu.CompilerParams(vmem_limit_bytes=60 << 20),
         cost_estimate=pl.CostEstimate(flops=0, bytes_accessed=9 << 20, transcendentals=0),
-        name="build_first",
-    )(*tables, pool)
+        name="build_rest" if part else "build_half",
+    )(*tables, pool, *earlier)
 
 
 def second_kernel(table, order, dest, pool, out, count, held, sems, out_sems):
@@ -373,26 +380,25 @@
     )(*tables, query, keys_values, values, pool)
 
 
-def join_kernel(here, own, mate, out):
+def join_kernel(here, blocks, out):
     me = here[0]
-    width = own.shape[2]
-    for k in range(4):
-        for other in range(2):
-            x = (me // 2 + 4 - k) % 4
-            y = (me + other) % 2
-            at = pl.multiple_of((x * 2 + y) * width, width)
-            out[:, pl.ds(at, width)] = (mate if other else own)[k]
-
-
-def join(here, own, mate):
-    _, rows, width = own.shape
+    width = blocks.shape[2]
+    for k in range(8):
+        x = (me // 2 + 4 - k % 4) % 4
+        y = (me + k // 4) % 2
+        at = pl.multiple_of((x * 2 + y) * width, width)
+        out[:, pl.ds(at, width)] = blocks[k]
+
+
+def join(here, blocks):
+    _, rows, width = blocks.shape
     return pl.pallas_call(
         join_kernel,
         out_shape=jax.ShapeDtypeStruct((rows, width * 8), jnp.bfloat16),
-        in_specs=[spec(SMEM), spec(VMEM), spec(VMEM)],
+        in_specs=[spec(SMEM), spec(VMEM)],
         out_specs=spec(VMEM),
         name="join_hidden",
-    )(here, own, mate)
+    )(here, blocks)
 
 
 def route_kernel(received, side, out, small, count, sem):
@@ -435,6 +441,56 @@
     )(received, side)
 
 
+def decode_kernel(here, longs, shorts, order, received, lens, load, small, sem):
+    copy = pltpu.make_async_copy(received.at[:, pl.ds(A_META, 16)], small, sem)
+    copy.start()
+    resident = jnp.int32(STEPS * (LONG + SHORT - MIG))
+    for i in range(LONG):
+        resident = resident + longs[0, i]
+    for i in range(MIG, SHORT):
+        resident = resident + shorts[0, order[0, i]]
+    copy.wait()
+
+    def total(x, axis=None):
+        return jnp.sum(x, axis=axis, keepdims=True)
+
+    x = jnp.max(small[...].astype(jnp.float32), axis=1)
+    lane = lax.broadcasted_iota(jnp.int32, x.shape, 1)
+    table = jnp.where(lane < INST * CAP, x + 256.0 * pltpu.roll(x, 96, 1), 0.0)
+    own = resident.astype(jnp.float32)
+    result = jnp.zeros_like(x)
+    for slot in range(CAP):
+        length = total(jnp.where(lane == here[0] * CAP + slot, table, 0.0), 1)
+        result = jnp.where(lane == slot, length, result)
+        own = own + total(jnp.where(length > 0.0, length + STEPS, 0.0))
+    lens[...] = result.astype(jnp.int32)
+    digits = jnp.where(lane == 64, 1.0, jnp.where(lane == 65, 128.0, jnp.where(lane == 66, 16384.0, 0.0)))
+    share = own * INST / total(x * digits)
+    double = jnp.where((table > 0.0) & (lane % 2 == 1), 1.0, 0.0)
+    sends = jnp.max(total(double, 1), keepdims=True)
+    takes = jnp.max(total(double, 0), keepdims=True)
+    over = jnp.where((sends > 1.0) | (takes > DUPS), 1.0, 0.0)
+    row = lax.broadcasted_iota(jnp.int32, (8, 128), 0)
+    load[...] = jnp.where(row == 0, share, over)
+
+
+def decode(here, longs, shorts, order, received):
+    return pl.pallas_call(
+        decode_kernel,
+        out_shape=(
+            jax.ShapeDtypeStruct((INST, 128), jnp.int32),
+            jax.ShapeDtypeStruct((8, 128), jnp.float32),
+        ),
+        in_specs=[spec(SMEM)] * 4 + [spec(pl.ANY)],
+        out_specs=(spec(VMEM), spec(VMEM)),
+        scratch_shapes=[
+            pltpu.VMEM((INST, 16, HD), jnp.bfloat16),
+            pltpu.SemaphoreType.DMA(()),
+        ],
+        name="decode_tables",
+    )(here, longs, shorts, order, received)
+
+
 def window_base(length):
     return pl.multiple_of(jnp.minimum(length // 16 * 16, MIGLEN - 32), 16)
 
@@ -468,7 +524,7 @@
 
 def place_kernel(lens, block, cache, window):
     s = pl.program_id(0)
-    length = lens[s * CAP]
+    length = lens[s, 0]
 
     def read(p, c):
         return block[0, pl.ds((p * 2 + c) * PAGE, PAGE)]
@@ -512,7 +568,7 @@
     def patch_copy(s, c):
         return pltpu.make_async_copy(
             patched.at[s, c],
-            cache.at[s * CAP, c, pl.ds(window_base(lens[s * CAP]), 32)],
+            cache.at[s * CAP, c, pl.ds(window_base(lens[s, 0]), 32)],
             sems.at[s * 2 + c],
         )
 
@@ -520,7 +576,7 @@
         return pltpu.make_async_copy(dups.at[s], cache.at[s * CAP + 1], dup_sems.at[s])
 
     for s in range(INST):
-        length = lens[s * CAP]
+        length = lens[s, 0]
 
         @pl.when(length > 0)
         def _():
@@ -535,7 +591,7 @@
 
     order = jnp.int32(0)
     for s in range(INST):
-        length = lens[s * CAP + 1]
+        length = lens[s, 1]
         rank = jnp.minimum(order, DUPS - 1)
         order = order + (length > 0).astype(jnp.int32)
 
@@ -558,16 +614,16 @@
 
     for s in range(INST):
         for slot in range(CAP):
-            filled = lens[s * CAP + slot] > 0
+            filled = lens[s, slot] > 0
             rows = second[s, pl.ds(slot * 32, ROWS)]
             out[s * CAP + slot] = jnp.where(filled, rows, jnp.zeros_like(rows))
     for s in range(INST):
-        @pl.when(lens[s * CAP] > 0)
+        @pl.when(lens[s, 0] > 0)
         def _():
             for c in range(2):
                 patch_copy(s, c).wait()
 
-        @pl.when(lens[s * CAP + 1] > 0)
+        @pl.when(lens[s, 1] > 0)
         def _():
             dup_copy(s).wait()
 
@@ -613,20 +669,25 @@
     tables = (page_table, long_lengths, short_lengths, mig_order, targets)
     pages = kv_pool.reshape(PAGES, 2 * PAGE, HD)
 
-    hidden = hidden_in.reshape(REQS * STEPS, -1)
-    pieces = [hidden]
-    for k in range(1, 4):
-        pieces.append(
-            lax.ppermute(hidden, "tp", [(i, (i // 2 + k) % 4 * 2 + i % 2) for i in range(8)])
-        )
-    own = jnp.stack(pieces)
-    own, late_targets = lax.optimization_barrier((own, targets))
-    mate = lax.ppermute(own, "tp", [(i, i ^ 1) for i in range(8)])
-    first = build((*tables[:4], late_targets), pages)
-    first, mate = lax.optimization_barrier((first, mate))
+    def from_x(value, k):
+        return lax.ppermute(value, "tp", [(i, (i // 2 + k) % 4 * 2 + i % 2) for i in range(8)])
+
+    def from_y(value):
+        return lax.ppermute(value, "tp", [(i, i ^ 1) for i in range(8)])
+
+    near = [hidden_in, from_x(hidden_in, 1), from_x(hidden_in, 2), from_x(hidden_in, 3)]
+    far = [from_y(hidden_in)]
+    half = build(0, tables, pages)
+    near[2], far[0], late_targets, half = lax.optimization_barrier(
+        (near[2], far[0], targets, half)
+    )
+    far += [from_x(far[0], 1), from_y(near[2]), from_x(far[0], 3)]
+    first = build(1, (*tables[:4], late_targets), pages, half)
+    first, *blocks = lax.optimization_barrier((first, *near[1:], *far))
+    blocks = jnp.stack([hidden_in, *blocks]).reshape(8, REQS * STEPS, -1)
     got_first = lax.all_to_all(first, "inst", split_axis=0, concat_axis=0, tiled=True)
 
-    hidden_all = join(tp_index.reshape(1), own, mate)
+    hidden_all = join(tp_index.reshape(1), blocks)
     fresh = jnp.einsum(
         "rd,dcn->rcn", hidden_all, kv_weight, preferred_element_type=jnp.float32
     ).astype(jnp.bfloat16)
@@ -643,25 +704,11 @@
     second = route(got_first, side)
     got_second = lax.all_to_all(second, "inst", split_axis=0, concat_axis=0, tiled=True)
 
-    meta = got_first[:, A_META].astype(jnp.float32).astype(jnp.int32)
-    lengths = (meta[:, :32] + 256 * meta[:, 32:64]).reshape(INST, INST, CAP)
-    all_load = jnp.sum(meta[:, 64] + 128 * meta[:, 65] + 16384 * meta[:, 66])
-    doubled = (lengths[:, :, 1] > 0).astype(jnp.int32)
-    overflow = (jnp.max(jnp.sum(doubled, axis=0)) > DUPS) | (jnp.max(jnp.sum(doubled, axis=1)) > 1)
-    index = jnp.arange(INST)
-    arriving = jnp.sum(
-        jnp.where(index[None, :, None] == inst_index, lengths, 0), axis=1
-    ).reshape(INST * CAP)
-    staying = jnp.any(
-        mig_order[0, MIG:][:, None] == jnp.arange(SHORT)[None, :], axis=0
+    arriving, load = decode(
+        inst_index.reshape(1), long_lengths, short_lengths, mig_order, got_first
     )
-    resident = (
-        jnp.sum(long_lengths)
-        + jnp.sum(jnp.where(staying, short_lengths[0], 0))
-        + STEPS * (LONG + SHORT - MIG)
-    )
-    own_load = resident + jnp.sum(jnp.where(arriving > 0, arriving + STEPS, 0))
-    load_share = (own_load.astype(jnp.float32) * INST / all_load.astype(jnp.float32)).reshape(1)
+    load_share = load[0, :1]
+    overflow = load[1, 0] > 0.5
 
     cache, window = place_first(arriving, got_first)
 

time: 122 us -> 116 us (0.951)
  waiting for transfers between devices: 46.4 us -> 40.8 us
  other arithmetic: 5.35 us -> 0 us
  Pallas kernels: 34.2 us -> 39.5 us
  between operations: 5.98 us -> 1.67 us
  starting transfers between devices: 20.3 us -> 24.6 us
    ppermute x4 -> x7, waiting for transfers between devices: 8.22 us -> 0.19 us  [the longest x5 0.19 us: from_x(): lax.ppermute(value, 'tp', [(i, (i // 2 + k) % 4 * 2 + i % 2) for i in ran...]
    pallas_call x1 -> x3, Pallas kernels: 5.59 us -> 10.7 us  [the longest x2 8.24 us: build(): pl.pallas_call(kernel, out_shape=jax.ShapeDtypeStruct((INST, A_ROWS, HD),...]
    all_to_all x1, waiting for transfers between devices: 0.01 us -> 3.13 us  [on_device(): lax.all_to_all(second, 'inst', split_axis=0, concat_axis=0, tiled=True)]
    reduce_sum x6 -> x0, other arithmetic: 3.09 us -> none  [the longest x1 0.71 us: on_device(): all_load = jnp.sum(meta[:, 64] + 128 * meta[:, 65] + 16384 * meta[:, 66])]
    ppermute x4 -> x7, starting transfers between devices: 5.88 us -> 8.74 us  [the longest x5 6.28 us: from_x(): lax.ppermute(value, 'tp', [(i, (i // 2 + k) % 4 * 2 + i % 2) for i in ran...]
    all_to_all x1, starting transfers between devices: 9.98 us -> 11.5 us  [on_device(): lax.all_to_all(first, 'inst', split_axis=0, concat_axis=0, tiled=True)]
    slice x0 -> x1, local copies, waits for them, and re-layouts: none -> 1.28 us  [on_device(): load_share = load[0, :1]]
    reduce_max x2 -> x0, other arithmetic: 1.27 us -> none  [the longest x1 0.64 us: on_device(): jnp.max(jnp.sum(doubled, axis=0)) > DUPS]
  transfers between devices with their start and end apart: 6 -> 9, of which waited for: 4 -> 3; matrix products, arithmetic and copies ran while one was open for 9% -> 5% of each run, Pallas kernels for 24% -> 30%
where the time goes in v3:
time: 116 us; the launch traced here: 115 us
  waiting for transfers between devices  40.8 us (35%)
  Pallas kernels  39.5 us (34%)
  starting transfers between devices  24.6 us (21%)
  local copies, waits for them, and re-layouts  4.79 us (4%)
  matrix products  3.27 us (3%)
  between operations  1.67 us (1%)
    all_to_all x1, waiting for transfers between devices, on_device(): lax.all_to_all(first, 'inst', split_axis=0, concat_axis=0, tiled=True)  37.5 us
    pallas_call x1, Pallas kernels, place_first(): pl.pallas_call(place_kernel, out_shape=(jax.ShapeDtypeStruct((INST * CAP,...  12 us
    all_to_all x1, starting transfers between devices, on_device(): lax.all_to_all(first, 'inst', split_axis=0, concat_axis=0, tiled=True)  11.5 us
    pallas_call x1, Pallas kernels, attend(): pl.pallas_call(attend_kernel, out_shape=(jax.ShapeDtypeStruct((REQS, ROWS...  9.37 us
    pallas_call x2, Pallas kernels, build(): pl.pallas_call(kernel, out_shape=jax.ShapeDtypeStruct((INST, A_ROWS, HD),...  8.24 us
    ppermute x5, starting transfers between devices, from_x(): lax.ppermute(value, 'tp', [(i, (i // 2 + k) % 4 * 2 + i % 2) for i in ran...  6.28 us
    all_to_all x1, starting transfers between devices, on_device(): lax.all_to_all(second, 'inst', split_axis=0, concat_axis=0, tiled=True)  4.43 us
    pallas_call x1, Pallas kernels, route(): pl.pallas_call(route_kernel, out_shape=jax.ShapeDtypeStruct((INST, B_ROWS...  3.34 us
  transfers between devices with their start and end apart: 9, of which 3 were waited for; matrix products, arithmetic and copies ran while one was open for 5% of the time, Pallas kernels for 30%

profile of v3, /device:TPU:1, one launch (start us, length us, event | category | flops | bytes accessed | tf_op | source)
XLA Modules:
  0.0 114.9 jit_solution(12586919089469171220)
XLA Ops:
  0.6 2.2 %collective-permute-start.1 = (bf16[22,2,1024]{2,1,0:T(2,128)(2,1)}, bf16[22,2,1024]{2,1,0:T(2,128)(2,1)S(1)}, u32[]{:S(2)}, u32[]{:S(2)}) collective-permute-start(bf16[22,2,1024]{2,1,0:T(2,128)(2,1)} %param.12), channel_id=1, source_target_pairs={{0,1},{1,0},{2,3},{3,2},{4,5},{5,4},{6,7},{7,6},{8,9},{9,8},{10,11... | collective-permute-start | bytes 270344 | tf_op jit(solution)/shard_map/ppermute | solution.py:676
  2.8 2.7 %collective-permute-start = (bf16[22,2,1024]{2,1,0:T(2,128)(2,1)}, bf16[22,2,1024]{2,1,0:T(2,128)(2,1)S(1)}, u32[]{:S(2)}, u32[]{:S(2)}) collective-permute-start(bf16[22,2,1024]{2,1,0:T(2,128)(2,1)} %param.12), channel_id=1, source_target_pairs={{0,4},{1,5},{2,6},{3,7},{4,0},{5,1},{6,2},{7,3},{8,12},{9,13},{10,... | collective-permute-start | bytes 270344 | tf_op jit(solution)/shard_map/ppermute | solution.py:673
  5.6 0.9 collective-permute-start.3
  6.4 0.6 collective-permute-start.2
  7.1 3.9 %build_half.1.refs_6_ = bf16[16,1104,128]{2,1,0:T(8,128)(2,1)} custom-call(s32[1,208]{1,0:T(1,128)} %table.1, s32[1,2]{1,0:T(1,128)} %longs.3, s32[1,20]{1,0:T(1,128)} %shorts.3, s32[1,20]{1,0:T(1,128)} %order.3, s32[1,16]{1,0:T(1,128)} %bitcast.25, bf16[208,256,128]{2,1,0:T(8,128)(2,1)} %bitcast.16), custom_call_target="tpu_custom_call" | custom-call | bytes 9437184 | tf_op jit(solution)/shard_map/build_half/pallas_call | solution.py:160
  11.3 2.1 %collective-permute-start.6 = (bf16[22,2,1024]{2,1,0:T(2,128)(2,1)S(1)}, bf16[22,2,1024]{2,1,0:T(2,128)(2,1)S(1)}, u32[]{:S(2)}, u32[]{:S(2)}) collective-permute-start(bf16[22,2,1024]{2,1,0:T(2,128)(2,1)S(1)} %collective-permute-done.1), channel_id=1, source_target_pairs={{0,6},{1,7},{2,0},{3,1},{4,2},{5,3},{6,4},{7,5},{8,14},{9,15},{10,... | collective-permute-start | bytes 270344 | tf_op jit(solution)/shard_map/ppermute | solution.py:673
  13.3 4.3 %build_rest.1 = bf16[16,1104,128]{2,1,0:T(8,128)(2,1)} custom-call(s32[1,208]{1,0:T(1,128)S(1)} %copy-done.8, s32[1,2]{1,0:T(1,128)} %longs.3, s32[1,20]{1,0:T(1,128)} %shorts.3, s32[1,20]{1,0:T(1,128)S(1)} %copy-done.9, s32[1,16]{1,0:T(1,128)S(1)} %bitcast.26, bf16[208,256,128]{2,1,0:T(8,128)(2,1)} %bitcast.17, ...), custom_call_target="tpu_custom_call", output_to_operand_aliasing={{}: (6, {})} | custom-call | bytes 9437184 | tf_op jit(solution)/shard_map/build_rest/pallas_call | solution.py:160
  17.9 11.5 %all-to-all-start.1 = ((bf16[16,1104,128]{2,1,0:T(8,128)(2,1)}), bf16[16,1104,128]{2,1,0:T(8,128)(2,1)}, u32[]{:S(2)}, u32[]{:S(2)}) async-start(bf16[16,1104,128]{2,1,0:T(8,128)(2,1)} %build_rest.1), calls=%async_computation.1 | async-start | bytes 9043968 | tf_op jit(solution)/shard_map/all_to_all | solution.py:688
  30.0 0.9 copy-done.4
  30.9 2.1 %join_hidden.1 = bf16[44,8192]{1,0:T(8,128)(2,1)} custom-call(s32[1]{0:T(128)} %bitcast.1.here, bf16[8,44,1024]{2,1,0:T(8,128)(2,1)} %copy-done.4), custom_call_target="tpu_custom_call" | custom-call | tf_op jit(solution)/shard_map/join_hidden/pallas_call | solution.py:395
  33.0 3.3 %fusion.2 = bf16[44,2,128]{2,0,1:T(8,128)(2,1)S(1)} fusion(bf16[8192,2,128]{2,1,0:T(2,128)(2,1)} %param.13, bf16[44,8192]{1,0:T(8,128)(2,1)} %join_hidden.1), kind=kOutput, calls=%fused_computation.2 | convolution fusion | flops 184560640 | bytes 4937728 | tf_op jit(solution)/shard_map/rd,dcn->rcn/dot_general | solution.py:691
  36.4 9.4 %attend_all.1 = (bf16[22,16,128]{2,1,0:T(8,128)(2,1)S(1)}, bf16[32,32,128]{2,1,0:T(8,128)(2,1)S(1)}) custom-call(s32[1,208]{1,0:T(1,128)S(1)} %copy-done.8, s32[1,2]{1,0:T(1,128)S(1)} %copy-done.1, s32[1,20]{1,0:T(1,128)S(1)} %copy-done.2, s32[1,20]{1,0:T(1,128)S(1)} %copy-done.9, s32[1,16]{1,0:T(1,128)S(1)} %bitcast.27, ...), custom_call_target="tpu_custom_call" | custom-call | flops 218103808 | bytes 14680064 | tf_op jit(solution)/shard_map/attend_all/pallas_call | solution.py:360
  45.8 0.7 copy-done
  46.5 37.5 %all-to-all-done.1.received.block = bf16[16,1104,128]{2,1,0:T(8,128)(2,1)} async-done(((bf16[16,1104,128]{2,1,0:T(8,128)(2,1)}), bf16[16,1104,128]{2,1,0:T(8,128)(2,1)}, u32[]{:S(2)}, u32[]{:S(2)}) %all-to-all-start.1) | async-done | bytes 4522016 | tf_op jit(solution)/shard_map/all_to_all | solution.py:688
  84.0 3.3 %route_pieces.1 = bf16[16,320,128]{2,1,0:T(8,128)(2,1)} custom-call(bf16[16,1104,128]{2,1,0:T(8,128)(2,1)} %all-to-all-done.1.received.block, bf16[32,32,128]{2,1,0:T(8,128)(2,1)} %copy-done), custom_call_target="tpu_custom_call" | custom-call | bytes 2097152 | tf_op jit(solution)/shard_map/route_pieces/pallas_call | solution.py:429
  87.3 4.4 %all-to-all-start.2 = ((bf16[16,320,128]{2,1,0:T(8,128)(2,1)}), bf16[16,320,128]{2,1,0:T(8,128)(2,1)S(1)}, u32[]{:S(2)}, u32[]{:S(2)}) async-start(bf16[16,320,128]{2,1,0:T(8,128)(2,1)} %route_pieces.1), calls=%async_computation.2 | async-start | bytes 2621440 | tf_op jit(solution)/shard_map/all_to_all | solution.py:705
  91.8 0.7 reshape.66
  92.4 2.4 %decode_tables.1 = (s32[16,128]{1,0:T(8,128)S(1)}, f32[8,128]{1,0:T(8,128)}) custom-call(s32[1]{0:T(128)} %bitcast.8.here, s32[1,2]{1,0:T(1,128)} %longs.3, s32[1,20]{1,0:T(1,128)} %shorts.3, s32[1,20]{1,0:T(1,128)S(1)} %copy-done.9, bf16[16,1104,128]{2,1,0:T(8,128)(2,1)} %all-to-all-done.1.received.block), custom_call_target="tpu_custom_call" | custom-call | tf_op jit(solution)/shard_map/decode_tables/pallas_call | solution.py:478
  94.9 1.3 %fusion.6 = (f32[1,1]{1,0:T(1,128)}, f32[1,1]{1,0:T(1,128)}) fusion(f32[8,128]{1,0:T(8,128)} %get-tuple-element.82), kind=kLoop, calls=%fused_computation.13 | loop fusion | bytes 16 | tf_op jit(solution)/shard_map/slice | solution.py:710
  96.8 12.0 %place_first.1 = (bf16[32,2,512,128]{3,2,1,0:T(8,128)(2,1)}, bf16[16,2,32,128]{3,2,1,0:T(8,128)(2,1)S(1)}) custom-call(s32[16,128]{1,0:T(8,128)S(1)} %get-tuple-element.83.lens, bf16[16,1104,128]{2,1,0:T(8,128)(2,1)} %all-to-all-done.1.received.block), custom_call_target="tpu_custom_call" | custom-call | bytes 13631488 | tf_op jit(solution)/shard_map/place_first/pallas_call | solution.py:544
  108.8 3.1 %all-to-all-done.2 = bf16[16,320,128]{2,1,0:T(8,128)(2,1)S(1)} async-done(((bf16[16,320,128]{2,1,0:T(8,128)(2,1)}), bf16[16,320,128]{2,1,0:T(8,128)(2,1)S(1)}, u32[]{:S(2)}, u32[]{:S(2)}) %all-to-all-start.2) | async-done | bytes 1310752 | tf_op jit(solution)/shard_map/all_to_all | solution.py:705
  111.9 2.3 %conditional.1 = (bf16[32,2,512,128]{3,2,1,0:T(8,128)(2,1)}, bf16[32,2,1024]{2,1,0:T(2,128)(2,1)S(1)}) conditional(s32[]{:T(128)} %bitcast.9, (s32[16,128]{1,0:T(8,128)S(1)}, bf16[16,2,32,128]{3,2,1,0:T(8,128)(2,1)S(1)}, bf16[16,320,128]{2,1,0:T(8,128)(2,1)S(1)}, bf16[32,2,512,128]{3,2,1,0:T(8,128)(2,1)}) %tuple.22, (s32[1,208]{1,0:T(1,128)S(1)}, ...), branch_computations={%region_0.1_spmd, %region_1.2_spmd} | conditional | bytes 67371104 | solution.py:725
  111.9 2.1 %settle_short.1 = (bf16[32,2,512,128]{3,2,1,0:T(8,128)(2,1)}, bf16[32,16,128]{2,1,0:T(8,128)(2,1)S(1)}) custom-call(s32[16,128]{1,0:T(8,128)S(1)} %get-tuple-element.29.refs_0_, bf16[16,2,32,128]{3,2,1,0:T(8,128)(2,1)S(1)} %get-tuple-element.30.refs_1_.refs_3_, bf16[16,320,128]{2,1,0:T(8,128)(2,1)S(1)} %get-tuple-element.31.refs_2_, ...), custom_call_target="tpu_custom_call", output_to_operand_aliasing={{0}: (4, {})} | custom-call | tf_op jit(solution)/shard_map/cond/branch_0_fun/settle_short/pallas_call | solution.py:635
  114.2 0.6 copy-done.5
  (50 shorter events, 1.1 us)
Async XLA Ops:
  0.6 10.4 %collective-permute-start.1 = (bf16[22,2,1024]{2,1,0:T(2,128)(2,1)}, bf16[22,2,1024]{2,1,0:T(2,128)(2,1)S(1)}, u32[]{:S(2)}, u32[]{:S(2)}) collective-permute-start(bf16[22,2,1024]{2,1,0:T(2,128)(2,1)} %param.12), channel_id=1, source_target_pairs={{0,1},{1,0},{2,3},{3,2},{4,5},{5,4},{6,7},{7,6},{8,9},{9,8},{10,11... | collective-permute-start | bytes 270344 | tf_op jit(solution)/shard_map/ppermute | solution.py:676
  2.8 8.2 %collective-permute-start = (bf16[22,2,1024]{2,1,0:T(2,128)(2,1)}, bf16[22,2,1024]{2,1,0:T(2,128)(2,1)S(1)}, u32[]{:S(2)}, u32[]{:S(2)}) collective-permute-start(bf16[22,2,1024]{2,1,0:T(2,128)(2,1)} %param.12), channel_id=1, source_target_pairs={{0,4},{1,5},{2,6},{3,7},{4,0},{5,1},{6,2},{7,3},{8,12},{9,13},{10,... | collective-permute-start | bytes 270344 | tf_op jit(solution)/shard_map/ppermute | solution.py:673
  5.6 12.1 %collective-permute-start.3 = (bf16[22,2,1024]{2,1,0:T(2,128)(2,1)}, bf16[22,2,1024]{2,1,0:T(2,128)(2,1)S(1)}, u32[]{:S(2)}, u32[]{:S(2)}) collective-permute-start(bf16[22,2,1024]{2,1,0:T(2,128)(2,1)} %param.12), channel_id=1, source_target_pairs={{0,6},{1,7},{2,0},{3,1},{4,2},{5,3},{6,4},{7,5},{8,14},{9,15},{10,... | collective-permute-start | bytes 270344 | tf_op jit(solution)/shard_map/ppermute | solution.py:673
  6.4 11.3 %collective-permute-start.2 = (bf16[22,2,1024]{2,1,0:T(2,128)(2,1)}, bf16[22,2,1024]{2,1,0:T(2,128)(2,1)S(1)}, u32[]{:S(2)}, u32[]{:S(2)}) collective-permute-start(bf16[22,2,1024]{2,1,0:T(2,128)(2,1)} %param.12), channel_id=1, source_target_pairs={{0,2},{1,3},{2,4},{3,5},{4,6},{5,7},{6,0},{7,1},{8,10},{9,11},{10,... | collective-permute-start | bytes 270344 | tf_op jit(solution)/shard_map/ppermute | solution.py:673
  7.0 6.3 %copy-start.8 = (s32[1,208]{1,0:T(1,128)S(1)}, s32[1,208]{1,0:T(1,128)}, u32[]{:S(2)}) copy-start(s32[1,208]{1,0:T(1,128)} %table.1) | copy-start | bytes 2500
  7.1 6.3 %copy-start.9 = (s32[1,20]{1,0:T(1,128)S(1)}, s32[1,20]{1,0:T(1,128)}, u32[]{:S(2)}) copy-start(s32[1,20]{1,0:T(1,128)} %order.3) | copy-start | bytes 244
  7.1 6.3 %copy-start.10 = (s32[16,1]{0,1:T(1,128)S(1)}, s32[16,1]{0,1:T(1,128)}, u32[]{:S(2)}) copy-start(s32[16,1]{0,1:T(1,128)} %param.19) | copy-start | bytes 196
  11.0 6.7 %collective-permute-start.5 = (bf16[22,2,1024]{2,1,0:T(2,128)(2,1)S(1)}, bf16[22,2,1024]{2,1,0:T(2,128)(2,1)S(1)}, u32[]{:S(2)}, u32[]{:S(2)}) collective-permute-start(bf16[22,2,1024]{2,1,0:T(2,128)(2,1)S(1)} %collective-permute-done), channel_id=1, source_target_pairs={{0,1},{1,0},{2,3},{3,2},{4,5},{5,4},{6,7},{7,6},{8,9},{9,8},{10,11... | collective-permute-start | bytes 270344 | tf_op jit(solution)/shard_map/ppermute | solution.py:676
  11.3 6.5 %collective-permute-start.6 = (bf16[22,2,1024]{2,1,0:T(2,128)(2,1)S(1)}, bf16[22,2,1024]{2,1,0:T(2,128)(2,1)S(1)}, u32[]{:S(2)}, u32[]{:S(2)}) collective-permute-start(bf16[22,2,1024]{2,1,0:T(2,128)(2,1)S(1)} %collective-permute-done.1), channel_id=1, source_target_pairs={{0,6},{1,7},{2,0},{3,1},{4,2},{5,3},{6,4},{7,5},{8,14},{9,15},{10,... | collective-permute-start | bytes 270344 | tf_op jit(solution)/shard_map/ppermute | solution.py:673
  13.3 4.6 %collective-permute-start.4 = (bf16[22,2,1024]{2,1,0:T(2,128)(2,1)S(1)}, bf16[22,2,1024]{2,1,0:T(2,128)(2,1)S(1)}, u32[]{:S(2)}, u32[]{:S(2)}) collective-permute-start(bf16[22,2,1024]{2,1,0:T(2,128)(2,1)S(1)} %collective-permute-done.1), channel_id=1, source_target_pairs={{0,2},{1,3},{2,4},{3,5},{4,6},{5,7},{6,0},{7,1},{8,10},{9,11},{10,... | collective-permute-start | bytes 270344 | tf_op jit(solution)/shard_map/ppermute | solution.py:673
  17.7 11.7 %copy-start.6 = (bf16[22,2,1024]{2,1,0:T(2,128)(2,1)S(1)}, bf16[22,2,1024]{2,1,0:T(2,128)(2,1)}, u32[]{:S(2)}) copy-start(bf16[22,2,1024]{2,1,0:T(2,128)(2,1)} %param.12) | copy-start | bytes 270340
  17.7 11.7 %copy-start.7 = (bf16[22,2,1024]{2,1,0:T(2,128)(2,1)S(1)}, bf16[22,2,1024]{2,1,0:T(2,128)(2,1)}, u32[]{:S(2)}) copy-start(bf16[22,2,1024]{2,1,0:T(2,128)(2,1)} %param.11) | copy-start | bytes 270340
  17.9 66.1 %all-to-all-start.1 = ((bf16[16,1104,128]{2,1,0:T(8,128)(2,1)}), bf16[16,1104,128]{2,1,0:T(8,128)(2,1)}, u32[]{:S(2)}, u32[]{:S(2)}) async-start(bf16[16,1104,128]{2,1,0:T(8,128)(2,1)} %build_rest.1), calls=%async_computation.1 | async-start | bytes 9043968 | tf_op jit(solution)/shard_map/all_to_all | solution.py:688
  29.9 6.5 %copy-start.1 = (s32[1,2]{1,0:T(1,128)S(1)}, s32[1,2]{1,0:T(1,128)}, u32[]{:S(2)}) copy-start(s32[1,2]{1,0:T(1,128)} %longs.3) | copy-start | bytes 28
  29.9 6.5 %copy-start.2 = (s32[1,20]{1,0:T(1,128)S(1)}, s32[1,20]{1,0:T(1,128)}, u32[]{:S(2)}) copy-start(s32[1,20]{1,0:T(1,128)} %shorts.3) | copy-start | bytes 244
  30.0 0.9 copy-start.4
  45.8 0.7 copy-start
  87.3 24.6 %all-to-all-start.2 = ((bf16[16,320,128]{2,1,0:T(8,128)(2,1)}), bf16[16,320,128]{2,1,0:T(8,128)(2,1)S(1)}, u32[]{:S(2)}, u32[]{:S(2)}) async-start(bf16[16,320,128]{2,1,0:T(8,128)(2,1)} %route_pieces.1), calls=%async_computation.2 | async-start | bytes 2621440 | tf_op jit(solution)/shard_map/all_to_all | solution.py:705
  114.2 0.7 copy-start.5

commit v4 on v3

--- a/solution.py
+++ b/solution.py
@@ -51,132 +51,114 @@
     return slot
 
 
-def build_kernel(part, table, longs, shorts, order, dest, pool, *refs):
-    out, count, held, extra, stage, sems, extra_sems, out_sems, stage_sem = refs[part:]
-    half = MIG // 2
-    begin_at, end_at = (half, MIG) if part else (0, half)
-
-    def load(k, p):
-        page = table[0, LONG * MAXPG + order[0, k] * MIGPG + p]
+def build_kernel(
+    table, longs, shorts, order, dest, pool, out, count, slots, held, extra, stage, sems, extra_sem, out_sems, stage_sem
+):
+    def load(page, k, p):
         return pltpu.make_async_copy(
-            pool.at[page], held.at[k - begin_at, pl.ds(p * 2 * PAGE, 2 * PAGE)], sems.at[k * MIGPG + p]
+            pool.at[page], held.at[k, pl.ds(p * 2 * PAGE, 2 * PAGE)], sems.at[k]
         )
-
-    def load_extra(k, p):
-        page = table[0, LONG * MAXPG + order[0, k] * MIGPG + p]
-        return pltpu.make_async_copy(pool.at[page], extra.at[p], extra_sems.at[p])
 
     def send(k):
         return pltpu.make_async_copy(
-            held.at[k - begin_at], out.at[dest[0, k], pl.ds(0, 2 * MIGLEN)], out_sems.at[k]
+            held.at[k], out.at[dest[0, k], pl.ds(0, 2 * MIGLEN)], out_sems.at[k]
         )
 
     clear(count)
 
     def begin(k, dup_at):
         slot = take_slot(count, dest[0, k])
-
-        @pl.when((slot == 0) & (k >= begin_at))
+        slots[k] = slot
+        first = LONG * MAXPG + order[0, k] * MIGPG
+
+        @pl.when(slot == 0)
         def _():
             for p in range(MIGPG):
-                load(k, p).start()
-
-        first = (slot == 1) & (dup_at < 0)
-        if part:
-            @pl.when(first)
-            def _():
-                for p in range(MIGPG):
-                    load_extra(k, p).start()
-
-        return jnp.where(first, k, dup_at)
-
-    dup_at = lax.fori_loop(0, end_at, begin, jnp.int32(-1))
-    clear(count)
+                load(table[0, first + p], k, p).start()
+
+        second = (slot == 1) & (dup_at < 0)
+
+        @pl.when(second)
+        def _():
+            for p in range(MIGPG):
+                pltpu.make_async_copy(pool.at[table[0, first + p]], extra.at[p], extra_sem).start()
+
+        return jnp.where(second, k, dup_at)
+
+    dup_at = lax.fori_loop(0, MIG, begin, jnp.int32(-1))
     lane = lax.broadcasted_iota(jnp.int32, (16, 128), 1)
-
-    def each(k, row):
-        to = dest[0, k]
-        slot = take_slot(count, to)
+    total = jnp.int32(STEPS * REQS)
+    for i in range(LONG):
+        total = total + longs[0, i]
+    for i in range(SHORT):
+        total = total + shorts[0, i]
+    dup_to = jnp.where(dup_at >= 0, dest[0, jnp.maximum(dup_at, 0)] + 1, 0)
+    row = jnp.zeros((16, 128), jnp.int32)
+    for at, value in ((64, total & 127), (65, (total >> 7) & 127), (66, total >> 14), (67, dup_to)):
+        row = jnp.where(lane == at, value, row)
+    for k in range(MIG):
+        at = dest[0, k] * CAP + slots[k]
         length = shorts[0, order[0, k]]
-
-        @pl.when((slot == 0) & (k >= begin_at))
-        def _():
-            for p in range(MIGPG):
-                load(k, p).wait()
+        row = jnp.where(lane == at, length & 255, row)
+        row = jnp.where(lane == at + 32, length >> 8, row)
+    tables = row.astype(jnp.float32).astype(jnp.bfloat16)
+    for m in range(INST):
+        stage[m, pl.ds(2 * PIECE, 16)] = tables
+
+    def each(k, carry):
+        @pl.when(slots[k] == 0)
+        def _():
+            pltpu.make_async_copy(held.at[k], held.at[k], sems.at[k]).wait()
             send(k).start()
 
-        at = to * CAP + slot
-        row = jnp.where(lane == at, length & 255, row)
-        return jnp.where(lane == at + 32, length >> 8, row)
-
-    row = lax.fori_loop(0, end_at, each, jnp.zeros((16, 128), jnp.int32))
-    if part:
-        last = pltpu.make_async_copy(stage, out.at[:, pl.ds(A_DUP, A_ROWS - A_DUP)], stage_sem)
-        total = jnp.int32(STEPS * REQS)
-        for i in range(LONG):
-            total = total + longs[0, i]
-        for i in range(SHORT):
-            total = total + shorts[0, i]
-        row = jnp.where(lane == 64, total & 127, row)
-        row = jnp.where(lane == 65, (total >> 7) & 127, row)
-        row = jnp.where(lane == 66, total >> 14, row)
-        dup_to = jnp.where(dup_at >= 0, dest[0, jnp.maximum(dup_at, 0)] + 1, 0)
-        row = jnp.where(lane == 67, dup_to, row)
-        tables = row.astype(jnp.float32).astype(jnp.bfloat16)
-
-        @pl.when(dup_at >= 0)
-        def _():
-            for p in range(MIGPG):
-                load_extra(dup_at, p).wait()
-            for m in range(INST):
-                for c in range(2):
-                    stage[m, pl.ds(c * PIECE, PIECE)] = extra[
-                        m // MIGPG, pl.ds(c * PAGE + m % MIGPG * PIECE, PIECE)
-                    ]
-
+        return carry
+
+    lax.fori_loop(0, MIG, each, 0)
+
+    @pl.when(dup_at >= 0)
+    def _():
+        pltpu.make_async_copy(extra, extra, extra_sem).wait()
         for m in range(INST):
-            stage[m, pl.ds(2 * PIECE, 16)] = tables
-        last.start()
-    clear(count)
+            for c in range(2):
+                stage[m, pl.ds(c * PIECE, PIECE)] = extra[
+                    m // MIGPG, pl.ds(c * PAGE + m % MIGPG * PIECE, PIECE)
+                ]
+
+    last = pltpu.make_async_copy(stage, out.at[:, pl.ds(A_DUP, A_ROWS - A_DUP)], stage_sem)
+    last.start()
 
     def finish(k, carry):
-        slot = take_slot(count, dest[0, k])
-
-        @pl.when((slot == 0) & (k >= begin_at))
+        @pl.when(slots[k] == 0)
         def _():
             send(k).wait()
 
         return carry
 
-    lax.fori_loop(0, end_at, finish, 0)
-    if part:
-        last.wait()
-
-
-def build(part, tables, pool, *earlier):
-    def kernel(*refs):
-        build_kernel(part, *refs)
-
+    lax.fori_loop(0, MIG, finish, 0)
+    last.wait()
+
+
+def build(tables, pool):
     return pl.pallas_call(
-        kernel,
+        build_kernel,
         out_shape=jax.ShapeDtypeStruct((INST, A_ROWS, HD), jnp.bfloat16),
-        in_specs=[spec(SMEM)] * 5 + [spec(pl.ANY)] + [spec(pltpu.HBM)] * len(earlier),
+        in_specs=[spec(SMEM)] * 5 + [spec(pl.ANY)],
         out_specs=spec(pltpu.HBM),
         scratch_shapes=[
             pltpu.SMEM((INST,), jnp.int32),
-            pltpu.VMEM((MIG // 2, 2 * MIGLEN, HD), jnp.bfloat16),
+            pltpu.SMEM((MIG,), jnp.int32),
+            pltpu.VMEM((MIG, 2 * MIGLEN, HD), jnp.bfloat16),
             pltpu.VMEM((MIGPG, 2 * PAGE, HD), jnp.bfloat16),
             pltpu.VMEM((INST, A_ROWS - A_DUP, HD), jnp.bfloat16),
-            pltpu.SemaphoreType.DMA((MIG * MIGPG,)),
-            pltpu.SemaphoreType.DMA((MIGPG,)),
+            pltpu.SemaphoreType.DMA((MIG,)),
+            pltpu.SemaphoreType.DMA(()),
             pltpu.SemaphoreType.DMA((MIG,)),
             pltpu.SemaphoreType.DMA(()),
         ],
-        input_output_aliases={6: 0} if part else {},
         compiler_params=pltpu.CompilerParams(vmem_limit_bytes=60 << 20),
         cost_estimate=pl.CostEstimate(flops=0, bytes_accessed=9 << 20, transcendentals=0),
-        name="build_rest" if part else "build_half",
-    )(*tables, pool, *earlier)
+        name="build_first",
+    )(*tables, pool)
 
 
 def second_kernel(table, order, dest, pool, out, count, held, sems, out_sems):
@@ -244,8 +226,8 @@
 
 
 def attend_kernel(
-    table, longs, shorts, order, dest, query, keys_values, values, pool, stay, side,
-    count, place, cache, score, page_sems,
+    table, longs, shorts, order, dest, query, keys_values, values, pool, stay, out,
+    count, place, cache, score, side, page_sems, long_sems, side_sem,
 ):
     def load(pg, sem):
         return pltpu.make_async_copy(pool.at[table[0, pg]], cache.at[:, pg], sem)
@@ -261,12 +243,15 @@
             return carry
 
         lax.fori_loop(0, GROUP * MIGPG, start_short, 0)
+    per = CHUNK // PAGE
+    chunks = [(longs[0, j] + CHUNK - 1) // CHUNK for j in range(LONG)]
     for j in range(LONG):
         def start_long(i, carry, j=j):
-            load(j * MAXPG + i, page_sems.at[SHORT // GROUP + j]).start()
+            for p in range(per):
+                load(j * MAXPG + i * per + p, long_sems.at[j, i]).start()
             return carry
 
-        lax.fori_loop(0, MAXPG, start_long, 0)
+        lax.fori_loop(0, chunks[j], start_long, 0)
 
     clear(count)
     for i in range(SHORT):
@@ -320,40 +305,50 @@
             @pl.when(at >= 0)
             def _():
                 stay[LONG + r] = jnp.zeros_like(o)
-                side[at, pl.ds(0, ROWS)] = o
-                side[at, pl.ds(ROWS, 16)] = keys_values[LONG + r]
+                row = pl.multiple_of(at % CAP * 32, 32)
+                side[at // CAP, pl.ds(row, ROWS)] = o
+                side[at // CAP, pl.ds(pl.multiple_of(row + ROWS, 16), 16)] = keys_values[LONG + r]
 
         return carry
 
     lax.fori_loop(0, SHORT // GROUP, short_group, 0)
 
+    side_copy = pltpu.make_async_copy(side, out.at[:, pl.ds(0, B_DUP)], side_sem)
+    side_copy.start()
+
     for j in range(LONG):
-        wait_pages(j * MAXPG, MAXPG, page_sems.at[SHORT // GROUP + j])
         q = query[j]
         new = fresh_scores(q, j)
-        top = jnp.max(new, 1, keepdims=True)
         length = longs[0, j]
-        steps = MAXPG * PAGE // CHUNK
-        per = CHUNK // PAGE
-        for i in range(steps):
-            k = cache[0, pl.ds(j * MAXPG + i * per, per)].reshape(CHUNK, HD)
-            s = dot_nt(q, k) * SCALE
+
+        def scores(i, top, j=j, q=q, length=length):
+            first = pl.multiple_of(j * MAXPG + i * per, per)
+            wait_pages(first, per, long_sems.at[j, i])
+            s = dot_nt(q, cache[0, pl.ds(first, per)].reshape(CHUNK, HD)) * SCALE
             pos = lax.broadcasted_iota(jnp.int32, s.shape, 1) + i * CHUNK
             s = jnp.where(pos < length, s, -1e30)
             score[j, i] = s
-            top = jnp.maximum(top, jnp.max(s, 1, keepdims=True))
+            return jnp.maximum(top, jnp.max(s, 1, keepdims=True))
+
+        top = lax.fori_loop(0, chunks[j], scores, jnp.max(new, 1, keepdims=True))
         new = jnp.exp(new - top)
-        denominator = jnp.sum(new, 1, keepdims=True)
-        for i in range(steps):
+
+        def exponents(i, denominator, j=j, top=top):
             e = jnp.exp(score[j, i] - top)
             score[j, i] = e
-            denominator = denominator + jnp.sum(e, 1, keepdims=True)
+            return denominator + jnp.sum(e, 1, keepdims=True)
+
+        denominator = lax.fori_loop(0, chunks[j], exponents, jnp.sum(new, 1, keepdims=True))
         inverse = 1.0 / denominator
+
+        def blend(i, o, j=j, inverse=inverse):
+            first = pl.multiple_of(j * MAXPG + i * per, per)
+            v = cache[1, pl.ds(first, per)].reshape(CHUNK, HD)
+            return o + dot_nn((score[j, i] * inverse).astype(jnp.bfloat16), v)
+
         o = dot_nn((new * inverse).astype(jnp.bfloat16), values[j])
-        for i in range(steps):
-            v = cache[1, pl.ds(j * MAXPG + i * per, per)].reshape(CHUNK, HD)
-            o = o + dot_nn((score[j, i] * inverse).astype(jnp.bfloat16), v)
-        stay[j] = o.astype(jnp.bfloat16)
+        stay[j] = lax.fori_loop(0, chunks[j], blend, o).astype(jnp.bfloat16)
+    side_copy.wait()
 
 
 def attend(tables, query, keys_values, values, pool):
@@ -361,16 +356,19 @@
         attend_kernel,
         out_shape=(
             jax.ShapeDtypeStruct((REQS, ROWS, HD), jnp.bfloat16),
-            jax.ShapeDtypeStruct((INST * CAP, 32, HD), jnp.bfloat16),
+            jax.ShapeDtypeStruct((INST, B_ROWS, HD), jnp.bfloat16),
         ),
         in_specs=[spec(SMEM)] * 5 + [spec(VMEM)] * 3 + [spec(pl.ANY)],
-        out_specs=(spec(VMEM), spec(VMEM)),
+        out_specs=(spec(VMEM), spec(pltpu.HBM)),
         scratch_shapes=[
             pltpu.SMEM((INST,), jnp.int32),
             pltpu.SMEM((SHORT,), jnp.int32),
             pltpu.VMEM((2, PAGES, PAGE, HD), jnp.bfloat16),
             pltpu.VMEM((LONG, MAXPG * PAGE // CHUNK, ROWS, CHUNK), jnp.float32),
-            pltpu.SemaphoreType.DMA((SHORT // GROUP + LONG,)),
+            pltpu.VMEM((INST, B_DUP, HD), jnp.bfloat16),
+            pltpu.SemaphoreType.DMA((SHORT // GROUP,)),
+            pltpu.SemaphoreType.DMA((LONG, MAXPG * PAGE // CHUNK)),
+            pltpu.SemaphoreType.DMA(()),
         ],
         compiler_params=pltpu.CompilerParams(vmem_limit_bytes=24 << 20),
         cost_estimate=pl.CostEstimate(
@@ -401,44 +399,57 @@
     )(here, blocks)
 
 
-def route_kernel(received, side, out, small, count, sem):
+def route_kernel(received, _, out, small, count, slots, sem, out_sems):
     copy = pltpu.make_async_copy(received.at[:, pl.ds(A_DUP, A_ROWS - A_DUP)], small, sem)
     copy.start()
     clear(count)
-    for d in range(INST):
-        for c in range(CAP):
-            out[d, pl.ds(c * 32, 32)] = side[d * CAP + c]
     copy.wait()
     lane = lax.broadcasted_iota(jnp.int32, (16, 128), 1)
     targets = []
     for s in range(INST):
         tables = small[s, pl.ds(2 * PIECE, 16)].astype(jnp.float32)
         targets.append(jnp.max(jnp.where(lane == 67, tables, 0.0)).astype(jnp.int32) - 1)
-    for s in range(INST):
-        to = targets[s]
-        at = jnp.maximum(to, 0)
-
-        @pl.when((to >= 0) & (count[at] < DUPS))
-        def _():
-            slot = take_slot(count, at)
-            row = pl.multiple_of(B_DUP + slot * 2 * PIECE, 2 * PIECE)
-            out[at, pl.ds(row, 2 * PIECE)] = small[s, pl.ds(0, 2 * PIECE)]
-
-
-def route(received, side):
+
+    def forward(s, to, slot):
+        row = pl.multiple_of(B_DUP + slot * 2 * PIECE, 2 * PIECE)
+        return pltpu.make_async_copy(
+            small.at[s, pl.ds(0, 2 * PIECE)], out.at[to, pl.ds(row, 2 * PIECE)], out_sems.at[s]
+        )
+
+    for s, to in enumerate(targets):
+        slots[s] = DUPS
+
+        @pl.when(to >= 0)
+        def _():
+            slots[s] = take_slot(count, to)
+
+        @pl.when((to >= 0) & (slots[s] < DUPS))
+        def _():
+            forward(s, to, slots[s]).start()
+
+    for s, to in enumerate(targets):
+        @pl.when((to >= 0) & (slots[s] < DUPS))
+        def _():
+            forward(s, to, slots[s]).wait()
+
+
+def route(received, second):
     return pl.pallas_call(
         route_kernel,
         out_shape=jax.ShapeDtypeStruct((INST, B_ROWS, HD), jnp.bfloat16),
-        in_specs=[spec(pl.ANY), spec(VMEM)],
-        out_specs=spec(VMEM),
+        in_specs=[spec(pl.ANY), spec(pltpu.HBM)],
+        out_specs=spec(pltpu.HBM),
         scratch_shapes=[
             pltpu.VMEM((INST, A_ROWS - A_DUP, HD), jnp.bfloat16),
             pltpu.SMEM((INST,), jnp.int32),
+            pltpu.SMEM((INST,), jnp.int32),
             pltpu.SemaphoreType.DMA(()),
+            pltpu.SemaphoreType.DMA((INST,)),
         ],
-        cost_estimate=pl.CostEstimate(flops=0, bytes_accessed=2 << 20, transcendentals=0),
+        input_output_aliases={1: 0},
+        cost_estimate=pl.CostEstimate(flops=0, bytes_accessed=1 << 20, transcendentals=0),
         name="route_pieces",
-    )(received, side)
+    )(received, second)
 
 
 def decode_kernel(here, longs, shorts, order, received, lens, load, small, sem):
@@ -677,12 +688,8 @@
 
     near = [hidden_in, from_x(hidden_in, 1), from_x(hidden_in, 2), from_x(hidden_in, 3)]
     far = [from_y(hidden_in)]
-    half = build(0, tables, pages)
-    near[2], far[0], late_targets, half = lax.optimization_barrier(
-        (near[2], far[0], targets, half)
-    )
     far += [from_x(far[0], 1), from_y(near[2]), from_x(far[0], 3)]
-    first = build(1, (*tables[:4], late_targets), pages, half)
+    first = build(tables, pages)
     first, *blocks = lax.optimization_barrier((first, *near[1:], *far))
     blocks = jnp.stack([hidden_in, *blocks]).reshape(8, REQS * STEPS, -1)
     got_first = lax.all_to_all(first, "inst", split_axis=0, concat_axis=0, tiled=True)
@@ -697,11 +704,11 @@
         fresh.transpose(0, 2, 1, 3).reshape(REQS, 2 * STEPS, HD),
         ((0, 0), (0, 16 - 2 * STEPS), (0, 0)),
     )
-    stay, side = attend(
+    stay, second = attend(
         tables, queries.reshape(REQS, ROWS, HD), keys_values, values, kv_pool
     )
     stay_out = stay.reshape(REQS, STEPS, KV_HEADS * HD)
-    second = route(got_first, side)
+    second = route(got_first, second)
     got_second = lax.all_to_all(second, "inst", split_axis=0, concat_axis=0, tiled=True)
 
     arriving, load = decode(

time: 116 us -> 111 us (0.957)
  waiting for transfers between devices: 40.8 us -> 37.6 us
  Pallas kernels: 39.5 us -> 37.5 us
    pallas_call x2 -> x1, Pallas kernels: 8.24 us -> 5.09 us  [build(): pl.pallas_call(build_kernel, out_shape=jax.ShapeDtypeStruct((INST, A_ROWS...]
    all_to_all x1, waiting for transfers between devices: 37.5 us -> 34.5 us  [on_device(): lax.all_to_all(first, 'inst', split_axis=0, concat_axis=0, tiled=True)]
    pallas_call x1, Pallas kernels: 9.37 us -> 11.9 us  [attend(): pl.pallas_call(attend_kernel, out_shape=(jax.ShapeDtypeStruct((REQS, ROWS...]
    ppermute x5, starting transfers between devices: 6.28 us -> 8.31 us  [from_x(): lax.ppermute(value, 'tp', [(i, (i // 2 + k) % 4 * 2 + i % 2) for i in ran...]
    pallas_call x1, Pallas kernels: 3.34 us -> 1.97 us  [route(): pl.pallas_call(route_kernel, out_shape=jax.ShapeDtypeStruct((INST, B_ROWS...]
  transfers between devices with their start and end apart: 9 -> 9, of which waited for: 3 -> 2; matrix products, arithmetic and copies ran while one was open for 5% -> 5% of each run, Pallas kernels for 30% -> 30%
where the time goes in v4:
time: 111 us
  waiting for transfers between devices  37.6 us (34%)
  Pallas kernels  37.5 us (34%)
  starting transfers between devices  25 us (23%)
  local copies, waits for them, and re-layouts  5.19 us (5%)
  matrix products  3.27 us (3%)
  between operations  1.68 us (2%)
    all_to_all x1, waiting for transfers between devices, on_device(): lax.all_to_all(first, 'inst', split_axis=0, concat_axis=0, tiled=True)  34.5 us
    pallas_call x1, Pallas kernels, place_first(): pl.pallas_call(place_kernel, out_shape=(jax.ShapeDtypeStruct((INST * CAP,...  12 us
    pallas_call x1, Pallas kernels, attend(): pl.pallas_call(attend_kernel, out_shape=(jax.ShapeDtypeStruct((REQS, ROWS...  11.9 us
    all_to_all x1, starting transfers between devices, on_device(): lax.all_to_all(first, 'inst', split_axis=0, concat_axis=0, tiled=True)  10.8 us
    ppermute x5, starting transfers between devices, from_x(): lax.ppermute(value, 'tp', [(i, (i // 2 + k) % 4 * 2 + i % 2) for i in ran...  8.31 us
    pallas_call x1, Pallas kernels, build(): pl.pallas_call(build_kernel, out_shape=jax.ShapeDtypeStruct((INST, A_ROWS...  5.09 us
    all_to_all x1, starting transfers between devices, on_device(): lax.all_to_all(second, 'inst', split_axis=0, concat_axis=0, tiled=True)  4.43 us
    dot_general x1, matrix products, on_device(): jnp.einsum('rd,dcn->rcn', hidden_all, kv_weight, preferred_element_type=j...  3.27 us
  transfers between devices with their start and end apart: 9, of which 2 were waited for; matrix products, arithmetic and copies ran while one was open for 5% of the time, Pallas kernels for 30%

profile of v4, /device:TPU:1, one launch (start us, length us, event | category | flops | bytes accessed | tf_op | source)
XLA Modules:
  0.0 110.5 jit_solution(605719203587673743)
XLA Ops:
  0.6 3.7 %collective-permute-start.1 = (bf16[22,2,1024]{2,1,0:T(2,128)(2,1)}, bf16[22,2,1024]{2,1,0:T(2,128)(2,1)S(1)}, u32[]{:S(2)}, u32[]{:S(2)}) collective-permute-start(bf16[22,2,1024]{2,1,0:T(2,128)(2,1)} %param.12), channel_id=1, source_target_pairs={{0,4},{1,5},{2,6},{3,7},{4,0},{5,1},{6,2},{7,3},{8,12},{9,13},{10,... | collective-permute-start | bytes 270344 | tf_op jit(solution)/shard_map/ppermute | solution.py:684
  4.3 1.3 %collective-permute-start.3 = (bf16[22,2,1024]{2,1,0:T(2,128)(2,1)}, bf16[22,2,1024]{2,1,0:T(2,128)(2,1)S(1)}, u32[]{:S(2)}, u32[]{:S(2)}) collective-permute-start(bf16[22,2,1024]{2,1,0:T(2,128)(2,1)} %param.12), channel_id=1, source_target_pairs={{0,1},{1,0},{2,3},{3,2},{4,5},{5,4},{6,7},{7,6},{8,9},{9,8},{10,11... | collective-permute-start | bytes 270344 | tf_op jit(solution)/shard_map/ppermute | solution.py:687
  5.6 0.3 collective-permute-start
  5.9 2.4 %collective-permute-start.2 = (bf16[22,2,1024]{2,1,0:T(2,128)(2,1)}, bf16[22,2,1024]{2,1,0:T(2,128)(2,1)S(1)}, u32[]{:S(2)}, u32[]{:S(2)}) collective-permute-start(bf16[22,2,1024]{2,1,0:T(2,128)(2,1)} %param.12), channel_id=1, source_target_pairs={{0,6},{1,7},{2,0},{3,1},{4,2},{5,3},{6,4},{7,5},{8,14},{9,15},{10,... | collective-permute-start | bytes 270344 | tf_op jit(solution)/shard_map/ppermute | solution.py:684
  8.3 0.2 collective-permute-start.5
  8.4 2.0 %collective-permute-start.6 = (bf16[22,2,1024]{2,1,0:T(2,128)(2,1)S(1)}, bf16[22,2,1024]{2,1,0:T(2,128)(2,1)S(1)}, u32[]{:S(2)}, u32[]{:S(2)}) collective-permute-start(bf16[22,2,1024]{2,1,0:T(2,128)(2,1)S(1)} %collective-permute-done.3), channel_id=1, source_target_pairs={{0,6},{1,7},{2,0},{3,1},{4,2},{5,3},{6,4},{7,5},{8,14},{9,15},{10,... | collective-permute-start | bytes 270344 | tf_op jit(solution)/shard_map/ppermute | solution.py:684
  10.4 5.1 %build_first.1 = bf16[16,1104,128]{2,1,0:T(8,128)(2,1)} custom-call(s32[1,208]{1,0:T(1,128)} %table.3, s32[1,2]{1,0:T(1,128)} %longs.5, s32[1,20]{1,0:T(1,128)} %shorts.5, s32[1,20]{1,0:T(1,128)} %order.5, s32[1,16]{1,0:T(1,128)} %bitcast.24, bf16[208,256,128]{2,1,0:T(8,128)(2,1)} %bitcast.16), custom_call_target="tpu_custom_call" | custom-call | bytes 9437184 | tf_op jit(solution)/shard_map/build_first/pallas_call | solution.py:142
  15.6 10.8 %all-to-all-start.1 = ((bf16[16,1104,128]{2,1,0:T(8,128)(2,1)}), bf16[16,1104,128]{2,1,0:T(8,128)(2,1)}, u32[]{:S(2)}, u32[]{:S(2)}) async-start(bf16[16,1104,128]{2,1,0:T(8,128)(2,1)} %build_first.1), calls=%async_computation.1 | async-start | bytes 9043968 | tf_op jit(solution)/shard_map/all_to_all | solution.py:695
  27.1 0.9 copy-done.4
  27.9 2.1 %join_hidden.1 = bf16[44,8192]{1,0:T(8,128)(2,1)} custom-call(s32[1]{0:T(128)} %bitcast.1.here, bf16[8,44,1024]{2,1,0:T(8,128)(2,1)} %copy-done.4), custom_call_target="tpu_custom_call" | custom-call | tf_op jit(solution)/shard_map/join_hidden/pallas_call | solution.py:393
  30.0 3.3 %fusion.2 = bf16[44,2,128]{2,0,1:T(8,128)(2,1)S(1)} fusion(bf16[8192,2,128]{2,1,0:T(2,128)(2,1)} %param.13, bf16[44,8192]{1,0:T(8,128)(2,1)} %join_hidden.1), kind=kOutput, calls=%fused_computation.2 | convolution fusion | flops 184560640 | bytes 4937728 | tf_op jit(solution)/shard_map/rd,dcn->rcn/dot_general | solution.py:698
  33.5 11.9 %attend_all.1 = (bf16[22,16,128]{2,1,0:T(8,128)(2,1)S(1)}, bf16[16,320,128]{2,1,0:T(8,128)(2,1)S(1)}) custom-call(s32[1,208]{1,0:T(1,128)S(1)} %copy-done.8, s32[1,2]{1,0:T(1,128)S(1)} %copy-done.1, s32[1,20]{1,0:T(1,128)S(1)} %copy-done.2, s32[1,20]{1,0:T(1,128)S(1)} %copy-done.9, s32[1,16]{1,0:T(1,128)S(1)} %bitcast.25, ...), custom_call_target="tpu_custom_call" | custom-call | flops 218103808 | bytes 14680064 | tf_op jit(solution)/shard_map/attend_all/pallas_call | solution.py:355
  45.5 1.1 copy-done
  46.5 34.5 %all-to-all-done.1.received.block = bf16[16,1104,128]{2,1,0:T(8,128)(2,1)} async-done(((bf16[16,1104,128]{2,1,0:T(8,128)(2,1)}), bf16[16,1104,128]{2,1,0:T(8,128)(2,1)}, u32[]{:S(2)}, u32[]{:S(2)}) %all-to-all-start.1) | async-done | bytes 4522016 | tf_op jit(solution)/shard_map/all_to_all | solution.py:695
  81.0 2.0 %route_pieces.1 = bf16[16,320,128]{2,1,0:T(8,128)(2,1)} custom-call(bf16[16,1104,128]{2,1,0:T(8,128)(2,1)} %all-to-all-done.1.received.block, bf16[16,320,128]{2,1,0:T(8,128)(2,1)} %copy-done), custom_call_target="tpu_custom_call", output_to_operand_aliasing={{}: (1, {})} | custom-call | bytes 1048576 | tf_op jit(solution)/shard_map/route_pieces/pallas_call | solution.py:437
  83.0 4.4 %all-to-all-start.2 = ((bf16[16,320,128]{2,1,0:T(8,128)(2,1)}), bf16[16,320,128]{2,1,0:T(8,128)(2,1)S(1)}, u32[]{:S(2)}, u32[]{:S(2)}) async-start(bf16[16,320,128]{2,1,0:T(8,128)(2,1)} %route_pieces.1), calls=%async_computation.2 | async-start | bytes 2621440 | tf_op jit(solution)/shard_map/all_to_all | solution.py:712
  87.4 0.7 reshape.66
  88.1 2.4 %decode_tables.1 = (s32[16,128]{1,0:T(8,128)S(1)}, f32[8,128]{1,0:T(8,128)}) custom-call(s32[1]{0:T(128)} %bitcast.8.here, s32[1,2]{1,0:T(1,128)} %longs.5, s32[1,20]{1,0:T(1,128)} %shorts.5, s32[1,20]{1,0:T(1,128)S(1)} %copy-done.9, bf16[16,1104,128]{2,1,0:T(8,128)(2,1)} %all-to-all-done.1.received.block), custom_call_target="tpu_custom_call" | custom-call | tf_op jit(solution)/shard_map/decode_tables/pallas_call | solution.py:489
  90.5 1.3 %fusion.6 = (f32[1,1]{1,0:T(1,128)}, f32[1,1]{1,0:T(1,128)}) fusion(f32[8,128]{1,0:T(8,128)} %get-tuple-element.74), kind=kLoop, calls=%fused_computation.13 | loop fusion | bytes 16 | tf_op jit(solution)/shard_map/slice | solution.py:717
  92.4 12.0 %place_first.1 = (bf16[32,2,512,128]{3,2,1,0:T(8,128)(2,1)}, bf16[16,2,32,128]{3,2,1,0:T(8,128)(2,1)S(1)}) custom-call(s32[16,128]{1,0:T(8,128)S(1)} %get-tuple-element.75.lens, bf16[16,1104,128]{2,1,0:T(8,128)(2,1)} %all-to-all-done.1.received.block), custom_call_target="tpu_custom_call" | custom-call | bytes 13631488 | tf_op jit(solution)/shard_map/place_first/pallas_call | solution.py:555
  104.4 3.2 %all-to-all-done.2 = bf16[16,320,128]{2,1,0:T(8,128)(2,1)S(1)} async-done(((bf16[16,320,128]{2,1,0:T(8,128)(2,1)}), bf16[16,320,128]{2,1,0:T(8,128)(2,1)S(1)}, u32[]{:S(2)}, u32[]{:S(2)}) %all-to-all-start.2) | async-done | bytes 1310752 | tf_op jit(solution)/shard_map/all_to_all | solution.py:712
  107.5 2.3 %conditional.1 = (bf16[32,2,512,128]{3,2,1,0:T(8,128)(2,1)}, bf16[32,2,1024]{2,1,0:T(2,128)(2,1)S(1)}) conditional(s32[]{:T(128)} %bitcast.9, (s32[16,128]{1,0:T(8,128)S(1)}, bf16[16,2,32,128]{3,2,1,0:T(8,128)(2,1)S(1)}, bf16[16,320,128]{2,1,0:T(8,128)(2,1)S(1)}, bf16[32,2,512,128]{3,2,1,0:T(8,128)(2,1)}) %tuple.20, (s32[1,208]{1,0:T(1,128)S(1)}, ...), branch_computations={%region_0.1_spmd, %region_1.2_spmd} | conditional | bytes 67371104 | solution.py:732
  107.5 2.0 %settle_short.1 = (bf16[32,2,512,128]{3,2,1,0:T(8,128)(2,1)}, bf16[32,16,128]{2,1,0:T(8,128)(2,1)S(1)}) custom-call(s32[16,128]{1,0:T(8,128)S(1)} %get-tuple-element.29.refs_0_, bf16[16,2,32,128]{3,2,1,0:T(8,128)(2,1)S(1)} %get-tuple-element.30.refs_1_.refs_3_, bf16[16,320,128]{2,1,0:T(8,128)(2,1)S(1)} %get-tuple-element.31.refs_2_, ...), custom_call_target="tpu_custom_call", output_to_operand_aliasing={{0}: (4, {})} | custom-call | tf_op jit(solution)/shard_map/cond/branch_0_fun/settle_short/pallas_call | solution.py:646
  109.9 0.6 copy-done.5
  (49 shorter events, 0.7 us)
Async XLA Ops:
  0.6 7.6 %collective-permute-start.1 = (bf16[22,2,1024]{2,1,0:T(2,128)(2,1)}, bf16[22,2,1024]{2,1,0:T(2,128)(2,1)S(1)}, u32[]{:S(2)}, u32[]{:S(2)}) collective-permute-start(bf16[22,2,1024]{2,1,0:T(2,128)(2,1)} %param.12), channel_id=1, source_target_pairs={{0,4},{1,5},{2,6},{3,7},{4,0},{5,1},{6,2},{7,3},{8,12},{9,13},{10,... | collective-permute-start | bytes 270344 | tf_op jit(solution)/shard_map/ppermute | solution.py:684
  4.3 4.2 %collective-permute-start.3 = (bf16[22,2,1024]{2,1,0:T(2,128)(2,1)}, bf16[22,2,1024]{2,1,0:T(2,128)(2,1)S(1)}, u32[]{:S(2)}, u32[]{:S(2)}) collective-permute-start(bf16[22,2,1024]{2,1,0:T(2,128)(2,1)} %param.12), channel_id=1, source_target_pairs={{0,1},{1,0},{2,3},{3,2},{4,5},{5,4},{6,7},{7,6},{8,9},{9,8},{10,11... | collective-permute-start | bytes 270344 | tf_op jit(solution)/shard_map/ppermute | solution.py:687
  5.6 10.0 %collective-permute-start = (bf16[22,2,1024]{2,1,0:T(2,128)(2,1)}, bf16[22,2,1024]{2,1,0:T(2,128)(2,1)S(1)}, u32[]{:S(2)}, u32[]{:S(2)}) collective-permute-start(bf16[22,2,1024]{2,1,0:T(2,128)(2,1)} %param.12), channel_id=1, source_target_pairs={{0,2},{1,3},{2,4},{3,5},{4,6},{5,7},{6,0},{7,1},{8,10},{9,11},{10,... | collective-permute-start | bytes 270344 | tf_op jit(solution)/shard_map/ppermute | solution.py:684
  5.9 9.7 %collective-permute-start.2 = (bf16[22,2,1024]{2,1,0:T(2,128)(2,1)}, bf16[22,2,1024]{2,1,0:T(2,128)(2,1)S(1)}, u32[]{:S(2)}, u32[]{:S(2)}) collective-permute-start(bf16[22,2,1024]{2,1,0:T(2,128)(2,1)} %param.12), channel_id=1, source_target_pairs={{0,6},{1,7},{2,0},{3,1},{4,2},{5,3},{6,4},{7,5},{8,14},{9,15},{10,... | collective-permute-start | bytes 270344 | tf_op jit(solution)/shard_map/ppermute | solution.py:684
  8.3 7.3 %collective-permute-start.5 = (bf16[22,2,1024]{2,1,0:T(2,128)(2,1)S(1)}, bf16[22,2,1024]{2,1,0:T(2,128)(2,1)S(1)}, u32[]{:S(2)}, u32[]{:S(2)}) collective-permute-start(bf16[22,2,1024]{2,1,0:T(2,128)(2,1)S(1)} %collective-permute-done.1), channel_id=1, source_target_pairs={{0,1},{1,0},{2,3},{3,2},{4,5},{5,4},{6,7},{7,6},{8,9},{9,8},{10,11... | collective-permute-start | bytes 270344 | tf_op jit(solution)/shard_map/ppermute | solution.py:687
  8.4 7.1 %collective-permute-start.6 = (bf16[22,2,1024]{2,1,0:T(2,128)(2,1)S(1)}, bf16[22,2,1024]{2,1,0:T(2,128)(2,1)S(1)}, u32[]{:S(2)}, u32[]{:S(2)}) collective-permute-start(bf16[22,2,1024]{2,1,0:T(2,128)(2,1)S(1)} %collective-permute-done.3), channel_id=1, source_target_pairs={{0,6},{1,7},{2,0},{3,1},{4,2},{5,3},{6,4},{7,5},{8,14},{9,15},{10,... | collective-permute-start | bytes 270344 | tf_op jit(solution)/shard_map/ppermute | solution.py:684
  10.4 5.2 %collective-permute-start.4 = (bf16[22,2,1024]{2,1,0:T(2,128)(2,1)S(1)}, bf16[22,2,1024]{2,1,0:T(2,128)(2,1)S(1)}, u32[]{:S(2)}, u32[]{:S(2)}) collective-permute-start(bf16[22,2,1024]{2,1,0:T(2,128)(2,1)S(1)} %collective-permute-done.3), channel_id=1, source_target_pairs={{0,2},{1,3},{2,4},{3,5},{4,6},{5,7},{6,0},{7,1},{8,10},{9,11},{10,... | collective-permute-start | bytes 270344 | tf_op jit(solution)/shard_map/ppermute | solution.py:684
  15.5 10.9 %copy-start.6 = (bf16[22,2,1024]{2,1,0:T(2,128)(2,1)S(1)}, bf16[22,2,1024]{2,1,0:T(2,128)(2,1)}, u32[]{:S(2)}) copy-start(bf16[22,2,1024]{2,1,0:T(2,128)(2,1)} %param.12) | copy-start | bytes 270340
  15.5 10.9 %copy-start.7 = (bf16[22,2,1024]{2,1,0:T(2,128)(2,1)S(1)}, bf16[22,2,1024]{2,1,0:T(2,128)(2,1)}, u32[]{:S(2)}) copy-start(bf16[22,2,1024]{2,1,0:T(2,128)(2,1)} %param.11) | copy-start | bytes 270340
  15.6 65.4 %all-to-all-start.1 = ((bf16[16,1104,128]{2,1,0:T(8,128)(2,1)}), bf16[16,1104,128]{2,1,0:T(8,128)(2,1)}, u32[]{:S(2)}, u32[]{:S(2)}) async-start(bf16[16,1104,128]{2,1,0:T(8,128)(2,1)} %build_first.1), calls=%async_computation.1 | async-start | bytes 9043968 | tf_op jit(solution)/shard_map/all_to_all | solution.py:695
  26.9 6.6 %copy-start.1 = (s32[1,2]{1,0:T(1,128)S(1)}, s32[1,2]{1,0:T(1,128)}, u32[]{:S(2)}) copy-start(s32[1,2]{1,0:T(1,128)} %longs.5) | copy-start | bytes 28
  26.9 6.6 %copy-start.2 = (s32[1,20]{1,0:T(1,128)S(1)}, s32[1,20]{1,0:T(1,128)}, u32[]{:S(2)}) copy-start(s32[1,20]{1,0:T(1,128)} %shorts.5) | copy-start | bytes 244
  26.9 6.6 %copy-start.8 = (s32[1,208]{1,0:T(1,128)S(1)}, s32[1,208]{1,0:T(1,128)}, u32[]{:S(2)}) copy-start(s32[1,208]{1,0:T(1,128)} %table.3) | copy-start | bytes 2500
  26.9 6.6 %copy-start.9 = (s32[1,20]{1,0:T(1,128)S(1)}, s32[1,20]{1,0:T(1,128)}, u32[]{:S(2)}) copy-start(s32[1,20]{1,0:T(1,128)} %order.5) | copy-start | bytes 244
  27.0 6.5 %copy-start.10 = (s32[16,1]{0,1:T(1,128)S(1)}, s32[16,1]{0,1:T(1,128)}, u32[]{:S(2)}) copy-start(s32[16,1]{0,1:T(1,128)} %param.19) | copy-start | bytes 196
  27.1 0.9 copy-start.4
  45.5 1.1 copy-start
  83.0 24.6 %all-to-all-start.2 = ((bf16[16,320,128]{2,1,0:T(8,128)(2,1)}), bf16[16,320,128]{2,1,0:T(8,128)(2,1)S(1)}, u32[]{:S(2)}, u32[]{:S(2)}) async-start(bf16[16,320,128]{2,1,0:T(8,128)(2,1)} %route_pieces.1), calls=%async_computation.2 | async-start | bytes 2621440 | tf_op jit(solution)/shard_map/all_to_all | solution.py:712
  109.9 0.7 copy-start.5

commit v5 on v4

--- a/solution.py
+++ b/solution.py
@@ -382,8 +382,8 @@
     me = here[0]
     width = blocks.shape[2]
     for k in range(8):
-        x = (me // 2 + 4 - k % 4) % 4
-        y = (me + k // 4) % 2
+        x = (me // 2 + 4 - k // 2) % 4
+        y = (me + k % 2) % 2
         at = pl.multiple_of((x * 2 + y) * width, width)
         out[:, pl.ds(at, width)] = blocks[k]
 
@@ -686,12 +686,12 @@
     def from_y(value):
         return lax.ppermute(value, "tp", [(i, i ^ 1) for i in range(8)])
 
-    near = [hidden_in, from_x(hidden_in, 1), from_x(hidden_in, 2), from_x(hidden_in, 3)]
-    far = [from_y(hidden_in)]
-    far += [from_x(far[0], 1), from_y(near[2]), from_x(far[0], 3)]
+    mate = from_y(hidden_in)
     first = build(tables, pages)
-    first, *blocks = lax.optimization_barrier((first, *near[1:], *far))
-    blocks = jnp.stack([hidden_in, *blocks]).reshape(8, REQS * STEPS, -1)
+    first, mate = lax.optimization_barrier((first, mate))
+    pair = jnp.stack([hidden_in, mate])
+    blocks = jnp.stack([pair, *[from_x(pair, k) for k in range(1, 4)]])
+    blocks = blocks.reshape(8, REQS * STEPS, -1)
     got_first = lax.all_to_all(first, "inst", split_axis=0, concat_axis=0, tiled=True)
 
     hidden_all = join(tp_index.reshape(1), blocks)

time: 111 us -> 102 us (0.919)
  waiting for transfers between devices: 37.6 us -> 27.9 us
  starting transfers between devices: 25 us -> 20.9 us
  Pallas kernels: 37.5 us -> 40.1 us
  other arithmetic: 0 us -> 1.83 us
    all_to_all x1, waiting for transfers between devices: 34.5 us -> 18.5 us  [on_device(): lax.all_to_all(first, 'inst', split_axis=0, concat_axis=0, tiled=True)]
    ppermute x5 -> x3, waiting for transfers between devices: 0.01 us -> 6.2 us  [from_x(): lax.ppermute(value, 'tp', [(i, (i // 2 + k) % 4 * 2 + i % 2) for i in ran...]
    ppermute x5 -> x3, starting transfers between devices: 8.31 us -> 5.5 us  [from_x(): lax.ppermute(value, 'tp', [(i, (i // 2 + k) % 4 * 2 + i % 2) for i in ran...]
    pallas_call x1, Pallas kernels: 11.9 us -> 14.5 us  [attend(): pl.pallas_call(attend_kernel, out_shape=(jax.ShapeDtypeStruct((REQS, ROWS...]
    all_to_all x1, starting transfers between devices: 10.8 us -> 8.76 us  [on_device(): lax.all_to_all(first, 'inst', split_axis=0, concat_axis=0, tiled=True)]
    another operation x0 -> x3, other arithmetic: none -> 1.83 us  [the longest x2 1.58 us: on_device(): blocks = jnp.stack([pair, *[from_x(pair, k) for k in range(1, 4)]])]
    reshape x0 -> x1, local copies, waits for them, and re-layouts: none -> 1.2 us  [on_device(): blocks = blocks.reshape(8, REQS * STEPS, -1)]
    unnamed x28 -> x19, local copies, waits for them, and re-layouts: 2.73 us -> 1.78 us
  transfers between devices with their start and end apart: 9 -> 6, of which waited for: 2 -> 4; matrix products, arithmetic and copies ran while one was open for 5% -> 8% of each run, Pallas kernels for 30% -> 36%
where the time goes in v5:
time: 102 us; the launch traced here: 101 us
  Pallas kernels  40.1 us (39%)
  waiting for transfers between devices  27.9 us (27%)
  starting transfers between devices  20.9 us (20%)
  local copies, waits for them, and re-layouts  5.12 us (5%)
  matrix products  3.27 us (3%)
  other arithmetic  1.83 us (2%)
  between operations  1.54 us (2%)
    all_to_all x1, waiting for transfers between devices, on_device(): lax.all_to_all(first, 'inst', split_axis=0, concat_axis=0, tiled=True)  18.5 us
    pallas_call x1, Pallas kernels, attend(): pl.pallas_call(attend_kernel, out_shape=(jax.ShapeDtypeStruct((REQS, ROWS...  14.5 us
    pallas_call x1, Pallas kernels, place_first(): pl.pallas_call(place_kernel, out_shape=(jax.ShapeDtypeStruct((INST * CAP,...  11.9 us
    all_to_all x1, starting transfers between devices, on_device(): lax.all_to_all(first, 'inst', split_axis=0, concat_axis=0, tiled=True)  8.76 us
    ppermute x3, waiting for transfers between devices, from_x(): lax.ppermute(value, 'tp', [(i, (i // 2 + k) % 4 * 2 + i % 2) for i in ran...  6.2 us
    ppermute x3, starting transfers between devices, from_x(): lax.ppermute(value, 'tp', [(i, (i // 2 + k) % 4 * 2 + i % 2) for i in ran...  5.5 us
    pallas_call x1, Pallas kernels, build(): pl.pallas_call(build_kernel, out_shape=jax.ShapeDtypeStruct((INST, A_ROWS...  5.09 us
    all_to_all x1, starting transfers between devices, on_device(): lax.all_to_all(second, 'inst', split_axis=0, concat_axis=0, tiled=True)  4.43 us
  transfers between devices with their start and end apart: 6, of which 4 were waited for; matrix products, arithmetic and copies ran while one was open for 8% of the time, Pallas kernels for 36%

profile of v5, /device:TPU:1, one launch (start us, length us, event | category | flops | bytes accessed | tf_op | source)
XLA Modules:
  0.0 100.9 jit_solution(14971717032764415701)
XLA Ops:
  0.6 2.2 %collective-permute-start = (bf16[22,2,1024]{2,1,0:T(2,128)(2,1)}, bf16[22,2,1024]{2,1,0:T(2,128)(2,1)S(1)}, u32[]{:S(2)}, u32[]{:S(2)}) collective-permute-start(bf16[22,2,1024]{2,1,0:T(2,128)(2,1)} %param.12), channel_id=1, source_target_pairs={{0,1},{1,0},{2,3},{3,2},{4,5},{5,4},{6,7},{7,6},{8,9},{9,8},{10,11... | collective-permute-start | bytes 270344 | tf_op jit(solution)/shard_map/ppermute | solution.py:687
  2.8 5.1 %build_first.1 = bf16[16,1104,128]{2,1,0:T(8,128)(2,1)} custom-call(s32[1,208]{1,0:T(1,128)} %table.3, s32[1,2]{1,0:T(1,128)} %longs.5, s32[1,20]{1,0:T(1,128)} %shorts.5, s32[1,20]{1,0:T(1,128)} %order.5, s32[1,16]{1,0:T(1,128)} %bitcast.38, bf16[208,256,128]{2,1,0:T(8,128)(2,1)} %bitcast.23), custom_call_target="tpu_custom_call" | custom-call | bytes 9437184 | tf_op jit(solution)/shard_map/build_first/pallas_call | solution.py:142
  8.0 8.8 %all-to-all-start.1 = ((bf16[16,1104,128]{2,1,0:T(8,128)(2,1)}), bf16[16,1104,128]{2,1,0:T(8,128)(2,1)}, u32[]{:S(2)}, u32[]{:S(2)}) async-start(bf16[16,1104,128]{2,1,0:T(8,128)(2,1)} %build_first.1), calls=%async_computation.1 | async-start | bytes 9043968 | tf_op jit(solution)/shard_map/all_to_all | solution.py:695
  17.0 2.8 %collective-permute-start.2 = (bf16[2,22,2,1024]{3,2,1,0:T(2,128)(2,1)S(1)}, bf16[2,22,2,1024]{3,2,1,0:T(2,128)(2,1)S(1)}, u32[]{:S(2)}, u32[]{:S(2)}) collective-permute-start(bf16[2,22,2,1024]{3,2,1,0:T(2,128)(2,1)S(1)} %pad_maximum_fusion.1), channel_id=1, source_target_pairs={{0,4},{1,5},{2,6},{3,7},{4,0},{5,1},{6,2},{7,3},{8,12},{9,13},{10,... | collective-permute-start | bytes 540680 | tf_op jit(solution)/shard_map/ppermute | solution.py:684
  20.1 2.4 %collective-permute-start.3 = (bf16[2,22,2,1024]{3,2,1,0:T(2,128)(2,1)S(1)}, bf16[2,22,2,1024]{3,2,1,0:T(2,128)(2,1)S(1)}, u32[]{:S(2)}, u32[]{:S(2)}) collective-permute-start(bf16[2,22,2,1024]{3,2,1,0:T(2,128)(2,1)S(1)} %pad_maximum_fusion.1), channel_id=1, source_target_pairs={{0,6},{1,7},{2,0},{3,1},{4,2},{5,3},{6,4},{7,5},{8,14},{9,15},{10,... | collective-permute-start | bytes 540680 | tf_op jit(solution)/shard_map/ppermute | solution.py:684
  22.8 1.9 %collective-permute-done.2 = bf16[2,22,2,1024]{3,2,1,0:T(2,128)(2,1)S(1)} collective-permute-done((bf16[2,22,2,1024]{3,2,1,0:T(2,128)(2,1)S(1)}, bf16[2,22,2,1024]{3,2,1,0:T(2,128)(2,1)S(1)}, u32[]{:S(2)}, u32[]{:S(2)}) %collective-permute-start.2) | collective-permute-done | bytes 180256 | tf_op jit(solution)/shard_map/ppermute | solution.py:684
  24.7 4.3 %collective-permute-done.1 = bf16[2,22,2,1024]{3,2,1,0:T(2,128)(2,1)S(1)} collective-permute-done((bf16[2,22,2,1024]{3,2,1,0:T(2,128)(2,1)S(1)}, bf16[2,22,2,1024]{3,2,1,0:T(2,128)(2,1)S(1)}, u32[]{:S(2)}, u32[]{:S(2)}) %collective-permute-start.1) | collective-permute-done | bytes 180256 | tf_op jit(solution)/shard_map/ppermute | solution.py:684
  29.0 1.3 %pad_maximum_fusion = bf16[4,2,22,2,1024]{4,3,2,1,0:T(2,128)(2,1)S(1)} fusion(bf16[1,2,22,2,1024]{4,3,2,1,0:T(2,128)(2,1)S(1)} %bitcast.35, bf16[1,2,22,2,1024]{4,3,2,1,0:T(2,128)(2,1)S(1)} %bitcast.33, bf16[1,2,22,2,1024]{4,3,2,1,0:T(2,128)(2,1)S(1)} %bitcast.34, bf16[1,2,22,2,1024]{4,3,2,1,0:T(2,128)(2,1)S(1)} %fusion.7), kind=kLoop, calls=%fused_computation.4 | loop fusion | flops 1081344 | bytes 1441792 | tf_op jit(solution)/shard_map/stack | solution.py:693
  30.4 1.2 %reshape.57.blocks = bf16[8,44,1024]{2,1,0:T(8,128)(2,1)} reshape(bf16[4,2,22,2,1024]{4,3,2,1,0:T(2,128)(2,1)S(1)} %pad_maximum_fusion) | data formatting | bytes 1441792 | tf_op jit(solution)/shard_map/reshape | solution.py:694
  31.6 2.1 %join_hidden.1 = bf16[44,8192]{1,0:T(8,128)(2,1)} custom-call(s32[1]{0:T(128)} %bitcast.1.here, bf16[8,44,1024]{2,1,0:T(8,128)(2,1)} %reshape.57.blocks), custom_call_target="tpu_custom_call" | custom-call | tf_op jit(solution)/shard_map/join_hidden/pallas_call | solution.py:393
  33.7 3.3 %fusion.2 = bf16[44,2,128]{2,0,1:T(8,128)(2,1)S(1)} fusion(bf16[8192,2,128]{2,1,0:T(2,128)(2,1)} %param.13, bf16[44,8192]{1,0:T(8,128)(2,1)} %join_hidden.1), kind=kOutput, calls=%fused_computation.2 | convolution fusion | flops 184560640 | bytes 4937728 | tf_op jit(solution)/shard_map/rd,dcn->rcn/dot_general | solution.py:698
  37.2 14.5 %attend_all.1 = (bf16[22,16,128]{2,1,0:T(8,128)(2,1)S(1)}, bf16[16,320,128]{2,1,0:T(8,128)(2,1)S(1)}) custom-call(s32[1,208]{1,0:T(1,128)S(1)} %copy-done.7, s32[1,2]{1,0:T(1,128)S(1)} %copy-done.1, s32[1,20]{1,0:T(1,128)S(1)} %copy-done.2, s32[1,20]{1,0:T(1,128)S(1)} %copy-done.8, s32[1,16]{1,0:T(1,128)S(1)} %bitcast.39, ...), custom_call_target="tpu_custom_call" | custom-call | flops 218103808 | bytes 14680064 | tf_op jit(solution)/shard_map/attend_all/pallas_call | solution.py:355
  51.8 1.1 %copy-done = bf16[16,320,128]{2,1,0:T(8,128)(2,1)} copy-done((bf16[16,320,128]{2,1,0:T(8,128)(2,1)}, bf16[16,320,128]{2,1,0:T(8,128)(2,1)S(1)}, u32[]{:S(2)}) %copy-start) | copy-done | bytes 1310744
  52.8 18.5 %all-to-all-done.1.received.block = bf16[16,1104,128]{2,1,0:T(8,128)(2,1)} async-done(((bf16[16,1104,128]{2,1,0:T(8,128)(2,1)}), bf16[16,1104,128]{2,1,0:T(8,128)(2,1)}, u32[]{:S(2)}, u32[]{:S(2)}) %all-to-all-start.1) | async-done | bytes 4522016 | tf_op jit(solution)/shard_map/all_to_all | solution.py:695
  71.3 2.0 %route_pieces.1 = bf16[16,320,128]{2,1,0:T(8,128)(2,1)} custom-call(bf16[16,1104,128]{2,1,0:T(8,128)(2,1)} %all-to-all-done.1.received.block, bf16[16,320,128]{2,1,0:T(8,128)(2,1)} %copy-done), custom_call_target="tpu_custom_call", output_to_operand_aliasing={{}: (1, {})} | custom-call | bytes 1048576 | tf_op jit(solution)/shard_map/route_pieces/pallas_call | solution.py:437
  73.3 4.4 %all-to-all-start.2 = ((bf16[16,320,128]{2,1,0:T(8,128)(2,1)}), bf16[16,320,128]{2,1,0:T(8,128)(2,1)S(1)}, u32[]{:S(2)}, u32[]{:S(2)}) async-start(bf16[16,320,128]{2,1,0:T(8,128)(2,1)} %route_pieces.1), calls=%async_computation.2 | async-start | bytes 2621440 | tf_op jit(solution)/shard_map/all_to_all | solution.py:712
  77.8 0.7 reshape.53
  78.4 2.4 %decode_tables.1 = (s32[16,128]{1,0:T(8,128)S(1)}, f32[8,128]{1,0:T(8,128)}) custom-call(s32[1]{0:T(128)} %bitcast.14.here, s32[1,2]{1,0:T(1,128)} %longs.5, s32[1,20]{1,0:T(1,128)} %shorts.5, s32[1,20]{1,0:T(1,128)S(1)} %copy-done.8, bf16[16,1104,128]{2,1,0:T(8,128)(2,1)} %all-to-all-done.1.received.block), custom_call_target="tpu_custom_call" | custom-call | tf_op jit(solution)/shard_map/decode_tables/pallas_call | solution.py:489
  80.8 1.3 %fusion.6 = (f32[1,1]{1,0:T(1,128)}, f32[1,1]{1,0:T(1,128)}) fusion(f32[8,128]{1,0:T(8,128)} %get-tuple-element.62), kind=kLoop, calls=%fused_computation.7 | loop fusion | bytes 16 | tf_op jit(solution)/shard_map/slice | solution.py:717
  82.8 11.9 %place_first.1 = (bf16[32,2,512,128]{3,2,1,0:T(8,128)(2,1)}, bf16[16,2,32,128]{3,2,1,0:T(8,128)(2,1)S(1)}) custom-call(s32[16,128]{1,0:T(8,128)S(1)} %get-tuple-element.63.lens, bf16[16,1104,128]{2,1,0:T(8,128)(2,1)} %all-to-all-done.1.received.block), custom_call_target="tpu_custom_call" | custom-call | bytes 13631488 | tf_op jit(solution)/shard_map/place_first/pallas_call | solution.py:555
  94.7 3.2 %all-to-all-done.2 = bf16[16,320,128]{2,1,0:T(8,128)(2,1)S(1)} async-done(((bf16[16,320,128]{2,1,0:T(8,128)(2,1)}), bf16[16,320,128]{2,1,0:T(8,128)(2,1)S(1)}, u32[]{:S(2)}, u32[]{:S(2)}) %all-to-all-start.2) | async-done | bytes 1310752 | tf_op jit(solution)/shard_map/all_to_all | solution.py:712
  97.9 2.3 %conditional.1 = (bf16[32,2,512,128]{3,2,1,0:T(8,128)(2,1)}, bf16[32,2,1024]{2,1,0:T(2,128)(2,1)S(1)}) conditional(s32[]{:T(128)} %bitcast.15, (s32[16,128]{1,0:T(8,128)S(1)}, bf16[16,2,32,128]{3,2,1,0:T(8,128)(2,1)S(1)}, bf16[16,320,128]{2,1,0:T(8,128)(2,1)S(1)}, bf16[32,2,512,128]{3,2,1,0:T(8,128)(2,1)}) %tuple.20, (s32[1,208]{1,0:T(1,128)S(1)}, ...), branch_computations={%region_0.1_spmd, %region_1.2_spmd} | conditional | bytes 67371104 | solution.py:732
  97.9 2.1 %settle_short.1 = (bf16[32,2,512,128]{3,2,1,0:T(8,128)(2,1)}, bf16[32,16,128]{2,1,0:T(8,128)(2,1)S(1)}) custom-call(s32[16,128]{1,0:T(8,128)S(1)} %get-tuple-element.29.refs_0_, bf16[16,2,32,128]{3,2,1,0:T(8,128)(2,1)S(1)} %get-tuple-element.30.refs_1_.refs_3_, bf16[16,320,128]{2,1,0:T(8,128)(2,1)S(1)} %get-tuple-element.31.refs_2_, ...), custom_call_target="tpu_custom_call", output_to_operand_aliasing={{0}: (4, {})} | custom-call | tf_op jit(solution)/shard_map/cond/branch_0_fun/settle_short/pallas_call | solution.py:646
  100.2 0.6 copy-done.5
  (29 shorter events, 1.1 us)
Async XLA Ops:
  0.6 7.3 %collective-permute-start = (bf16[22,2,1024]{2,1,0:T(2,128)(2,1)}, bf16[22,2,1024]{2,1,0:T(2,128)(2,1)S(1)}, u32[]{:S(2)}, u32[]{:S(2)}) collective-permute-start(bf16[22,2,1024]{2,1,0:T(2,128)(2,1)} %param.12), channel_id=1, source_target_pairs={{0,1},{1,0},{2,3},{3,2},{4,5},{5,4},{6,7},{7,6},{8,9},{9,8},{10,11... | collective-permute-start | bytes 270344 | tf_op jit(solution)/shard_map/ppermute | solution.py:687
  7.9 8.8 %copy-start.4 = (bf16[22,2,1024]{2,1,0:T(2,128)(2,1)S(1)}, bf16[22,2,1024]{2,1,0:T(2,128)(2,1)}, u32[]{:S(2)}) copy-start(bf16[22,2,1024]{2,1,0:T(2,128)(2,1)} %param.12) | copy-start | bytes 270340
  7.9 14.6 %copy-start.6 = (bf16[22,2,1024]{2,1,0:T(2,128)(2,1)S(1)}, bf16[22,2,1024]{2,1,0:T(2,128)(2,1)}, u32[]{:S(2)}) copy-start(bf16[22,2,1024]{2,1,0:T(2,128)(2,1)} %param.11) | copy-start | bytes 270340
  8.0 63.4 %all-to-all-start.1 = ((bf16[16,1104,128]{2,1,0:T(8,128)(2,1)}), bf16[16,1104,128]{2,1,0:T(8,128)(2,1)}, u32[]{:S(2)}, u32[]{:S(2)}) async-start(bf16[16,1104,128]{2,1,0:T(8,128)(2,1)} %build_first.1), calls=%async_computation.1 | async-start | bytes 9043968 | tf_op jit(solution)/shard_map/all_to_all | solution.py:695
  17.0 7.7 %collective-permute-start.2 = (bf16[2,22,2,1024]{3,2,1,0:T(2,128)(2,1)S(1)}, bf16[2,22,2,1024]{3,2,1,0:T(2,128)(2,1)S(1)}, u32[]{:S(2)}, u32[]{:S(2)}) collective-permute-start(bf16[2,22,2,1024]{3,2,1,0:T(2,128)(2,1)S(1)} %pad_maximum_fusion.1), channel_id=1, source_target_pairs={{0,4},{1,5},{2,6},{3,7},{4,0},{5,1},{6,2},{7,3},{8,12},{9,13},{10,... | collective-permute-start | bytes 540680 | tf_op jit(solution)/shard_map/ppermute | solution.py:684
  19.8 9.2 %collective-permute-start.1 = (bf16[2,22,2,1024]{3,2,1,0:T(2,128)(2,1)S(1)}, bf16[2,22,2,1024]{3,2,1,0:T(2,128)(2,1)S(1)}, u32[]{:S(2)}, u32[]{:S(2)}) collective-permute-start(bf16[2,22,2,1024]{3,2,1,0:T(2,128)(2,1)S(1)} %pad_maximum_fusion.1), channel_id=1, source_target_pairs={{0,2},{1,3},{2,4},{3,5},{4,6},{5,7},{6,0},{7,1},{8,10},{9,11},{10,... | collective-permute-start | bytes 540680 | tf_op jit(solution)/shard_map/ppermute | solution.py:684
  20.1 8.9 %collective-permute-start.3 = (bf16[2,22,2,1024]{3,2,1,0:T(2,128)(2,1)S(1)}, bf16[2,22,2,1024]{3,2,1,0:T(2,128)(2,1)S(1)}, u32[]{:S(2)}, u32[]{:S(2)}) collective-permute-start(bf16[2,22,2,1024]{3,2,1,0:T(2,128)(2,1)S(1)} %pad_maximum_fusion.1), channel_id=1, source_target_pairs={{0,6},{1,7},{2,0},{3,1},{4,2},{5,3},{6,4},{7,5},{8,14},{9,15},{10,... | collective-permute-start | bytes 540680 | tf_op jit(solution)/shard_map/ppermute | solution.py:684
  30.4 6.8 %copy-start.1 = (s32[1,2]{1,0:T(1,128)S(1)}, s32[1,2]{1,0:T(1,128)}, u32[]{:S(2)}) copy-start(s32[1,2]{1,0:T(1,128)} %longs.5) | copy-start | bytes 28
  30.4 6.8 %copy-start.2 = (s32[1,20]{1,0:T(1,128)S(1)}, s32[1,20]{1,0:T(1,128)}, u32[]{:S(2)}) copy-start(s32[1,20]{1,0:T(1,128)} %shorts.5) | copy-start | bytes 244
  30.4 6.8 %copy-start.7 = (s32[1,208]{1,0:T(1,128)S(1)}, s32[1,208]{1,0:T(1,128)}, u32[]{:S(2)}) copy-start(s32[1,208]{1,0:T(1,128)} %table.3) | copy-start | bytes 2500
  30.4 6.8 %copy-start.8 = (s32[1,20]{1,0:T(1,128)S(1)}, s32[1,20]{1,0:T(1,128)}, u32[]{:S(2)}) copy-start(s32[1,20]{1,0:T(1,128)} %order.5) | copy-start | bytes 244
  30.4 6.8 %copy-start.9 = (s32[16,1]{0,1:T(1,128)S(1)}, s32[16,1]{0,1:T(1,128)}, u32[]{:S(2)}) copy-start(s32[16,1]{0,1:T(1,128)} %param.19) | copy-start | bytes 196
  51.7 1.1 %copy-start = (bf16[16,320,128]{2,1,0:T(8,128)(2,1)}, bf16[16,320,128]{2,1,0:T(8,128)(2,1)S(1)}, u32[]{:S(2)}) copy-start(bf16[16,320,128]{2,1,0:T(8,128)(2,1)S(1)} %get-tuple-element.65._) | copy-start | bytes 3932164
  73.3 24.6 %all-to-all-start.2 = ((bf16[16,320,128]{2,1,0:T(8,128)(2,1)}), bf16[16,320,128]{2,1,0:T(8,128)(2,1)S(1)}, u32[]{:S(2)}, u32[]{:S(2)}) async-start(bf16[16,320,128]{2,1,0:T(8,128)(2,1)} %route_pieces.1), calls=%async_computation.2 | async-start | bytes 2621440 | tf_op jit(solution)/shard_map/all_to_all | solution.py:712
  100.2 0.7 copy-start.5

commit v6 on v5

--- a/solution.py
+++ b/solution.py
@@ -29,7 +29,8 @@
 A_DUP = 2 * MIGLEN
 A_META = A_DUP + 2 * PIECE
 A_ROWS = A_META + 16
-B_DUP = 64
+B_FRESH = CAP * 16
+B_DUP = B_FRESH + 16
 B_ROWS = B_DUP + DUPS * 2 * PIECE
 
 SMEM = pltpu.SMEM
@@ -85,7 +86,21 @@
 
         return jnp.where(second, k, dup_at)
 
-    dup_at = lax.fori_loop(0, MIG, begin, jnp.int32(-1))
+    dup_at = jnp.int32(-1)
+    for k in range(MIG):
+        dup_at = begin(k, dup_at)
+
+    def each(k, carry):
+        @pl.when(slots[k] == 0)
+        def _():
+            pltpu.make_async_copy(held.at[k], held.at[k], sems.at[k]).wait()
+            send(k).start()
+
+        return carry
+
+    for k in range(MIG):
+        each(k, 0)
+
     lane = lax.broadcasted_iota(jnp.int32, (16, 128), 1)
     total = jnp.int32(STEPS * REQS)
     for i in range(LONG):
@@ -104,16 +119,6 @@
     tables = row.astype(jnp.float32).astype(jnp.bfloat16)
     for m in range(INST):
         stage[m, pl.ds(2 * PIECE, 16)] = tables
-
-    def each(k, carry):
-        @pl.when(slots[k] == 0)
-        def _():
-            pltpu.make_async_copy(held.at[k], held.at[k], sems.at[k]).wait()
-            send(k).start()
-
-        return carry
-
-    lax.fori_loop(0, MIG, each, 0)
 
     @pl.when(dup_at >= 0)
     def _():
@@ -227,7 +232,7 @@
 
 def attend_kernel(
     table, longs, shorts, order, dest, query, keys_values, values, pool, stay, out,
-    count, place, cache, score, side, page_sems, long_sems, side_sem,
+    count, place, cache, score, side, rows, page_sems, long_sems, side_sem,
 ):
     def load(pg, sem):
         return pltpu.make_async_copy(pool.at[table[0, pg]], cache.at[:, pg], sem)
@@ -305,14 +310,16 @@
             @pl.when(at >= 0)
             def _():
                 stay[LONG + r] = jnp.zeros_like(o)
-                row = pl.multiple_of(at % CAP * 32, 32)
-                side[at // CAP, pl.ds(row, ROWS)] = o
-                side[at // CAP, pl.ds(pl.multiple_of(row + ROWS, 16), 16)] = keys_values[LONG + r]
+                side[at // CAP, pl.ds(pl.multiple_of(at % CAP * ROWS, ROWS), ROWS)] = o
+                rows[at // CAP, pl.ds(pl.multiple_of(at % CAP * 8, 8), 8)] = keys_values[
+                    LONG + r
+                ].astype(jnp.float32)[:8]
 
         return carry
 
     lax.fori_loop(0, SHORT // GROUP, short_group, 0)
 
+    side[:, pl.ds(B_FRESH, 16)] = rows[...].astype(jnp.bfloat16)
     side_copy = pltpu.make_async_copy(side, out.at[:, pl.ds(0, B_DUP)], side_sem)
     side_copy.start()
 
@@ -366,6 +373,7 @@
             pltpu.VMEM((2, PAGES, PAGE, HD), jnp.bfloat16),
             pltpu.VMEM((LONG, MAXPG * PAGE // CHUNK, ROWS, CHUNK), jnp.float32),
             pltpu.VMEM((INST, B_DUP, HD), jnp.bfloat16),
+            pltpu.VMEM((INST, 16, HD), jnp.float32),
             pltpu.SemaphoreType.DMA((SHORT // GROUP,)),
             pltpu.SemaphoreType.DMA((LONG, MAXPG * PAGE // CHUNK)),
             pltpu.SemaphoreType.DMA(()),
@@ -411,7 +419,7 @@
         targets.append(jnp.max(jnp.where(lane == 67, tables, 0.0)).astype(jnp.int32) - 1)
 
     def forward(s, to, slot):
-        row = pl.multiple_of(B_DUP + slot * 2 * PIECE, 2 * PIECE)
+        row = pl.multiple_of(B_DUP + slot * 2 * PIECE, 16)
         return pltpu.make_async_copy(
             small.at[s, pl.ds(0, 2 * PIECE)], out.at[to, pl.ds(row, 2 * PIECE)], out_sems.at[s]
         )
@@ -527,7 +535,7 @@
         for c in range(2):
             x = jnp.where(at < length, read(p, c).astype(jnp.float32), 0.0)
             if fresh is not None:
-                rows = fresh().astype(jnp.float32)
+                rows = fresh()
                 for t in range(STEPS):
                     x = jnp.where(at == length + t, rows[c * 2 + t:c * 2 + t + 1], x)
             write(p, c, x.astype(jnp.bfloat16))
@@ -591,7 +599,7 @@
 
         @pl.when(length > 0)
         def _():
-            fresh = second[s, pl.ds(ROWS, 16)].astype(jnp.float32)
+            fresh = second[s, pl.ds(B_FRESH, 16)].astype(jnp.float32)[:8]
             where = at + window_base(length)
             for c in range(2):
                 x = window[s, c].astype(jnp.float32)
@@ -611,7 +619,7 @@
             def read(p, c):
                 if full:
                     return extra[s, pl.ds((p * 2 + c) * PAGE, PAGE)]
-                row = pl.multiple_of(B_DUP + rank * 2 * PIECE + c * PIECE, PIECE)
+                row = pl.multiple_of(B_DUP + rank * 2 * PIECE + c * PIECE, 16)
                 return jnp.concatenate(
                     [second[p * MIGPG + i, pl.ds(row, PIECE)] for i in range(MIGPG)], axis=0
                 )
@@ -620,13 +628,13 @@
                 dups[s, c, pl.ds(p * PAGE, PAGE)] = x
 
             for p in range(MIGPG):
-                masked_page(read, write, length, lambda: second[s, pl.ds(32 + ROWS, 16)], p)
+                masked_page(read, write, length, lambda: second[s, pl.ds(B_FRESH, 16)].astype(jnp.float32)[8:], p)
             dup_copy(s).start()
 
     for s in range(INST):
         for slot in range(CAP):
             filled = lens[s, slot] > 0
-            rows = second[s, pl.ds(slot * 32, ROWS)]
+            rows = second[s, pl.ds(slot * ROWS, ROWS)]
             out[s * CAP + slot] = jnp.where(filled, rows, jnp.zeros_like(rows))
     for s in range(INST):
         @pl.when(lens[s, 0] > 0)

time: 102 us -> 101 us (level)
  Pallas kernels: 40.1 us -> 37 us
  waiting for transfers between devices: 27.9 us -> 30.3 us
    all_to_all x1, waiting for transfers between devices: 18.5 us -> 21.6 us  [on_device(): lax.all_to_all(first, 'inst', split_axis=0, concat_axis=0, tiled=True)]
    pallas_call x1, Pallas kernels: 14.5 us -> 11.4 us  [attend(): pl.pallas_call(attend_kernel, out_shape=(jax.ShapeDtypeStruct((REQS, ROWS...]
  transfers between devices with their start and end apart: 6 -> 6, of which waited for: 4 -> 4; matrix products, arithmetic and copies ran while one was open for 8% -> 8% of each run, Pallas kernels for 36% -> 33%
where the time goes in v6:
time: 101 us; the launch traced here: 100 us
  Pallas kernels  37 us (37%)
  waiting for transfers between devices  30.3 us (30%)
  starting transfers between devices  20.9 us (21%)
  local copies, waits for them, and re-layouts  5.1 us (5%)
  matrix products  3.27 us (3%)
  other arithmetic  1.83 us (2%)
  between operations  1.54 us (2%)
    all_to_all x1, waiting for transfers between devices, on_device(): lax.all_to_all(first, 'inst', split_axis=0, concat_axis=0, tiled=True)  21.6 us
    pallas_call x1, Pallas kernels, place_first(): pl.pallas_call(place_kernel, out_shape=(jax.ShapeDtypeStruct((INST * CAP,...  11.9 us
    pallas_call x1, Pallas kernels, attend(): pl.pallas_call(attend_kernel, out_shape=(jax.ShapeDtypeStruct((REQS, ROWS...  11.4 us
    all_to_all x1, starting transfers between devices, on_device(): lax.all_to_all(first, 'inst', split_axis=0, concat_axis=0, tiled=True)  8.76 us
    ppermute x3, waiting for transfers between devices, from_x(): lax.ppermute(value, 'tp', [(i, (i // 2 + k) % 4 * 2 + i % 2) for i in ran...  6.2 us
    ppermute x3, starting transfers between devices, from_x(): lax.ppermute(value, 'tp', [(i, (i // 2 + k) % 4 * 2 + i % 2) for i in ran...  5.5 us
    pallas_call x1, Pallas kernels, build(): pl.pallas_call(build_kernel, out_shape=jax.ShapeDtypeStruct((INST, A_ROWS...  5.06 us
    all_to_all x1, starting transfers between devices, on_device(): lax.all_to_all(second, 'inst', split_axis=0, concat_axis=0, tiled=True)  4.43 us
  transfers between devices with their start and end apart: 6, of which 4 were waited for; matrix products, arithmetic and copies ran while one was open for 8% of the time, Pallas kernels for 33%

profile of v6, /device:TPU:1, one launch (start us, length us, event | category | flops | bytes accessed | tf_op | source)
XLA Modules:
  0.0 100.1 jit_solution(18053513534522099237)
XLA Ops:
  0.6 2.2 %collective-permute-start = (bf16[22,2,1024]{2,1,0:T(2,128)(2,1)}, bf16[22,2,1024]{2,1,0:T(2,128)(2,1)S(1)}, u32[]{:S(2)}, u32[]{:S(2)}) collective-permute-start(bf16[22,2,1024]{2,1,0:T(2,128)(2,1)} %param.12), channel_id=1, source_target_pairs={{0,1},{1,0},{2,3},{3,2},{4,5},{5,4},{6,7},{7,6},{8,9},{9,8},{10,11... | collective-permute-start | bytes 270344 | tf_op jit(solution)/shard_map/ppermute | solution.py:695
  2.8 5.1 %build_first.1 = bf16[16,1104,128]{2,1,0:T(8,128)(2,1)} custom-call(s32[1,208]{1,0:T(1,128)} %table.3, s32[1,2]{1,0:T(1,128)} %longs.5, s32[1,20]{1,0:T(1,128)} %shorts.5, s32[1,20]{1,0:T(1,128)} %order.5, s32[1,16]{1,0:T(1,128)} %bitcast.38, bf16[208,256,128]{2,1,0:T(8,128)(2,1)} %bitcast.23), custom_call_target="tpu_custom_call" | custom-call | bytes 9437184 | tf_op jit(solution)/shard_map/build_first/pallas_call | solution.py:147
  7.9 8.8 %all-to-all-start.1 = ((bf16[16,1104,128]{2,1,0:T(8,128)(2,1)}), bf16[16,1104,128]{2,1,0:T(8,128)(2,1)}, u32[]{:S(2)}, u32[]{:S(2)}) async-start(bf16[16,1104,128]{2,1,0:T(8,128)(2,1)} %build_first.1), calls=%async_computation.1 | async-start | bytes 9043968 | tf_op jit(solution)/shard_map/all_to_all | solution.py:703
  17.0 2.8 %collective-permute-start.2 = (bf16[2,22,2,1024]{3,2,1,0:T(2,128)(2,1)S(1)}, bf16[2,22,2,1024]{3,2,1,0:T(2,128)(2,1)S(1)}, u32[]{:S(2)}, u32[]{:S(2)}) collective-permute-start(bf16[2,22,2,1024]{3,2,1,0:T(2,128)(2,1)S(1)} %pad_maximum_fusion.1), channel_id=1, source_target_pairs={{0,4},{1,5},{2,6},{3,7},{4,0},{5,1},{6,2},{7,3},{8,12},{9,13},{10,... | collective-permute-start | bytes 540680 | tf_op jit(solution)/shard_map/ppermute | solution.py:692
  20.1 2.4 %collective-permute-start.3 = (bf16[2,22,2,1024]{3,2,1,0:T(2,128)(2,1)S(1)}, bf16[2,22,2,1024]{3,2,1,0:T(2,128)(2,1)S(1)}, u32[]{:S(2)}, u32[]{:S(2)}) collective-permute-start(bf16[2,22,2,1024]{3,2,1,0:T(2,128)(2,1)S(1)} %pad_maximum_fusion.1), channel_id=1, source_target_pairs={{0,6},{1,7},{2,0},{3,1},{4,2},{5,3},{6,4},{7,5},{8,14},{9,15},{10,... | collective-permute-start | bytes 540680 | tf_op jit(solution)/shard_map/ppermute | solution.py:692
  22.8 1.9 %collective-permute-done.2 = bf16[2,22,2,1024]{3,2,1,0:T(2,128)(2,1)S(1)} collective-permute-done((bf16[2,22,2,1024]{3,2,1,0:T(2,128)(2,1)S(1)}, bf16[2,22,2,1024]{3,2,1,0:T(2,128)(2,1)S(1)}, u32[]{:S(2)}, u32[]{:S(2)}) %collective-permute-start.2) | collective-permute-done | bytes 180256 | tf_op jit(solution)/shard_map/ppermute | solution.py:692
  24.7 4.3 %collective-permute-done.1 = bf16[2,22,2,1024]{3,2,1,0:T(2,128)(2,1)S(1)} collective-permute-done((bf16[2,22,2,1024]{3,2,1,0:T(2,128)(2,1)S(1)}, bf16[2,22,2,1024]{3,2,1,0:T(2,128)(2,1)S(1)}, u32[]{:S(2)}, u32[]{:S(2)}) %collective-permute-start.1) | collective-permute-done | bytes 180256 | tf_op jit(solution)/shard_map/ppermute | solution.py:692
  29.0 1.3 %pad_maximum_fusion = bf16[4,2,22,2,1024]{4,3,2,1,0:T(2,128)(2,1)S(1)} fusion(bf16[1,2,22,2,1024]{4,3,2,1,0:T(2,128)(2,1)S(1)} %bitcast.35, bf16[1,2,22,2,1024]{4,3,2,1,0:T(2,128)(2,1)S(1)} %bitcast.33, bf16[1,2,22,2,1024]{4,3,2,1,0:T(2,128)(2,1)S(1)} %bitcast.34, bf16[1,2,22,2,1024]{4,3,2,1,0:T(2,128)(2,1)S(1)} %fusion.7), kind=kLoop, calls=%fused_computation.4 | loop fusion | flops 1081344 | bytes 1441792 | tf_op jit(solution)/shard_map/stack | solution.py:701
  30.4 1.2 %reshape.57.blocks = bf16[8,44,1024]{2,1,0:T(8,128)(2,1)} reshape(bf16[4,2,22,2,1024]{4,3,2,1,0:T(2,128)(2,1)S(1)} %pad_maximum_fusion) | data formatting | bytes 1441792 | tf_op jit(solution)/shard_map/reshape | solution.py:702
  31.6 2.1 %join_hidden.1 = bf16[44,8192]{1,0:T(8,128)(2,1)} custom-call(s32[1]{0:T(128)} %bitcast.1.here, bf16[8,44,1024]{2,1,0:T(8,128)(2,1)} %reshape.57.blocks), custom_call_target="tpu_custom_call" | custom-call | tf_op jit(solution)/shard_map/join_hidden/pallas_call | solution.py:401
  33.7 3.3 %fusion.2 = bf16[44,2,128]{2,0,1:T(8,128)(2,1)S(1)} fusion(bf16[8192,2,128]{2,1,0:T(2,128)(2,1)} %param.13, bf16[44,8192]{1,0:T(8,128)(2,1)} %join_hidden.1), kind=kOutput, calls=%fused_computation.2 | convolution fusion | flops 184560640 | bytes 4937728 | tf_op jit(solution)/shard_map/rd,dcn->rcn/dot_general | solution.py:706
  37.2 11.4 %attend_all.1 = (bf16[22,16,128]{2,1,0:T(8,128)(2,1)S(1)}, bf16[16,304,128]{2,1,0:T(8,128)(2,1)S(1)}) custom-call(s32[1,208]{1,0:T(1,128)S(1)} %copy-done.7, s32[1,2]{1,0:T(1,128)S(1)} %copy-done.1, s32[1,20]{1,0:T(1,128)S(1)} %copy-done.2, s32[1,20]{1,0:T(1,128)S(1)} %copy-done.8, s32[1,16]{1,0:T(1,128)S(1)} %bitcast.39, ...), custom_call_target="tpu_custom_call" | custom-call | flops 218103808 | bytes 14680064 | tf_op jit(solution)/shard_map/attend_all/pallas_call | solution.py:362
  48.6 1.1 %copy-done = bf16[16,304,128]{2,1,0:T(8,128)(2,1)} copy-done((bf16[16,304,128]{2,1,0:T(8,128)(2,1)}, bf16[16,304,128]{2,1,0:T(8,128)(2,1)S(1)}, u32[]{:S(2)}) %copy-start) | copy-done | bytes 1245208
  49.7 21.6 %all-to-all-done.1.received.block = bf16[16,1104,128]{2,1,0:T(8,128)(2,1)} async-done(((bf16[16,1104,128]{2,1,0:T(8,128)(2,1)}), bf16[16,1104,128]{2,1,0:T(8,128)(2,1)}, u32[]{:S(2)}, u32[]{:S(2)}) %all-to-all-start.1) | async-done | bytes 4522016 | tf_op jit(solution)/shard_map/all_to_all | solution.py:703
  71.3 1.9 %route_pieces.1 = bf16[16,304,128]{2,1,0:T(8,128)(2,1)} custom-call(bf16[16,1104,128]{2,1,0:T(8,128)(2,1)} %all-to-all-done.1.received.block, bf16[16,304,128]{2,1,0:T(8,128)(2,1)} %copy-done), custom_call_target="tpu_custom_call", output_to_operand_aliasing={{}: (1, {})} | custom-call | bytes 1048576 | tf_op jit(solution)/shard_map/route_pieces/pallas_call | solution.py:445
  73.3 4.4 %all-to-all-start.2 = ((bf16[16,304,128]{2,1,0:T(8,128)(2,1)}), bf16[16,304,128]{2,1,0:T(8,128)(2,1)S(1)}, u32[]{:S(2)}, u32[]{:S(2)}) async-start(bf16[16,304,128]{2,1,0:T(8,128)(2,1)} %route_pieces.1), calls=%async_computation.2 | async-start | bytes 2490368 | tf_op jit(solution)/shard_map/all_to_all | solution.py:720
  77.7 0.7 reshape.53
  78.4 2.4 %decode_tables.1 = (s32[16,128]{1,0:T(8,128)S(1)}, f32[8,128]{1,0:T(8,128)}) custom-call(s32[1]{0:T(128)} %bitcast.14.here, s32[1,2]{1,0:T(1,128)} %longs.5, s32[1,20]{1,0:T(1,128)} %shorts.5, s32[1,20]{1,0:T(1,128)S(1)} %copy-done.8, bf16[16,1104,128]{2,1,0:T(8,128)(2,1)} %all-to-all-done.1.received.block), custom_call_target="tpu_custom_call" | custom-call | tf_op jit(solution)/shard_map/decode_tables/pallas_call | solution.py:497
  80.8 1.3 %fusion.6 = (f32[1,1]{1,0:T(1,128)}, f32[1,1]{1,0:T(1,128)}) fusion(f32[8,128]{1,0:T(8,128)} %get-tuple-element.62), kind=kLoop, calls=%fused_computation.7 | loop fusion | bytes 16 | tf_op jit(solution)/shard_map/slice | solution.py:725
  82.7 11.9 %place_first.1 = (bf16[32,2,512,128]{3,2,1,0:T(8,128)(2,1)}, bf16[16,2,32,128]{3,2,1,0:T(8,128)(2,1)S(1)}) custom-call(s32[16,128]{1,0:T(8,128)S(1)} %get-tuple-element.63.lens, bf16[16,1104,128]{2,1,0:T(8,128)(2,1)} %all-to-all-done.1.received.block), custom_call_target="tpu_custom_call" | custom-call | bytes 13631488 | tf_op jit(solution)/shard_map/place_first/pallas_call | solution.py:563
  94.7 2.5 %all-to-all-done.2 = bf16[16,304,128]{2,1,0:T(8,128)(2,1)S(1)} async-done(((bf16[16,304,128]{2,1,0:T(8,128)(2,1)}), bf16[16,304,128]{2,1,0:T(8,128)(2,1)S(1)}, u32[]{:S(2)}, u32[]{:S(2)}) %all-to-all-start.2) | async-done | bytes 1245216 | tf_op jit(solution)/shard_map/all_to_all | solution.py:720
  97.1 2.3 %conditional.1 = (bf16[32,2,512,128]{3,2,1,0:T(8,128)(2,1)}, bf16[32,2,1024]{2,1,0:T(2,128)(2,1)S(1)}) conditional(s32[]{:T(128)} %bitcast.15, (s32[16,128]{1,0:T(8,128)S(1)}, bf16[16,2,32,128]{3,2,1,0:T(8,128)(2,1)S(1)}, bf16[16,304,128]{2,1,0:T(8,128)(2,1)S(1)}, bf16[32,2,512,128]{3,2,1,0:T(8,128)(2,1)}) %tuple.20, (s32[1,208]{1,0:T(1,128)S(1)}, ...), branch_computations={%region_0.1_spmd, %region_1.2_spmd} | conditional | bytes 67371104 | solution.py:740
  97.1 2.0 %settle_short.1 = (bf16[32,2,512,128]{3,2,1,0:T(8,128)(2,1)}, bf16[32,16,128]{2,1,0:T(8,128)(2,1)S(1)}) custom-call(s32[16,128]{1,0:T(8,128)S(1)} %get-tuple-element.29.refs_0_, bf16[16,2,32,128]{3,2,1,0:T(8,128)(2,1)S(1)} %get-tuple-element.30.refs_1_.refs_3_, bf16[16,304,128]{2,1,0:T(8,128)(2,1)S(1)} %get-tuple-element.31.refs_2_, ...), custom_call_target="tpu_custom_call", output_to_operand_aliasing={{0}: (4, {})} | custom-call | tf_op jit(solution)/shard_map/cond/branch_0_fun/settle_short/pallas_call | solution.py:654
  99.5 0.6 copy-done.5
  (29 shorter events, 1.1 us)
Async XLA Ops:
  0.6 7.3 %collective-permute-start = (bf16[22,2,1024]{2,1,0:T(2,128)(2,1)}, bf16[22,2,1024]{2,1,0:T(2,128)(2,1)S(1)}, u32[]{:S(2)}, u32[]{:S(2)}) collective-permute-start(bf16[22,2,1024]{2,1,0:T(2,128)(2,1)} %param.12), channel_id=1, source_target_pairs={{0,1},{1,0},{2,3},{3,2},{4,5},{5,4},{6,7},{7,6},{8,9},{9,8},{10,11... | collective-permute-start | bytes 270344 | tf_op jit(solution)/shard_map/ppermute | solution.py:695
  7.9 8.8 %copy-start.4 = (bf16[22,2,1024]{2,1,0:T(2,128)(2,1)S(1)}, bf16[22,2,1024]{2,1,0:T(2,128)(2,1)}, u32[]{:S(2)}) copy-start(bf16[22,2,1024]{2,1,0:T(2,128)(2,1)} %param.12) | copy-start | bytes 270340
  7.9 14.6 %copy-start.6 = (bf16[22,2,1024]{2,1,0:T(2,128)(2,1)S(1)}, bf16[22,2,1024]{2,1,0:T(2,128)(2,1)}, u32[]{:S(2)}) copy-start(bf16[22,2,1024]{2,1,0:T(2,128)(2,1)} %param.11) | copy-start | bytes 270340
  7.9 63.4 %all-to-all-start.1 = ((bf16[16,1104,128]{2,1,0:T(8,128)(2,1)}), bf16[16,1104,128]{2,1,0:T(8,128)(2,1)}, u32[]{:S(2)}, u32[]{:S(2)}) async-start(bf16[16,1104,128]{2,1,0:T(8,128)(2,1)} %build_first.1), calls=%async_computation.1 | async-start | bytes 9043968 | tf_op jit(solution)/shard_map/all_to_all | solution.py:703
  17.0 7.7 %collective-permute-start.2 = (bf16[2,22,2,1024]{3,2,1,0:T(2,128)(2,1)S(1)}, bf16[2,22,2,1024]{3,2,1,0:T(2,128)(2,1)S(1)}, u32[]{:S(2)}, u32[]{:S(2)}) collective-permute-start(bf16[2,22,2,1024]{3,2,1,0:T(2,128)(2,1)S(1)} %pad_maximum_fusion.1), channel_id=1, source_target_pairs={{0,4},{1,5},{2,6},{3,7},{4,0},{5,1},{6,2},{7,3},{8,12},{9,13},{10,... | collective-permute-start | bytes 540680 | tf_op jit(solution)/shard_map/ppermute | solution.py:692
  19.8 9.2 %collective-permute-start.1 = (bf16[2,22,2,1024]{3,2,1,0:T(2,128)(2,1)S(1)}, bf16[2,22,2,1024]{3,2,1,0:T(2,128)(2,1)S(1)}, u32[]{:S(2)}, u32[]{:S(2)}) collective-permute-start(bf16[2,22,2,1024]{3,2,1,0:T(2,128)(2,1)S(1)} %pad_maximum_fusion.1), channel_id=1, source_target_pairs={{0,2},{1,3},{2,4},{3,5},{4,6},{5,7},{6,0},{7,1},{8,10},{9,11},{10,... | collective-permute-start | bytes 540680 | tf_op jit(solution)/shard_map/ppermute | solution.py:692
  20.1 8.9 %collective-permute-start.3 = (bf16[2,22,2,1024]{3,2,1,0:T(2,128)(2,1)S(1)}, bf16[2,22,2,1024]{3,2,1,0:T(2,128)(2,1)S(1)}, u32[]{:S(2)}, u32[]{:S(2)}) collective-permute-start(bf16[2,22,2,1024]{3,2,1,0:T(2,128)(2,1)S(1)} %pad_maximum_fusion.1), channel_id=1, source_target_pairs={{0,6},{1,7},{2,0},{3,1},{4,2},{5,3},{6,4},{7,5},{8,14},{9,15},{10,... | collective-permute-start | bytes 540680 | tf_op jit(solution)/shard_map/ppermute | solution.py:692
  30.3 6.8 %copy-start.1 = (s32[1,2]{1,0:T(1,128)S(1)}, s32[1,2]{1,0:T(1,128)}, u32[]{:S(2)}) copy-start(s32[1,2]{1,0:T(1,128)} %longs.5) | copy-start | bytes 28
  30.4 6.8 %copy-start.2 = (s32[1,20]{1,0:T(1,128)S(1)}, s32[1,20]{1,0:T(1,128)}, u32[]{:S(2)}) copy-start(s32[1,20]{1,0:T(1,128)} %shorts.5) | copy-start | bytes 244
  30.4 6.8 %copy-start.7 = (s32[1,208]{1,0:T(1,128)S(1)}, s32[1,208]{1,0:T(1,128)}, u32[]{:S(2)}) copy-start(s32[1,208]{1,0:T(1,128)} %table.3) | copy-start | bytes 2500
  30.4 6.8 %copy-start.8 = (s32[1,20]{1,0:T(1,128)S(1)}, s32[1,20]{1,0:T(1,128)}, u32[]{:S(2)}) copy-start(s32[1,20]{1,0:T(1,128)} %order.5) | copy-start | bytes 244
  30.4 6.8 %copy-start.9 = (s32[16,1]{0,1:T(1,128)S(1)}, s32[16,1]{0,1:T(1,128)}, u32[]{:S(2)}) copy-start(s32[16,1]{0,1:T(1,128)} %param.19) | copy-start | bytes 196
  48.6 1.1 %copy-start = (bf16[16,304,128]{2,1,0:T(8,128)(2,1)}, bf16[16,304,128]{2,1,0:T(8,128)(2,1)S(1)}, u32[]{:S(2)}) copy-start(bf16[16,304,128]{2,1,0:T(8,128)(2,1)S(1)} %get-tuple-element.65._) | copy-start | bytes 3735556
  73.3 23.9 %all-to-all-start.2 = ((bf16[16,304,128]{2,1,0:T(8,128)(2,1)}), bf16[16,304,128]{2,1,0:T(8,128)(2,1)S(1)}, u32[]{:S(2)}, u32[]{:S(2)}) async-start(bf16[16,304,128]{2,1,0:T(8,128)(2,1)} %route_pieces.1), calls=%async_computation.2 | async-start | bytes 2490368 | tf_op jit(solution)/shard_map/all_to_all | solution.py:720
  99.4 0.7 copy-start.5

commit v7 on v6

--- a/solution.py
+++ b/solution.py
@@ -407,21 +407,24 @@
     )(here, blocks)
 
 
-def route_kernel(received, _, out, small, count, slots, sem, out_sems):
-    copy = pltpu.make_async_copy(received.at[:, pl.ds(A_DUP, A_ROWS - A_DUP)], small, sem)
-    copy.start()
+def route_kernel(received, _, out, tables, small, count, slots, sem, small_sem, out_sems):
+    first = pltpu.make_async_copy(received.at[:, pl.ds(A_META, 16)], tables, sem)
+    rest = pltpu.make_async_copy(received.at[:, pl.ds(A_DUP, 2 * PIECE)], small, small_sem)
+    first.start()
+    rest.start()
     clear(count)
-    copy.wait()
+    first.wait()
     lane = lax.broadcasted_iota(jnp.int32, (16, 128), 1)
     targets = []
     for s in range(INST):
-        tables = small[s, pl.ds(2 * PIECE, 16)].astype(jnp.float32)
-        targets.append(jnp.max(jnp.where(lane == 67, tables, 0.0)).astype(jnp.int32) - 1)
+        found = jnp.where(lane == 67, tables[s].astype(jnp.float32), 0.0)
+        targets.append(jnp.max(found).astype(jnp.int32) - 1)
+    rest.wait()
 
     def forward(s, to, slot):
         row = pl.multiple_of(B_DUP + slot * 2 * PIECE, 16)
         return pltpu.make_async_copy(
-            small.at[s, pl.ds(0, 2 * PIECE)], out.at[to, pl.ds(row, 2 * PIECE)], out_sems.at[s]
+            small.at[s], out.at[to, pl.ds(row, 2 * PIECE)], out_sems.at[s]
         )
 
     for s, to in enumerate(targets):
@@ -448,9 +451,11 @@
         in_specs=[spec(pl.ANY), spec(pltpu.HBM)],
         out_specs=spec(pltpu.HBM),
         scratch_shapes=[
-            pltpu.VMEM((INST, A_ROWS - A_DUP, HD), jnp.bfloat16),
+            pltpu.VMEM((INST, 16, HD), jnp.bfloat16),
+            pltpu.VMEM((INST, 2 * PIECE, HD), jnp.bfloat16),
             pltpu.SMEM((INST,), jnp.int32),
             pltpu.SMEM((INST,), jnp.int32),
+            pltpu.SemaphoreType.DMA(()),
             pltpu.SemaphoreType.DMA(()),
             pltpu.SemaphoreType.DMA((INST,)),
         ],
@@ -740,6 +745,7 @@
     moved_cache, moved = lax.cond(
         overflow, long_path, short_path, (arriving, window, got_second, cache)
     )
+    moved = lax.optimization_barrier(moved)
     moved_out = moved.reshape(INST * CAP, STEPS, KV_HEADS * HD)
     return (stay_out, moved_out, moved_cache, load_share)
 

time: 101 us -> 101 us (level)
  Pallas kernels: 37 us -> 34.8 us
  waiting for transfers between devices: 30.3 us -> 32.4 us
    all_to_all x1, waiting for transfers between devices: 21.6 us -> 23.7 us  [on_device(): lax.all_to_all(first, 'inst', split_axis=0, concat_axis=0, tiled=True)]
    pallas_call x1, Pallas kernels: 11.4 us -> 9.37 us  [attend(): pl.pallas_call(attend_kernel, out_shape=(jax.ShapeDtypeStruct((REQS, ROWS...]
  transfers between devices with their start and end apart: 6 -> 6, of which waited for: 4 -> 4; matrix products, arithmetic and copies ran while one was open for 8% -> 8% of each run, Pallas kernels for 33% -> 31%
where the time goes in v7:
time: 101 us; the launch traced here: 100 us
  Pallas kernels  34.8 us (34%)
  waiting for transfers between devices  32.4 us (32%)
  starting transfers between devices  20.9 us (21%)
  local copies, waits for them, and re-layouts  5.09 us (5%)
  matrix products  3.27 us (3%)
  other arithmetic  1.83 us (2%)
  between operations  1.53 us (2%)
    all_to_all x1, waiting for transfers between devices, on_device(): lax.all_to_all(first, 'inst', split_axis=0, concat_axis=0, tiled=True)  23.7 us
    pallas_call x1, Pallas kernels, place_first(): pl.pallas_call(place_kernel, out_shape=(jax.ShapeDtypeStruct((INST * CAP,...  11.9 us
    pallas_call x1, Pallas kernels, attend(): pl.pallas_call(attend_kernel, out_shape=(jax.ShapeDtypeStruct((REQS, ROWS...  9.37 us
    all_to_all x1, starting transfers between devices, on_device(): lax.all_to_all(first, 'inst', split_axis=0, concat_axis=0, tiled=True)  8.76 us
    ppermute x3, waiting for transfers between devices, from_x(): lax.ppermute(value, 'tp', [(i, (i // 2 + k) % 4 * 2 + i % 2) for i in ran...  6.2 us
    ppermute x3, starting transfers between devices, from_x(): lax.ppermute(value, 'tp', [(i, (i // 2 + k) % 4 * 2 + i % 2) for i in ran...  5.5 us
    pallas_call x1, Pallas kernels, build(): pl.pallas_call(build_kernel, out_shape=jax.ShapeDtypeStruct((INST, A_ROWS...  5.06 us
    all_to_all x1, starting transfers between devices, on_device(): lax.all_to_all(second, 'inst', split_axis=0, concat_axis=0, tiled=True)  4.43 us
  transfers between devices with their start and end apart: 6, of which 4 were waited for; matrix products, arithmetic and copies ran while one was open for 8% of the time, Pallas kernels for 31%

profile of v7, /device:TPU:1, one launch (start us, length us, event | category | flops | bytes accessed | tf_op | source)
XLA Modules:
  0.0 100.1 jit_solution(2162687974194731)
XLA Ops:
  0.6 2.2 %collective-permute-start = (bf16[22,2,1024]{2,1,0:T(2,128)(2,1)}, bf16[22,2,1024]{2,1,0:T(2,128)(2,1)S(1)}, u32[]{:S(2)}, u32[]{:S(2)}) collective-permute-start(bf16[22,2,1024]{2,1,0:T(2,128)(2,1)} %param.12), channel_id=1, source_target_pairs={{0,1},{1,0},{2,3},{3,2},{4,5},{5,4},{6,7},{7,6},{8,9},{9,8},{10,11... | collective-permute-start | bytes 270344 | tf_op jit(solution)/shard_map/ppermute | solution.py:700
  2.8 5.1 %build_first.1 = bf16[16,1104,128]{2,1,0:T(8,128)(2,1)} custom-call(s32[1,208]{1,0:T(1,128)} %table.3, s32[1,2]{1,0:T(1,128)} %longs.5, s32[1,20]{1,0:T(1,128)} %shorts.5, s32[1,20]{1,0:T(1,128)} %order.5, s32[1,16]{1,0:T(1,128)} %bitcast.36, bf16[208,256,128]{2,1,0:T(8,128)(2,1)} %bitcast.23), custom_call_target="tpu_custom_call" | custom-call | bytes 9437184 | tf_op jit(solution)/shard_map/build_first/pallas_call | solution.py:147
  7.9 8.8 %all-to-all-start.1 = ((bf16[16,1104,128]{2,1,0:T(8,128)(2,1)}), bf16[16,1104,128]{2,1,0:T(8,128)(2,1)}, u32[]{:S(2)}, u32[]{:S(2)}) async-start(bf16[16,1104,128]{2,1,0:T(8,128)(2,1)} %build_first.1), calls=%async_computation.1 | async-start | bytes 9043968 | tf_op jit(solution)/shard_map/all_to_all | solution.py:708
  17.0 2.8 %collective-permute-start.2 = (bf16[2,22,2,1024]{3,2,1,0:T(2,128)(2,1)S(1)}, bf16[2,22,2,1024]{3,2,1,0:T(2,128)(2,1)S(1)}, u32[]{:S(2)}, u32[]{:S(2)}) collective-permute-start(bf16[2,22,2,1024]{3,2,1,0:T(2,128)(2,1)S(1)} %pad_maximum_fusion.1), channel_id=1, source_target_pairs={{0,4},{1,5},{2,6},{3,7},{4,0},{5,1},{6,2},{7,3},{8,12},{9,13},{10,... | collective-permute-start | bytes 540680 | tf_op jit(solution)/shard_map/ppermute | solution.py:697
  20.1 2.4 %collective-permute-start.3 = (bf16[2,22,2,1024]{3,2,1,0:T(2,128)(2,1)S(1)}, bf16[2,22,2,1024]{3,2,1,0:T(2,128)(2,1)S(1)}, u32[]{:S(2)}, u32[]{:S(2)}) collective-permute-start(bf16[2,22,2,1024]{3,2,1,0:T(2,128)(2,1)S(1)} %pad_maximum_fusion.1), channel_id=1, source_target_pairs={{0,6},{1,7},{2,0},{3,1},{4,2},{5,3},{6,4},{7,5},{8,14},{9,15},{10,... | collective-permute-start | bytes 540680 | tf_op jit(solution)/shard_map/ppermute | solution.py:697
  22.8 1.9 %collective-permute-done.2 = bf16[2,22,2,1024]{3,2,1,0:T(2,128)(2,1)S(1)} collective-permute-done((bf16[2,22,2,1024]{3,2,1,0:T(2,128)(2,1)S(1)}, bf16[2,22,2,1024]{3,2,1,0:T(2,128)(2,1)S(1)}, u32[]{:S(2)}, u32[]{:S(2)}) %collective-permute-start.2) | collective-permute-done | bytes 180256 | tf_op jit(solution)/shard_map/ppermute | solution.py:697
  24.7 4.3 %collective-permute-done.1 = bf16[2,22,2,1024]{3,2,1,0:T(2,128)(2,1)S(1)} collective-permute-done((bf16[2,22,2,1024]{3,2,1,0:T(2,128)(2,1)S(1)}, bf16[2,22,2,1024]{3,2,1,0:T(2,128)(2,1)S(1)}, u32[]{:S(2)}, u32[]{:S(2)}) %collective-permute-start.1) | collective-permute-done | bytes 180256 | tf_op jit(solution)/shard_map/ppermute | solution.py:697
  29.0 1.3 %pad_maximum_fusion = bf16[4,2,22,2,1024]{4,3,2,1,0:T(2,128)(2,1)S(1)} fusion(bf16[1,2,22,2,1024]{4,3,2,1,0:T(2,128)(2,1)S(1)} %bitcast.33, bf16[1,2,22,2,1024]{4,3,2,1,0:T(2,128)(2,1)S(1)} %bitcast.31, bf16[1,2,22,2,1024]{4,3,2,1,0:T(2,128)(2,1)S(1)} %bitcast.32, bf16[1,2,22,2,1024]{4,3,2,1,0:T(2,128)(2,1)S(1)} %fusion.7), kind=kLoop, calls=%fused_computation.4 | loop fusion | flops 1081344 | bytes 1441792 | tf_op jit(solution)/shard_map/stack | solution.py:706
  30.4 1.2 %reshape.54.blocks = bf16[8,44,1024]{2,1,0:T(8,128)(2,1)} reshape(bf16[4,2,22,2,1024]{4,3,2,1,0:T(2,128)(2,1)S(1)} %pad_maximum_fusion) | data formatting | bytes 1441792 | tf_op jit(solution)/shard_map/reshape | solution.py:707
  31.6 2.1 %join_hidden.1 = bf16[44,8192]{1,0:T(8,128)(2,1)} custom-call(s32[1]{0:T(128)} %bitcast.1.here, bf16[8,44,1024]{2,1,0:T(8,128)(2,1)} %reshape.54.blocks), custom_call_target="tpu_custom_call" | custom-call | tf_op jit(solution)/shard_map/join_hidden/pallas_call | solution.py:401
  33.7 3.3 %fusion.2 = bf16[44,2,128]{2,0,1:T(8,128)(2,1)S(1)} fusion(bf16[8192,2,128]{2,1,0:T(2,128)(2,1)} %param.13, bf16[44,8192]{1,0:T(8,128)(2,1)} %join_hidden.1), kind=kOutput, calls=%fused_computation.2 | convolution fusion | flops 184560640 | bytes 4937728 | tf_op jit(solution)/shard_map/rd,dcn->rcn/dot_general | solution.py:711
  37.2 9.4 %attend_all.1 = (bf16[22,16,128]{2,1,0:T(8,128)(2,1)S(1)}, bf16[16,304,128]{2,1,0:T(8,128)(2,1)S(1)}) custom-call(s32[1,208]{1,0:T(1,128)S(1)} %copy-done.5, s32[1,2]{1,0:T(1,128)S(1)} %copy-done.1, s32[1,20]{1,0:T(1,128)S(1)} %copy-done.2, s32[1,20]{1,0:T(1,128)S(1)} %copy-done.6, s32[1,16]{1,0:T(1,128)S(1)} %bitcast.37, ...), custom_call_target="tpu_custom_call" | custom-call | flops 218103808 | bytes 14680064 | tf_op jit(solution)/shard_map/attend_all/pallas_call | solution.py:362
  46.5 1.1 %copy-done = bf16[16,304,128]{2,1,0:T(8,128)(2,1)} copy-done((bf16[16,304,128]{2,1,0:T(8,128)(2,1)}, bf16[16,304,128]{2,1,0:T(8,128)(2,1)S(1)}, u32[]{:S(2)}) %copy-start) | copy-done | bytes 1245208
  47.6 23.7 %all-to-all-done.1.received.block = bf16[16,1104,128]{2,1,0:T(8,128)(2,1)} async-done(((bf16[16,1104,128]{2,1,0:T(8,128)(2,1)}), bf16[16,1104,128]{2,1,0:T(8,128)(2,1)}, u32[]{:S(2)}, u32[]{:S(2)}) %all-to-all-start.1) | async-done | bytes 4522016 | tf_op jit(solution)/shard_map/all_to_all | solution.py:708
  71.3 1.9 %route_pieces.1 = bf16[16,304,128]{2,1,0:T(8,128)(2,1)} custom-call(bf16[16,1104,128]{2,1,0:T(8,128)(2,1)} %all-to-all-done.1.received.block, bf16[16,304,128]{2,1,0:T(8,128)(2,1)} %copy-done), custom_call_target="tpu_custom_call", output_to_operand_aliasing={{}: (1, {})} | custom-call | bytes 1048576 | tf_op jit(solution)/shard_map/route_pieces/pallas_call | solution.py:448
  73.2 4.4 %all-to-all-start.2 = ((bf16[16,304,128]{2,1,0:T(8,128)(2,1)}), bf16[16,304,128]{2,1,0:T(8,128)(2,1)S(1)}, u32[]{:S(2)}, u32[]{:S(2)}) async-start(bf16[16,304,128]{2,1,0:T(8,128)(2,1)} %route_pieces.1), calls=%async_computation.2 | async-start | bytes 2490368 | tf_op jit(solution)/shard_map/all_to_all | solution.py:725
  77.6 0.7 reshape.49
  78.3 2.4 %decode_tables.1 = (s32[16,128]{1,0:T(8,128)S(1)}, f32[8,128]{1,0:T(8,128)}) custom-call(s32[1]{0:T(128)} %bitcast.14.here, s32[1,2]{1,0:T(1,128)} %longs.5, s32[1,20]{1,0:T(1,128)} %shorts.5, s32[1,20]{1,0:T(1,128)S(1)} %copy-done.6, bf16[16,1104,128]{2,1,0:T(8,128)(2,1)} %all-to-all-done.1.received.block), custom_call_target="tpu_custom_call" | custom-call | tf_op jit(solution)/shard_map/decode_tables/pallas_call | solution.py:502
  80.7 1.3 %fusion.6 = (f32[1,1]{1,0:T(1,128)}, f32[1,1]{1,0:T(1,128)}) fusion(f32[8,128]{1,0:T(8,128)} %get-tuple-element.53), kind=kLoop, calls=%fused_computation.7 | loop fusion | bytes 16 | tf_op jit(solution)/shard_map/slice | solution.py:730
  82.7 11.9 %place_first.1 = (bf16[32,2,512,128]{3,2,1,0:T(8,128)(2,1)}, bf16[16,2,32,128]{3,2,1,0:T(8,128)(2,1)S(1)}) custom-call(s32[16,128]{1,0:T(8,128)S(1)} %get-tuple-element.54.lens, bf16[16,1104,128]{2,1,0:T(8,128)(2,1)} %all-to-all-done.1.received.block), custom_call_target="tpu_custom_call" | custom-call | bytes 13631488 | tf_op jit(solution)/shard_map/place_first/pallas_call | solution.py:568
  94.6 2.5 %all-to-all-done.2 = bf16[16,304,128]{2,1,0:T(8,128)(2,1)S(1)} async-done(((bf16[16,304,128]{2,1,0:T(8,128)(2,1)}), bf16[16,304,128]{2,1,0:T(8,128)(2,1)S(1)}, u32[]{:S(2)}, u32[]{:S(2)}) %all-to-all-start.2) | async-done | bytes 1245216 | tf_op jit(solution)/shard_map/all_to_all | solution.py:725
  97.1 2.3 %conditional.1 = ((bf16[32,2,512,128]{3,2,1,0:T(8,128)(2,1)}, bf16[32,16,128]{2,1,0:T(8,128)(2,1)S(1)})) conditional(s32[]{:T(128)} %bitcast.15, (s32[16,128]{1,0:T(8,128)S(1)}, bf16[16,2,32,128]{3,2,1,0:T(8,128)(2,1)S(1)}, bf16[16,304,128]{2,1,0:T(8,128)(2,1)S(1)}, bf16[32,2,512,128]{3,2,1,0:T(8,128)(2,1)}) %tuple.16, (s32[1,208]{1,0:T(1,128)S(1)}, ...), branch_computations={%region_0.1_spmd, %region_1.2_spmd} | conditional | bytes 8388616 | solution.py:745
  97.1 2.1 %settle_short.1 = (bf16[32,2,512,128]{3,2,1,0:T(8,128)(2,1)}, bf16[32,16,128]{2,1,0:T(8,128)(2,1)S(1)}) custom-call(s32[16,128]{1,0:T(8,128)S(1)} %get-tuple-element.24.refs_0_, bf16[16,2,32,128]{3,2,1,0:T(8,128)(2,1)S(1)} %get-tuple-element.25.refs_1_.refs_3_, bf16[16,304,128]{2,1,0:T(8,128)(2,1)S(1)} %get-tuple-element.26.refs_2_, ...), custom_call_target="tpu_custom_call", output_to_operand_aliasing={{0}: (4, {})} | custom-call | tf_op jit(solution)/shard_map/cond/branch_0_fun/settle_short/pallas_call | solution.py:659
  99.4 0.7 reshape.51
  (27 shorter events, 1.0 us)
Async XLA Ops:
  0.6 7.3 %collective-permute-start = (bf16[22,2,1024]{2,1,0:T(2,128)(2,1)}, bf16[22,2,1024]{2,1,0:T(2,128)(2,1)S(1)}, u32[]{:S(2)}, u32[]{:S(2)}) collective-permute-start(bf16[22,2,1024]{2,1,0:T(2,128)(2,1)} %param.12), channel_id=1, source_target_pairs={{0,1},{1,0},{2,3},{3,2},{4,5},{5,4},{6,7},{7,6},{8,9},{9,8},{10,11... | collective-permute-start | bytes 270344 | tf_op jit(solution)/shard_map/ppermute | solution.py:700
  7.9 8.8 %copy-start.3 = (bf16[22,2,1024]{2,1,0:T(2,128)(2,1)S(1)}, bf16[22,2,1024]{2,1,0:T(2,128)(2,1)}, u32[]{:S(2)}) copy-start(bf16[22,2,1024]{2,1,0:T(2,128)(2,1)} %param.12) | copy-start | bytes 270340
  7.9 14.6 %copy-start.4 = (bf16[22,2,1024]{2,1,0:T(2,128)(2,1)S(1)}, bf16[22,2,1024]{2,1,0:T(2,128)(2,1)}, u32[]{:S(2)}) copy-start(bf16[22,2,1024]{2,1,0:T(2,128)(2,1)} %param.11) | copy-start | bytes 270340
  7.9 63.4 %all-to-all-start.1 = ((bf16[16,1104,128]{2,1,0:T(8,128)(2,1)}), bf16[16,1104,128]{2,1,0:T(8,128)(2,1)}, u32[]{:S(2)}, u32[]{:S(2)}) async-start(bf16[16,1104,128]{2,1,0:T(8,128)(2,1)} %build_first.1), calls=%async_computation.1 | async-start | bytes 9043968 | tf_op jit(solution)/shard_map/all_to_all | solution.py:708
  17.0 7.7 %collective-permute-start.2 = (bf16[2,22,2,1024]{3,2,1,0:T(2,128)(2,1)S(1)}, bf16[2,22,2,1024]{3,2,1,0:T(2,128)(2,1)S(1)}, u32[]{:S(2)}, u32[]{:S(2)}) collective-permute-start(bf16[2,22,2,1024]{3,2,1,0:T(2,128)(2,1)S(1)} %pad_maximum_fusion.1), channel_id=1, source_target_pairs={{0,4},{1,5},{2,6},{3,7},{4,0},{5,1},{6,2},{7,3},{8,12},{9,13},{10,... | collective-permute-start | bytes 540680 | tf_op jit(solution)/shard_map/ppermute | solution.py:697
  19.8 9.2 %collective-permute-start.1 = (bf16[2,22,2,1024]{3,2,1,0:T(2,128)(2,1)S(1)}, bf16[2,22,2,1024]{3,2,1,0:T(2,128)(2,1)S(1)}, u32[]{:S(2)}, u32[]{:S(2)}) collective-permute-start(bf16[2,22,2,1024]{3,2,1,0:T(2,128)(2,1)S(1)} %pad_maximum_fusion.1), channel_id=1, source_target_pairs={{0,2},{1,3},{2,4},{3,5},{4,6},{5,7},{6,0},{7,1},{8,10},{9,11},{10,... | collective-permute-start | bytes 540680 | tf_op jit(solution)/shard_map/ppermute | solution.py:697
  20.1 8.9 %collective-permute-start.3 = (bf16[2,22,2,1024]{3,2,1,0:T(2,128)(2,1)S(1)}, bf16[2,22,2,1024]{3,2,1,0:T(2,128)(2,1)S(1)}, u32[]{:S(2)}, u32[]{:S(2)}) collective-permute-start(bf16[2,22,2,1024]{3,2,1,0:T(2,128)(2,1)S(1)} %pad_maximum_fusion.1), channel_id=1, source_target_pairs={{0,6},{1,7},{2,0},{3,1},{4,2},{5,3},{6,4},{7,5},{8,14},{9,15},{10,... | collective-permute-start | bytes 540680 | tf_op jit(solution)/shard_map/ppermute | solution.py:697
  30.3 6.8 %copy-start.1 = (s32[1,2]{1,0:T(1,128)S(1)}, s32[1,2]{1,0:T(1,128)}, u32[]{:S(2)}) copy-start(s32[1,2]{1,0:T(1,128)} %longs.5) | copy-start | bytes 28
  30.4 6.8 %copy-start.2 = (s32[1,20]{1,0:T(1,128)S(1)}, s32[1,20]{1,0:T(1,128)}, u32[]{:S(2)}) copy-start(s32[1,20]{1,0:T(1,128)} %shorts.5) | copy-start | bytes 244
  30.4 6.8 %copy-start.5 = (s32[1,208]{1,0:T(1,128)S(1)}, s32[1,208]{1,0:T(1,128)}, u32[]{:S(2)}) copy-start(s32[1,208]{1,0:T(1,128)} %table.3) | copy-start | bytes 2500
  30.4 6.8 %copy-start.6 = (s32[1,20]{1,0:T(1,128)S(1)}, s32[1,20]{1,0:T(1,128)}, u32[]{:S(2)}) copy-start(s32[1,20]{1,0:T(1,128)} %order.5) | copy-start | bytes 244
  30.4 6.8 %copy-start.7 = (s32[16,1]{0,1:T(1,128)S(1)}, s32[16,1]{0,1:T(1,128)}, u32[]{:S(2)}) copy-start(s32[16,1]{0,1:T(1,128)} %param.19) | copy-start | bytes 196
  46.5 1.1 %copy-start = (bf16[16,304,128]{2,1,0:T(8,128)(2,1)}, bf16[16,304,128]{2,1,0:T(8,128)(2,1)S(1)}, u32[]{:S(2)}) copy-start(bf16[16,304,128]{2,1,0:T(8,128)(2,1)S(1)} %get-tuple-element.56._) | copy-start | bytes 3735556
  73.2 23.9 %all-to-all-start.2 = ((bf16[16,304,128]{2,1,0:T(8,128)(2,1)}), bf16[16,304,128]{2,1,0:T(8,128)(2,1)S(1)}, u32[]{:S(2)}, u32[]{:S(2)}) async-start(bf16[16,304,128]{2,1,0:T(8,128)(2,1)} %route_pieces.1), calls=%async_computation.2 | async-start | bytes 2490368 | tf_op jit(solution)/shard_map/all_to_all | solution.py:725

commit v8 on v7

--- a/solution.py
+++ b/solution.py
@@ -601,17 +601,14 @@
 
     for s in range(INST):
         length = lens[s, 0]
-
-        @pl.when(length > 0)
-        def _():
-            fresh = second[s, pl.ds(B_FRESH, 16)].astype(jnp.float32)[:8]
-            where = at + window_base(length)
-            for c in range(2):
-                x = window[s, c].astype(jnp.float32)
-                for t in range(STEPS):
-                    x = jnp.where(where == length + t, fresh[c * 2 + t:c * 2 + t + 1], x)
-                patched[s, c] = x.astype(jnp.bfloat16)
-                patch_copy(s, c).start()
+        fresh = second[s, pl.ds(B_FRESH, 16)].astype(jnp.float32)[:8]
+        where = at + window_base(length) - jnp.where(length > 0, length, -MIGLEN)
+        for c in range(2):
+            x = window[s, c].astype(jnp.float32)
+            for t in range(STEPS):
+                x = jnp.where(where == t, fresh[c * 2 + t:c * 2 + t + 1], x)
+            patched[s, c] = x.astype(jnp.bfloat16)
+            patch_copy(s, c).start()
 
     order = jnp.int32(0)
     for s in range(INST):
@@ -642,10 +639,8 @@
             rows = second[s, pl.ds(slot * ROWS, ROWS)]
             out[s * CAP + slot] = jnp.where(filled, rows, jnp.zeros_like(rows))
     for s in range(INST):
-        @pl.when(lens[s, 0] > 0)
-        def _():
-            for c in range(2):
-                patch_copy(s, c).wait()
+        for c in range(2):
+            patch_copy(s, c).wait()
 
         @pl.when(lens[s, 1] > 0)
         def _():

time: 101 us -> 101 us (level)
  waiting for transfers between devices: 32.4 us -> 28.8 us
  Pallas kernels: 34.8 us -> 38.2 us
    all_to_all x1, waiting for transfers between devices: 23.7 us -> 20.1 us  [on_device(): lax.all_to_all(first, 'inst', split_axis=0, concat_axis=0, tiled=True)]
    pallas_call x1, Pallas kernels: 9.37 us -> 13 us  [attend(): pl.pallas_call(attend_kernel, out_shape=(jax.ShapeDtypeStruct((REQS, ROWS...]
  transfers between devices with their start and end apart: 6 -> 6, of which waited for: 4 -> 4; matrix products, arithmetic and copies ran while one was open for 8% -> 8% of each run, Pallas kernels for 31% -> 35%
where the time goes in v8:
time: 101 us; the launch traced here: 99.9 us
  Pallas kernels  38.2 us (38%)
  waiting for transfers between devices  28.8 us (29%)
  starting transfers between devices  20.9 us (21%)
  local copies, waits for them, and re-layouts  5.09 us (5%)
  matrix products  3.27 us (3%)
  other arithmetic  1.83 us (2%)
  between operations  1.53 us (2%)
    all_to_all x1, waiting for transfers between devices, on_device(): lax.all_to_all(first, 'inst', split_axis=0, concat_axis=0, tiled=True)  20.1 us
    pallas_call x1, Pallas kernels, attend(): pl.pallas_call(attend_kernel, out_shape=(jax.ShapeDtypeStruct((REQS, ROWS...  13 us
    pallas_call x1, Pallas kernels, place_first(): pl.pallas_call(place_kernel, out_shape=(jax.ShapeDtypeStruct((INST * CAP,...  11.9 us
    all_to_all x1, starting transfers between devices, on_device(): lax.all_to_all(first, 'inst', split_axis=0, concat_axis=0, tiled=True)  8.76 us
    ppermute x3, waiting for transfers between devices, from_x(): lax.ppermute(value, 'tp', [(i, (i // 2 + k) % 4 * 2 + i % 2) for i in ran...  6.2 us
    ppermute x3, starting transfers between devices, from_x(): lax.ppermute(value, 'tp', [(i, (i // 2 + k) % 4 * 2 + i % 2) for i in ran...  5.5 us
    pallas_call x1, Pallas kernels, build(): pl.pallas_call(build_kernel, out_shape=jax.ShapeDtypeStruct((INST, A_ROWS...  5.06 us
    all_to_all x1, starting transfers between devices, on_device(): lax.all_to_all(second, 'inst', split_axis=0, concat_axis=0, tiled=True)  4.43 us
  transfers between devices with their start and end apart: 6, of which 4 were waited for; matrix products, arithmetic and copies ran while one was open for 8% of the time, Pallas kernels for 35%

profile of v8, /device:TPU:1, one launch (start us, length us, event | category | flops | bytes accessed | tf_op | source)
XLA Modules:
  0.0 99.9 jit_solution(10902013524060186347)
XLA Ops:
  0.6 2.2 %collective-permute-start = (bf16[22,2,1024]{2,1,0:T(2,128)(2,1)}, bf16[22,2,1024]{2,1,0:T(2,128)(2,1)S(1)}, u32[]{:S(2)}, u32[]{:S(2)}) collective-permute-start(bf16[22,2,1024]{2,1,0:T(2,128)(2,1)} %param.12), channel_id=1, source_target_pairs={{0,1},{1,0},{2,3},{3,2},{4,5},{5,4},{6,7},{7,6},{8,9},{9,8},{10,11... | collective-permute-start | bytes 270344 | tf_op jit(solution)/shard_map/ppermute | solution.py:695
  2.8 5.1 %build_first.1 = bf16[16,1104,128]{2,1,0:T(8,128)(2,1)} custom-call(s32[1,208]{1,0:T(1,128)} %table.3, s32[1,2]{1,0:T(1,128)} %longs.5, s32[1,20]{1,0:T(1,128)} %shorts.5, s32[1,20]{1,0:T(1,128)} %order.5, s32[1,16]{1,0:T(1,128)} %bitcast.36, bf16[208,256,128]{2,1,0:T(8,128)(2,1)} %bitcast.23), custom_call_target="tpu_custom_call" | custom-call | bytes 9437184 | tf_op jit(solution)/shard_map/build_first/pallas_call | solution.py:147
  7.9 8.8 %all-to-all-start.1 = ((bf16[16,1104,128]{2,1,0:T(8,128)(2,1)}), bf16[16,1104,128]{2,1,0:T(8,128)(2,1)}, u32[]{:S(2)}, u32[]{:S(2)}) async-start(bf16[16,1104,128]{2,1,0:T(8,128)(2,1)} %build_first.1), calls=%async_computation.1 | async-start | bytes 9043968 | tf_op jit(solution)/shard_map/all_to_all | solution.py:703
  17.0 2.8 %collective-permute-start.2 = (bf16[2,22,2,1024]{3,2,1,0:T(2,128)(2,1)S(1)}, bf16[2,22,2,1024]{3,2,1,0:T(2,128)(2,1)S(1)}, u32[]{:S(2)}, u32[]{:S(2)}) collective-permute-start(bf16[2,22,2,1024]{3,2,1,0:T(2,128)(2,1)S(1)} %pad_maximum_fusion.1), channel_id=1, source_target_pairs={{0,4},{1,5},{2,6},{3,7},{4,0},{5,1},{6,2},{7,3},{8,12},{9,13},{10,... | collective-permute-start | bytes 540680 | tf_op jit(solution)/shard_map/ppermute | solution.py:692
  20.1 2.4 %collective-permute-start.3 = (bf16[2,22,2,1024]{3,2,1,0:T(2,128)(2,1)S(1)}, bf16[2,22,2,1024]{3,2,1,0:T(2,128)(2,1)S(1)}, u32[]{:S(2)}, u32[]{:S(2)}) collective-permute-start(bf16[2,22,2,1024]{3,2,1,0:T(2,128)(2,1)S(1)} %pad_maximum_fusion.1), channel_id=1, source_target_pairs={{0,6},{1,7},{2,0},{3,1},{4,2},{5,3},{6,4},{7,5},{8,14},{9,15},{10,... | collective-permute-start | bytes 540680 | tf_op jit(solution)/shard_map/ppermute | solution.py:692
  22.8 1.9 %collective-permute-done.2 = bf16[2,22,2,1024]{3,2,1,0:T(2,128)(2,1)S(1)} collective-permute-done((bf16[2,22,2,1024]{3,2,1,0:T(2,128)(2,1)S(1)}, bf16[2,22,2,1024]{3,2,1,0:T(2,128)(2,1)S(1)}, u32[]{:S(2)}, u32[]{:S(2)}) %collective-permute-start.2) | collective-permute-done | bytes 180256 | tf_op jit(solution)/shard_map/ppermute | solution.py:692
  24.7 4.3 %collective-permute-done.1 = bf16[2,22,2,1024]{3,2,1,0:T(2,128)(2,1)S(1)} collective-permute-done((bf16[2,22,2,1024]{3,2,1,0:T(2,128)(2,1)S(1)}, bf16[2,22,2,1024]{3,2,1,0:T(2,128)(2,1)S(1)}, u32[]{:S(2)}, u32[]{:S(2)}) %collective-permute-start.1) | collective-permute-done | bytes 180256 | tf_op jit(solution)/shard_map/ppermute | solution.py:692
  29.0 1.3 %pad_maximum_fusion = bf16[4,2,22,2,1024]{4,3,2,1,0:T(2,128)(2,1)S(1)} fusion(bf16[1,2,22,2,1024]{4,3,2,1,0:T(2,128)(2,1)S(1)} %bitcast.33, bf16[1,2,22,2,1024]{4,3,2,1,0:T(2,128)(2,1)S(1)} %bitcast.31, bf16[1,2,22,2,1024]{4,3,2,1,0:T(2,128)(2,1)S(1)} %bitcast.32, bf16[1,2,22,2,1024]{4,3,2,1,0:T(2,128)(2,1)S(1)} %fusion.7), kind=kLoop, calls=%fused_computation.4 | loop fusion | flops 1081344 | bytes 1441792 | tf_op jit(solution)/shard_map/stack | solution.py:701
  30.4 1.2 %reshape.54.blocks = bf16[8,44,1024]{2,1,0:T(8,128)(2,1)} reshape(bf16[4,2,22,2,1024]{4,3,2,1,0:T(2,128)(2,1)S(1)} %pad_maximum_fusion) | data formatting | bytes 1441792 | tf_op jit(solution)/shard_map/reshape | solution.py:702
  31.6 2.1 %join_hidden.1 = bf16[44,8192]{1,0:T(8,128)(2,1)} custom-call(s32[1]{0:T(128)} %bitcast.1.here, bf16[8,44,1024]{2,1,0:T(8,128)(2,1)} %reshape.54.blocks), custom_call_target="tpu_custom_call" | custom-call | tf_op jit(solution)/shard_map/join_hidden/pallas_call | solution.py:401
  33.7 3.3 %fusion.2 = bf16[44,2,128]{2,0,1:T(8,128)(2,1)S(1)} fusion(bf16[8192,2,128]{2,1,0:T(2,128)(2,1)} %param.13, bf16[44,8192]{1,0:T(8,128)(2,1)} %join_hidden.1), kind=kOutput, calls=%fused_computation.2 | convolution fusion | flops 184560640 | bytes 4937728 | tf_op jit(solution)/shard_map/rd,dcn->rcn/dot_general | solution.py:706
  37.2 13.0 %attend_all.1 = (bf16[22,16,128]{2,1,0:T(8,128)(2,1)S(1)}, bf16[16,304,128]{2,1,0:T(8,128)(2,1)S(1)}) custom-call(s32[1,208]{1,0:T(1,128)S(1)} %copy-done.5, s32[1,2]{1,0:T(1,128)S(1)} %copy-done.1, s32[1,20]{1,0:T(1,128)S(1)} %copy-done.2, s32[1,20]{1,0:T(1,128)S(1)} %copy-done.6, s32[1,16]{1,0:T(1,128)S(1)} %bitcast.37, ...), custom_call_target="tpu_custom_call" | custom-call | flops 218103808 | bytes 14680064 | tf_op jit(solution)/shard_map/attend_all/pallas_call | solution.py:362
  50.2 1.1 %copy-done = bf16[16,304,128]{2,1,0:T(8,128)(2,1)} copy-done((bf16[16,304,128]{2,1,0:T(8,128)(2,1)}, bf16[16,304,128]{2,1,0:T(8,128)(2,1)S(1)}, u32[]{:S(2)}) %copy-start) | copy-done | bytes 1245208
  51.2 20.1 %all-to-all-done.1.received.block = bf16[16,1104,128]{2,1,0:T(8,128)(2,1)} async-done(((bf16[16,1104,128]{2,1,0:T(8,128)(2,1)}), bf16[16,1104,128]{2,1,0:T(8,128)(2,1)}, u32[]{:S(2)}, u32[]{:S(2)}) %all-to-all-start.1) | async-done | bytes 4522016 | tf_op jit(solution)/shard_map/all_to_all | solution.py:703
  71.3 1.9 %route_pieces.1 = bf16[16,304,128]{2,1,0:T(8,128)(2,1)} custom-call(bf16[16,1104,128]{2,1,0:T(8,128)(2,1)} %all-to-all-done.1.received.block, bf16[16,304,128]{2,1,0:T(8,128)(2,1)} %copy-done), custom_call_target="tpu_custom_call", output_to_operand_aliasing={{}: (1, {})} | custom-call | bytes 1048576 | tf_op jit(solution)/shard_map/route_pieces/pallas_call | solution.py:448
  73.2 4.4 %all-to-all-start.2 = ((bf16[16,304,128]{2,1,0:T(8,128)(2,1)}), bf16[16,304,128]{2,1,0:T(8,128)(2,1)S(1)}, u32[]{:S(2)}, u32[]{:S(2)}) async-start(bf16[16,304,128]{2,1,0:T(8,128)(2,1)} %route_pieces.1), calls=%async_computation.2 | async-start | bytes 2490368 | tf_op jit(solution)/shard_map/all_to_all | solution.py:720
  77.6 0.7 reshape.49
  78.3 2.4 %decode_tables.1 = (s32[16,128]{1,0:T(8,128)S(1)}, f32[8,128]{1,0:T(8,128)}) custom-call(s32[1]{0:T(128)} %bitcast.14.here, s32[1,2]{1,0:T(1,128)} %longs.5, s32[1,20]{1,0:T(1,128)} %shorts.5, s32[1,20]{1,0:T(1,128)S(1)} %copy-done.6, bf16[16,1104,128]{2,1,0:T(8,128)(2,1)} %all-to-all-done.1.received.block), custom_call_target="tpu_custom_call" | custom-call | tf_op jit(solution)/shard_map/decode_tables/pallas_call | solution.py:502
  80.7 1.3 %fusion.6 = (f32[1,1]{1,0:T(1,128)}, f32[1,1]{1,0:T(1,128)}) fusion(f32[8,128]{1,0:T(8,128)} %get-tuple-element.53), kind=kLoop, calls=%fused_computation.7 | loop fusion | bytes 16 | tf_op jit(solution)/shard_map/slice | solution.py:725
  82.6 11.9 %place_first.1 = (bf16[32,2,512,128]{3,2,1,0:T(8,128)(2,1)}, bf16[16,2,32,128]{3,2,1,0:T(8,128)(2,1)S(1)}) custom-call(s32[16,128]{1,0:T(8,128)S(1)} %get-tuple-element.54.lens, bf16[16,1104,128]{2,1,0:T(8,128)(2,1)} %all-to-all-done.1.received.block), custom_call_target="tpu_custom_call" | custom-call | bytes 13631488 | tf_op jit(solution)/shard_map/place_first/pallas_call | solution.py:568
  94.6 2.5 %all-to-all-done.2 = bf16[16,304,128]{2,1,0:T(8,128)(2,1)S(1)} async-done(((bf16[16,304,128]{2,1,0:T(8,128)(2,1)}), bf16[16,304,128]{2,1,0:T(8,128)(2,1)S(1)}, u32[]{:S(2)}, u32[]{:S(2)}) %all-to-all-start.2) | async-done | bytes 1245216 | tf_op jit(solution)/shard_map/all_to_all | solution.py:720
  97.0 2.1 %conditional.1 = ((bf16[32,2,512,128]{3,2,1,0:T(8,128)(2,1)}, bf16[32,16,128]{2,1,0:T(8,128)(2,1)S(1)})) conditional(s32[]{:T(128)} %bitcast.15, (s32[16,128]{1,0:T(8,128)S(1)}, bf16[16,2,32,128]{3,2,1,0:T(8,128)(2,1)S(1)}, bf16[16,304,128]{2,1,0:T(8,128)(2,1)S(1)}, bf16[32,2,512,128]{3,2,1,0:T(8,128)(2,1)}) %tuple.16, (s32[1,208]{1,0:T(1,128)S(1)}, ...), branch_computations={%region_0.1_spmd, %region_1.2_spmd} | conditional | bytes 8388616 | solution.py:740
  97.0 1.9 %settle_short.1 = (bf16[32,2,512,128]{3,2,1,0:T(8,128)(2,1)}, bf16[32,16,128]{2,1,0:T(8,128)(2,1)S(1)}) custom-call(s32[16,128]{1,0:T(8,128)S(1)} %get-tuple-element.24.refs_0_, bf16[16,2,32,128]{3,2,1,0:T(8,128)(2,1)S(1)} %get-tuple-element.25.refs_1_.refs_3_, bf16[16,304,128]{2,1,0:T(8,128)(2,1)S(1)} %get-tuple-element.26.refs_2_, ...), custom_call_target="tpu_custom_call", output_to_operand_aliasing={{0}: (4, {})} | custom-call | tf_op jit(solution)/shard_map/cond/branch_0_fun/settle_short/pallas_call | solution.py:654
  99.2 0.7 reshape.51
  (27 shorter events, 1.0 us)
Async XLA Ops:
  0.6 7.3 %collective-permute-start = (bf16[22,2,1024]{2,1,0:T(2,128)(2,1)}, bf16[22,2,1024]{2,1,0:T(2,128)(2,1)S(1)}, u32[]{:S(2)}, u32[]{:S(2)}) collective-permute-start(bf16[22,2,1024]{2,1,0:T(2,128)(2,1)} %param.12), channel_id=1, source_target_pairs={{0,1},{1,0},{2,3},{3,2},{4,5},{5,4},{6,7},{7,6},{8,9},{9,8},{10,11... | collective-permute-start | bytes 270344 | tf_op jit(solution)/shard_map/ppermute | solution.py:695
  7.9 8.8 %copy-start.3 = (bf16[22,2,1024]{2,1,0:T(2,128)(2,1)S(1)}, bf16[22,2,1024]{2,1,0:T(2,128)(2,1)}, u32[]{:S(2)}) copy-start(bf16[22,2,1024]{2,1,0:T(2,128)(2,1)} %param.12) | copy-start | bytes 270340
  7.9 14.6 %copy-start.4 = (bf16[22,2,1024]{2,1,0:T(2,128)(2,1)S(1)}, bf16[22,2,1024]{2,1,0:T(2,128)(2,1)}, u32[]{:S(2)}) copy-start(bf16[22,2,1024]{2,1,0:T(2,128)(2,1)} %param.11) | copy-start | bytes 270340
  7.9 63.4 %all-to-all-start.1 = ((bf16[16,1104,128]{2,1,0:T(8,128)(2,1)}), bf16[16,1104,128]{2,1,0:T(8,128)(2,1)}, u32[]{:S(2)}, u32[]{:S(2)}) async-start(bf16[16,1104,128]{2,1,0:T(8,128)(2,1)} %build_first.1), calls=%async_computation.1 | async-start | bytes 9043968 | tf_op jit(solution)/shard_map/all_to_all | solution.py:703
  17.0 7.7 %collective-permute-start.2 = (bf16[2,22,2,1024]{3,2,1,0:T(2,128)(2,1)S(1)}, bf16[2,22,2,1024]{3,2,1,0:T(2,128)(2,1)S(1)}, u32[]{:S(2)}, u32[]{:S(2)}) collective-permute-start(bf16[2,22,2,1024]{3,2,1,0:T(2,128)(2,1)S(1)} %pad_maximum_fusion.1), channel_id=1, source_target_pairs={{0,4},{1,5},{2,6},{3,7},{4,0},{5,1},{6,2},{7,3},{8,12},{9,13},{10,... | collective-permute-start | bytes 540680 | tf_op jit(solution)/shard_map/ppermute | solution.py:692
  19.8 9.2 %collective-permute-start.1 = (bf16[2,22,2,1024]{3,2,1,0:T(2,128)(2,1)S(1)}, bf16[2,22,2,1024]{3,2,1,0:T(2,128)(2,1)S(1)}, u32[]{:S(2)}, u32[]{:S(2)}) collective-permute-start(bf16[2,22,2,1024]{3,2,1,0:T(2,128)(2,1)S(1)} %pad_maximum_fusion.1), channel_id=1, source_target_pairs={{0,2},{1,3},{2,4},{3,5},{4,6},{5,7},{6,0},{7,1},{8,10},{9,11},{10,... | collective-permute-start | bytes 540680 | tf_op jit(solution)/shard_map/ppermute | solution.py:692
  20.1 8.9 %collective-permute-start.3 = (bf16[2,22,2,1024]{3,2,1,0:T(2,128)(2,1)S(1)}, bf16[2,22,2,1024]{3,2,1,0:T(2,128)(2,1)S(1)}, u32[]{:S(2)}, u32[]{:S(2)}) collective-permute-start(bf16[2,22,2,1024]{3,2,1,0:T(2,128)(2,1)S(1)} %pad_maximum_fusion.1), channel_id=1, source_target_pairs={{0,6},{1,7},{2,0},{3,1},{4,2},{5,3},{6,4},{7,5},{8,14},{9,15},{10,... | collective-permute-start | bytes 540680 | tf_op jit(solution)/shard_map/ppermute | solution.py:692
  30.3 6.8 %copy-start.1 = (s32[1,2]{1,0:T(1,128)S(1)}, s32[1,2]{1,0:T(1,128)}, u32[]{:S(2)}) copy-start(s32[1,2]{1,0:T(1,128)} %longs.5) | copy-start | bytes 28
  30.4 6.8 %copy-start.2 = (s32[1,20]{1,0:T(1,128)S(1)}, s32[1,20]{1,0:T(1,128)}, u32[]{:S(2)}) copy-start(s32[1,20]{1,0:T(1,128)} %shorts.5) | copy-start | bytes 244
  30.4 6.8 %copy-start.5 = (s32[1,208]{1,0:T(1,128)S(1)}, s32[1,208]{1,0:T(1,128)}, u32[]{:S(2)}) copy-start(s32[1,208]{1,0:T(1,128)} %table.3) | copy-start | bytes 2500
  30.4 6.8 %copy-start.6 = (s32[1,20]{1,0:T(1,128)S(1)}, s32[1,20]{1,0:T(1,128)}, u32[]{:S(2)}) copy-start(s32[1,20]{1,0:T(1,128)} %order.5) | copy-start | bytes 244
  30.4 6.8 %copy-start.7 = (s32[16,1]{0,1:T(1,128)S(1)}, s32[16,1]{0,1:T(1,128)}, u32[]{:S(2)}) copy-start(s32[16,1]{0,1:T(1,128)} %param.19) | copy-start | bytes 196
  50.2 1.1 %copy-start = (bf16[16,304,128]{2,1,0:T(8,128)(2,1)}, bf16[16,304,128]{2,1,0:T(8,128)(2,1)S(1)}, u32[]{:S(2)}) copy-start(bf16[16,304,128]{2,1,0:T(8,128)(2,1)S(1)} %get-tuple-element.56._) | copy-start | bytes 3735556
  73.2 23.9 %all-to-all-start.2 = ((bf16[16,304,128]{2,1,0:T(8,128)(2,1)}), bf16[16,304,128]{2,1,0:T(8,128)(2,1)S(1)}, u32[]{:S(2)}, u32[]{:S(2)}) async-start(bf16[16,304,128]{2,1,0:T(8,128)(2,1)} %route_pieces.1), calls=%async_computation.2 | async-start | bytes 2490368 | tf_op jit(solution)/shard_map/all_to_all | solution.py:720
